TPU v7x, 32 devices: a whole 2x2x4 slice. The times are simulated.
32 devices in a mesh: groups: 1, lat: 16 (over z, y, x), lon: 2 (over core).
Axes of the slice: x: 2, y: 2, z: 4, core: 2. Of those that a mesh axis runs over, the one named last changes fastest.
Arguments:
- fields: bfloat16 [64, 128, 256], P('groups', 'lat', 'lon'), may hold values from -6 to 6
- conv_first: bfloat16 [64, 64, 3, 3], replicated, may hold values from -0.25 to 0.25
- conv_second: bfloat16 [64, 64, 3, 3], replicated, may hold values from -0.25 to 0.25
- mixing: bfloat16 [64, 64, 64], P(None, 'lon'), may hold values from -0.75 to 0.75
Outputs:
- result: bfloat16 [64, 128, 256], P(('groups', 'lon'), 'lat')
All inputs are finite; a program needn't handle non-finite values.
Results may differ from a plain program's by a relative error of at most 0.0095.
Values may be sent and summed in bfloat16 or wider, within the bound.
No kernel may reach another device: no remote copies, remote signals or barrier semaphores. Data moves between devices by JAX's collectives and lax.ppermute only.
A program may use at most 64 MiB of HBM per device.

v0:
```python
import math

import jax
import jax.numpy as jnp
from jax import lax
from jax.sharding import PartitionSpec as P


def padded_2(block, sides, width, periodic):
    for axis, dim in sides:
        count = lax.axis_size(axis)
        forward = [(i, i + 1) for i in range(count - 1)]
        if periodic:
            forward.append((count - 1, 0))
        backward = [(target, source) for source, target in forward]
        low = lax.ppermute(
            lax.slice_in_dim(block, block.shape[dim] - width, None, axis=dim), axis, forward
        )
        high = lax.ppermute(lax.slice_in_dim(block, 0, width, axis=dim), axis, backward)
        block = jnp.concatenate([low, block, high], axis=dim)
    return block


def forward_table(lon_total, orders):
    points = jnp.arange(lon_total, dtype=jnp.int32)[:, None]
    waves = jnp.arange(orders, dtype=jnp.int32)[None, :]
    angle = (points * waves % lon_total).astype(jnp.float32) * (2.0 * math.pi / lon_total)
    stacked = jnp.stack([jnp.cos(angle), -jnp.sin(angle)], axis=-1)
    return stacked.reshape(lon_total, 2 * orders).astype(jnp.bfloat16)


def inverse_table(lon_total, orders):
    waves = jnp.arange(orders, dtype=jnp.int32)[:, None]
    points = jnp.arange(lon_total, dtype=jnp.int32)[None, :]
    angle = (points * waves % lon_total).astype(jnp.float32) * (2.0 * math.pi / lon_total)
    factor = jnp.where(waves == 0, 1.0, 2.0).astype(jnp.float32)
    stacked = jnp.stack([factor * jnp.cos(angle), -factor * jnp.sin(angle)], axis=1)
    return stacked.reshape(2 * orders, lon_total).astype(jnp.bfloat16)


def quadrature(lat_total, lon_total):
    lat_rows = jnp.arange(lat_total, dtype=jnp.int32).astype(jnp.float32)
    colatitude = (lat_rows + 0.5) * (math.pi / lat_total)
    return jnp.sin(colatitude) * (math.pi / lat_total / lon_total)


def legendre_table(order_ids, degrees, lat_total):
    half_rows = lat_total // 2
    lat_rows = jnp.arange(half_rows, dtype=jnp.int32).astype(jnp.float32)
    colatitude = (lat_rows + 0.5) * (math.pi / lat_total)
    cosine = jnp.cos(colatitude)[None, :]
    sine_theta = jnp.sin(colatitude)[None, :]
    orders = order_ids.astype(jnp.float32)[:, None]
    counter = jnp.arange(1, degrees + 1, dtype=jnp.int32).astype(jnp.float32)
    log_terms = jnp.log((2.0 * counter - 1.0) / (2.0 * counter))
    below = counter[None, :] <= orders
    log_start = 0.5 * jnp.log(orders + 0.5) + 0.5 * jnp.sum(
        jnp.where(below, log_terms[None, :], 0.0), axis=1, keepdims=True
    )
    log_start = log_start + orders * jnp.log(sine_theta)
    block_span = 32

    def advance(carry, block_index):
        current, previous, log_scale = carry
        emitted = []
        for offset in range(block_span):
            degree = (block_index * block_span + offset).astype(jnp.float32)
            earlier = degree - 1.0
            coef_a = jnp.sqrt(
                jnp.maximum(4.0 * degree * degree - 1.0, 1.0)
                / jnp.maximum(degree * degree - orders * orders, 1.0)
            )
            coef_b = jnp.sqrt(
                jnp.maximum(earlier * earlier - orders * orders, 0.0)
                / jnp.maximum(4.0 * earlier * earlier - 1.0, 1.0)
            )
            newest = coef_a * (cosine * current - coef_b * previous)
            is_start = degree == orders
            before = degree < orders
            newest = jnp.where(before, 0.0, jnp.where(is_start, 1.0, newest))
            log_scale = jnp.where(is_start, log_start, log_scale)
            previous = jnp.where(is_start | before, 0.0, current)
            current = newest
            emitted.append(newest * jnp.exp(log_scale))
        size_now = jnp.maximum(jnp.abs(current), jnp.abs(previous))
        safe_size = jnp.where(size_now > 0.0, size_now, 1.0)
        carry_out = (current / safe_size, previous / safe_size, log_scale + jnp.log(safe_size))
        return (carry_out, jnp.stack(emitted, axis=-1))

    zeros = jnp.zeros((order_ids.shape[0], half_rows), jnp.float32)
    blocks = jnp.arange(degrees // block_span, dtype=jnp.int32)
    unused, stacked = lax.scan(advance, (zeros, zeros, zeros), blocks)
    northern = jnp.transpose(stacked, (1, 2, 0, 3)).reshape(order_ids.shape[0], half_rows, degrees)
    degree_ids = jnp.arange(degrees, dtype=jnp.int32)
    parity = (1 - 2 * ((degree_ids[None, :] + order_ids[:, None]) % 2)).astype(jnp.float32)
    southern = northern[:, ::-1, :] * parity[:, None, :]
    return jnp.concatenate([northern, southern], axis=1).astype(jnp.bfloat16)


def convolve(padded, kernel):
    return lax.conv_general_dilated(
        padded[None],
        kernel,
        (1, 1),
        "VALID",
        dimension_numbers=("NCHW", "OIHW", "NCHW"),
        preferred_element_type=jnp.float32,
    )[0]


def conv_layer(values, kernel):
    rimmed = padded_2(values, (("lat", 1),), 1, False)
    wrapped = padded_2(rimmed, (("lon", 2),), 1, True)
    return jnp.maximum(convolve(wrapped, kernel), 0.0).astype(jnp.bfloat16)


def local(fields, conv_first, conv_second, mixing):
    lat_count = lax.axis_size("lat")
    lon_count = lax.axis_size("lon")
    row_count = fields.shape[1]
    lat_total = row_count * lat_count
    lon_total = fields.shape[2] * lon_count
    orders = lat_total // 2
    degrees = mixing.shape[0]
    per_device = orders // lat_count
    lat_index = lax.axis_index("lat")
    hidden = conv_layer(conv_layer(fields, conv_first), conv_second)
    dft_table = forward_table(lon_total, orders)
    regrouped = lax.all_to_all(hidden, "lon", split_axis=0, concat_axis=2, tiled=True)
    spectra = jnp.dot(
        regrouped.reshape(-1, lon_total), dft_table, preferred_element_type=jnp.float32
    )
    spectra = spectra.reshape(regrouped.shape[0], row_count, 2 * orders)
    row_weights = lax.dynamic_slice_in_dim(
        quadrature(lat_total, lon_total), lat_index * row_count, row_count, 0
    )
    coeffs = (spectra * row_weights[None, :, None]).astype(jnp.bfloat16)
    order_ids = lat_index * per_device + jnp.arange(per_device, dtype=jnp.int32)
    legendre = legendre_table(order_ids, degrees, lat_total)
    item_block = lax.all_to_all(coeffs, "lat", split_axis=2, concat_axis=1, tiled=True)
    pieces = item_block.reshape(item_block.shape[0], lat_total, per_device, 2)
    spectral = jnp.einsum("cjmr,mjl->lcmr", pieces, legendre, preferred_element_type=jnp.float32)
    spectral = spectral.astype(jnp.bfloat16).reshape(degrees, item_block.shape[0], 2 * per_device)
    gathered = lax.all_gather(spectral, "lon", axis=1, tiled=True)
    mixed_coef = jnp.einsum(
        "lcx,loc->lox", gathered, mixing, preferred_element_type=jnp.float32
    ).astype(jnp.bfloat16)
    out_channels = mixed_coef.shape[1]
    mixed_pieces = mixed_coef.reshape(degrees, out_channels, per_device, 2)
    synthesis = jnp.einsum(
        "lomr,mjl->ojmr", mixed_pieces, legendre, preferred_element_type=jnp.float32
    )
    synthesis = synthesis.astype(jnp.bfloat16).reshape(out_channels, lat_total, 2 * per_device)
    back_table = inverse_table(lon_total, orders)
    item_block = lax.all_to_all(synthesis, "lat", split_axis=1, concat_axis=2, tiled=True)
    product = jnp.dot(
        item_block.reshape(-1, 2 * orders), back_table, preferred_element_type=jnp.float32
    )
    return product.reshape(item_block.shape[0], row_count, lon_total).astype(jnp.bfloat16)


def solution(mesh):
    in_specs = (P("groups", "lat", "lon"), P(), P(), P(None, "lon", None))
    out_specs = P(("groups", "lon"), "lat", None)
    return jax.shard_map(local, mesh=mesh, in_specs=in_specs, out_specs=out_specs, check_vma=False)
```

profile of v0, /device:TPU:0, one launch (start us, length us, event | category | flops | bytes accessed | tf_op | source)
XLA Modules:
  0.0 80.1 jit_solution(9734672846849882325)
XLA Ops:
  0.0 1.1 %fusion.139 = (bf16[64,1,128]{2,1,0:T(2,128)(2,1)S(1)}, bf16[64,1,128]{2,1,0:T(2,128)(2,1)S(1)}) fusion(bf16[64,8,128]{2,1,0:T(8,128)(2,1)} %param.6), kind=kLoop, calls=%fused_computation.367 | loop fusion | bytes 65536 | tf_op jit(solution)/shard_map/slice | solution.py:17
  1.1 4.8 %collective-permute-start = (bf16[64,1,128]{2,1,0:T(2,128)(2,1)S(1)}, bf16[64,1,128]{2,1,0:T(2,128)(2,1)S(1)}, u32[]{:S(2)}, u32[]{:S(2)}) collective-permute-start(bf16[64,1,128]{2,1,0:T(2,128)(2,1)S(1)} %get-tuple-element.867), channel_id=1, source_target_pairs={{0,2},{2,4},{4,6},{6,8},{8,10},{10,12},{12,14},{14,16},{16,18},{18... | collective-permute-start | bytes 49160 | tf_op jit(solution)/shard_map/ppermute | solution.py:16
  5.9 1.3 %collective-permute-start.1 = (bf16[64,1,128]{2,1,0:T(2,128)(2,1)S(1)}, bf16[64,1,128]{2,1,0:T(2,128)(2,1)S(1)}, u32[]{:S(2)}, u32[]{:S(2)}) collective-permute-start(bf16[64,1,128]{2,1,0:T(2,128)(2,1)S(1)} %get-tuple-element.868), channel_id=1, source_target_pairs={{2,0},{4,2},{6,4},{8,6},{10,8},{12,10},{14,12},{16,14},{18,16},{20... | collective-permute-start | bytes 49160 | tf_op jit(solution)/shard_map/ppermute | solution.py:19
  7.4 0.2 select_reduce_fusion
  7.6 11.8 %while.23 = (s32[]{:T(128)}, f32[4,64]{1,0:T(4,128)S(1)}, f32[4,64]{1,0:T(4,128)S(1)}, f32[4,64]{1,0:T(4,128)S(1)}, f32[2,4,64,32]{2,1,3,0:T(4,128)S(1)}, /*inde...) while((s32[]{:T(128)}, f32[4,64]{1,0:T(4,128)S(1)}, ...), condition=%wide.region_2.3_spmd.clone.clone.clone.clone, body=%wide.region_1.2_spmd.clone.clone.clone.clone.sunk | while | flops 110306 | bytes 652777 | solution.py:92
  7.6 0.7 dynamic_slice.17
  13.5 0.7 dynamic_slice.17
  19.7 0.9 %copy-done.1 = bf16[64,8,128]{2,1,0:T(8,128)(2,1)S(1)} copy-done((bf16[64,8,128]{2,1,0:T(8,128)(2,1)S(1)}, bf16[64,8,128]{2,1,0:T(8,128)(2,1)}, u32[]{:S(2)}) %copy-start.1) | copy-done | bytes 131096
  20.9 0.5 collective-permute-start.3
  21.4 0.3 negate_convert_fusion
  21.7 0.7 collective-permute-done.2
  22.5 0.4 collective-permute-done.3
  22.8 0.6 maximum_bitcast_fusion
  23.4 0.4 copy.163
  24.2 0.8 %copy-done.2 = bf16[64,64,3,3]{1,0,3,2:T(8,128)(2,1)S(1)} copy-done((bf16[64,64,3,3]{1,0,3,2:T(8,128)(2,1)S(1)}, bf16[64,64,3,3]{1,0,3,2:T(8,128)(2,1)}, u32[]{:S(2)}) %copy-start.2) | copy-done | bytes 73752
  25.0 0.8 %fusion.46 = bf16[8,8,17,64]{3,1,2,0:T(8,128)(2,1)S(1)} fusion(bf16[64,64,3,3]{1,0,3,2:T(8,128)(2,1)S(1)} %copy-done.2, bf16[64,10,1,7,2]{0,3,4,1,2:T(8,128)(2,1)S(1)} %slice.38, bf16[64,10,1,8,17]{0,3,4,1,2:T(8,128)(2,1)S(1)} %copy.134, pred[8,17]{0,1:T(8,128)(4,1)S(1)} %copy-done.4), kind=kOutput, calls=%fused_computation.245 | convolution fusion | flops 81008640 | bytes 405128 | tf_op jit(solution)/shard_map/conv_general_dilated | solution.py:101
  26.0 4.5 %collective-permute-start.4 = (bf16[64,1,128]{0,1,2:T(2,128)(2,1)S(1)}, bf16[64,1,128]{0,1,2:T(2,128)(2,1)S(1)}, u32[]{:S(2)}, u32[]{:S(2)}) collective-permute-start(bf16[64,1,128]{0,1,2:T(2,128)(2,1)S(1)} %get-tuple-element.861), channel_id=1, source_target_pairs={{0,2},{2,4},{4,6},{6,8},{8,10},{10,12},{12,14},{14,16},{16,18},{18... | collective-permute-start | bytes 49160 | tf_op jit(solution)/shard_map/ppermute | solution.py:16
  30.5 1.3 %collective-permute-start.5 = (bf16[64,1,128]{0,1,2:T(2,128)(2,1)S(1)}, bf16[64,1,128]{0,1,2:T(2,128)(2,1)S(1)}, u32[]{:S(2)}, u32[]{:S(2)}) collective-permute-start(bf16[64,1,128]{0,1,2:T(2,128)(2,1)S(1)} %get-tuple-element.862), channel_id=1, source_target_pairs={{2,0},{4,2},{6,4},{8,6},{10,8},{12,10},{14,12},{16,14},{18,16},{20... | collective-permute-start | bytes 49160 | tf_op jit(solution)/shard_map/ppermute | solution.py:19
  31.9 0.2 copy.137
  32.1 0.4 collective-permute-done.4
  32.5 4.6 %collective-permute-done.5 = bf16[64,1,128]{0,1,2:T(2,128)(2,1)S(1)} collective-permute-done((bf16[64,1,128]{0,1,2:T(2,128)(2,1)S(1)}, bf16[64,1,128]{0,1,2:T(2,128)(2,1)S(1)}, u32[]{:S(2)}, u32[]{:S(2)}) %collective-permute-start.5) | collective-permute-done | bytes 16416 | tf_op jit(solution)/shard_map/ppermute | solution.py:19
  37.4 0.5 collective-permute-start.7
  38.2 0.6 collective-permute-done.6
  38.8 0.2 collective-permute-done.7
  39.0 0.2 maximum_bitcast_fusion.1
  39.3 0.3 copy.164
  39.8 0.8 %copy-done.3 = bf16[64,64,3,3]{1,0,3,2:T(8,128)(2,1)S(1)} copy-done((bf16[64,64,3,3]{1,0,3,2:T(8,128)(2,1)S(1)}, bf16[64,64,3,3]{1,0,3,2:T(8,128)(2,1)}, u32[]{:S(2)}) %copy-start.3) | copy-done | bytes 73752
  40.6 0.8 %fusion.47 = bf16[8,8,17,64]{3,1,2,0:T(8,128)(2,1)S(1)} fusion(bf16[64,64,3,3]{1,0,3,2:T(8,128)(2,1)S(1)} %copy-done.3, bf16[64,10,1,7,2]{0,3,4,1,2:T(8,128)(2,1)S(1)} %slice.44, bf16[64,10,1,8,17]{0,3,4,1,2:T(8,128)(2,1)S(1)} %copy.141, pred[8,17]{0,1:T(8,128)(4,1)S(1)} %copy-done.4), kind=kOutput, calls=%fused_computation.246 | convolution fusion | flops 81008640 | bytes 405128 | tf_op jit(solution)/shard_map/conv_general_dilated | solution.py:101
  41.5 0.2 copy.143
  41.8 3.8 %all_to_all.45 = bf16[64,8,128]{2,1,0:T(8,128)(2,1)S(1)} all-to-all(bf16[64,8,128]{2,1,0:T(8,128)(2,1)S(1)} %copy.143), channel_id=1, replica_groups=mesh['groups'=1,'lat'=16,'lon'=2] {'lon'}, dimensions={0} | all-to-all | bytes 262144 | tf_op jit(solution)/shard_map/all_to_all | solution.py:129
  45.6 0.2 fusion.48
  45.8 0.2 copy.147
  46.0 0.9 %reshape.2414 = bf16[16,2,1024]{2,1,0:T(2,128)(2,1)} reshape(bf16[128,8,32]{2,1,0:T(8,128)(2,1)S(1)} %bitcast.697) | data formatting | bytes 131072
  46.9 9.1 %all-to-all-start.1 = ((bf16[16,2,1024]{2,1,0:T(2,128)(2,1)}), bf16[16,2,1024]{2,1,0:T(2,128)(2,1)S(1)}, u32[]{:S(2)}, u32[]{:S(2)}) async-start(bf16[16,2,1024]{2,1,0:T(2,128)(2,1)} %reshape.2414), calls=%async_computation.1 | async-start | bytes 131072 | tf_op jit(solution)/shard_map/all_to_all | solution.py:140
  56.0 7.5 %all-to-all-done.1 = bf16[16,2,1024]{2,1,0:T(2,128)(2,1)S(1)} async-done(((bf16[16,2,1024]{2,1,0:T(2,128)(2,1)}), bf16[16,2,1024]{2,1,0:T(2,128)(2,1)S(1)}, u32[]{:S(2)}, u32[]{:S(2)}) %all-to-all-start.1) | async-done | bytes 65568 | tf_op jit(solution)/shard_map/all_to_all | solution.py:140
  63.5 0.2 reshape.2415
  63.8 0.2 convolution_convert_fusion.3
  64.1 1.9 %all_gather.3 = bf16[64,64,8]{0,2,1:T(8,128)(2,1)S(1)} all-gather(bf16[64,32,8]{0,2,1:T(8,128)(2,1)S(1)} %copy.151), channel_id=1, replica_groups=mesh['groups'=1,'lat'=16,'lon'=2] {'lon'}, dimensions={1}, use_global_device_ids=true | all-gather | bytes 98304 | tf_op jit(solution)/shard_map/all_gather | solution.py:144
  66.0 0.2 copy.152
  66.1 0.4 convolution_convert_fusion
  66.5 0.3 convolution_convert_fusion.2
  66.8 0.2 copy.154
  67.0 0.9 %reshape.2416 = bf16[16,2,1024]{2,1,0:T(2,128)(2,1)} reshape(bf16[128,8,32]{2,1,0:T(8,128)(2,1)S(1)} %bitcast.698) | data formatting | bytes 131072
  67.9 3.5 %all-to-all-start.2 = ((bf16[16,2,1024]{2,1,0:T(2,128)(2,1)}), bf16[16,2,1024]{2,1,0:T(2,128)(2,1)S(1)}, u32[]{:S(2)}, u32[]{:S(2)}) async-start(bf16[16,2,1024]{2,1,0:T(2,128)(2,1)} %reshape.2416), calls=%async_computation.2 | async-start | bytes 131072 | tf_op jit(solution)/shard_map/all_to_all | solution.py:155
  71.4 0.3 multiply_convert_fusion.1
  71.8 7.1 %all-to-all-done.2 = bf16[16,2,1024]{2,1,0:T(2,128)(2,1)S(1)} async-done(((bf16[16,2,1024]{2,1,0:T(2,128)(2,1)}), bf16[16,2,1024]{2,1,0:T(2,128)(2,1)S(1)}, u32[]{:S(2)}, u32[]{:S(2)}) %all-to-all-start.2) | async-done | bytes 65568 | tf_op jit(solution)/shard_map/all_to_all | solution.py:155
  78.9 0.2 reshape.2417
  79.3 0.8 %convolution_convert_fusion.1 = bf16[32,8,256]{2,1,0:T(8,128)(2,1)} fusion(bf16[32,8,128]{2,1,0:T(8,128)(2,1)S(1)} %copy.157, bf16[128,256,1]{1,0,2:T(8,128)(2,1)S(1)} %reshape.2412), kind=kOutput, calls=%fused_computation.248 | convolution fusion | flops 16842752 | bytes 262144 | tf_op jit(solution)/shard_map/dot_general | solution.py:156
  (225 shorter events, 10.0 us)
Async XLA Ops:
  0.0 66.1 %copy-start = (bf16[64,32,64]{2,1,0:T(8,128)(2,1)S(1)}, bf16[64,32,64]{2,1,0:T(8,128)(2,1)}, u32[]{:S(2)}) copy-start(bf16[64,32,64]{2,1,0:T(8,128)(2,1)} %param.9) | copy-start | bytes 786436
  1.1 18.6 %collective-permute-start = (bf16[64,1,128]{2,1,0:T(2,128)(2,1)S(1)}, bf16[64,1,128]{2,1,0:T(2,128)(2,1)S(1)}, u32[]{:S(2)}, u32[]{:S(2)}) collective-permute-start(bf16[64,1,128]{2,1,0:T(2,128)(2,1)S(1)} %get-tuple-element.867), channel_id=1, source_target_pairs={{0,2},{2,4},{4,6},{6,8},{8,10},{10,12},{12,14},{14,16},{16,18},{18... | collective-permute-start | bytes 49160 | tf_op jit(solution)/shard_map/ppermute | solution.py:16
  5.9 13.8 %collective-permute-start.1 = (bf16[64,1,128]{2,1,0:T(2,128)(2,1)S(1)}, bf16[64,1,128]{2,1,0:T(2,128)(2,1)S(1)}, u32[]{:S(2)}, u32[]{:S(2)}) collective-permute-start(bf16[64,1,128]{2,1,0:T(2,128)(2,1)S(1)} %get-tuple-element.868), channel_id=1, source_target_pairs={{2,0},{4,2},{6,4},{8,6},{10,8},{12,10},{14,12},{16,14},{18,16},{20... | collective-permute-start | bytes 49160 | tf_op jit(solution)/shard_map/ppermute | solution.py:19
  19.6 0.9 %copy-start.1 = (bf16[64,8,128]{2,1,0:T(8,128)(2,1)S(1)}, bf16[64,8,128]{2,1,0:T(8,128)(2,1)}, u32[]{:S(2)}) copy-start(bf16[64,8,128]{2,1,0:T(8,128)(2,1)} %param.6) | copy-start | bytes 393220
  20.9 1.6 %collective-permute-start.2 = (bf16[64,10,1]{2,1,0:T(8,128)(2,1)S(1)}, bf16[64,10,1]{2,1,0:T(8,128)(2,1)S(1)}, u32[]{:S(2)}, u32[]{:S(2)}) collective-permute-start(bf16[64,10,1]{2,1,0:T(8,128)(2,1)S(1)} %get-tuple-element.863), channel_id=1, source_target_pairs={{0,1},{1,0},{2,3},{3,2},{4,5},{5,4},{6,7},{7,6},{8,9},{9,8},{10,11... | collective-permute-start | bytes 3848 | tf_op jit(solution)/shard_map/ppermute | solution.py:16
  20.9 1.9 %collective-permute-start.3 = (bf16[64,10,1]{2,1,0:T(8,128)(2,1)S(1)}, bf16[64,10,1]{2,1,0:T(8,128)(2,1)S(1)}, u32[]{:S(2)}, u32[]{:S(2)}) collective-permute-start(bf16[64,10,1]{2,1,0:T(8,128)(2,1)S(1)} %get-tuple-element.864), channel_id=1, source_target_pairs={{1,0},{0,1},{3,2},{2,3},{5,4},{4,5},{7,6},{6,7},{9,8},{8,9},{11,10... | collective-permute-start | bytes 3848 | tf_op jit(solution)/shard_map/ppermute | solution.py:19
  24.1 0.9 %copy-start.2 = (bf16[64,64,3,3]{1,0,3,2:T(8,128)(2,1)S(1)}, bf16[64,64,3,3]{1,0,3,2:T(8,128)(2,1)}, u32[]{:S(2)}) copy-start(bf16[64,64,3,3]{1,0,3,2:T(8,128)(2,1)} %param.7) | copy-start | bytes 221188
  24.1 0.8 %copy-start.4 = (pred[8,17]{0,1:T(8,128)(4,1)S(1)}, pred[8,17]{0,1:T(8,128)(4,1)}, u32[]{:S(2)}) copy-start(pred[8,17]{0,1:T(8,128)(4,1)} %constant.444) | copy-start | bytes 412
  26.0 6.4 %collective-permute-start.4 = (bf16[64,1,128]{0,1,2:T(2,128)(2,1)S(1)}, bf16[64,1,128]{0,1,2:T(2,128)(2,1)S(1)}, u32[]{:S(2)}, u32[]{:S(2)}) collective-permute-start(bf16[64,1,128]{0,1,2:T(2,128)(2,1)S(1)} %get-tuple-element.861), channel_id=1, source_target_pairs={{0,2},{2,4},{4,6},{6,8},{8,10},{10,12},{12,14},{14,16},{16,18},{18... | collective-permute-start | bytes 49160 | tf_op jit(solution)/shard_map/ppermute | solution.py:16
  30.5 6.5 %collective-permute-start.5 = (bf16[64,1,128]{0,1,2:T(2,128)(2,1)S(1)}, bf16[64,1,128]{0,1,2:T(2,128)(2,1)S(1)}, u32[]{:S(2)}, u32[]{:S(2)}) collective-permute-start(bf16[64,1,128]{0,1,2:T(2,128)(2,1)S(1)} %get-tuple-element.862), channel_id=1, source_target_pairs={{2,0},{4,2},{6,4},{8,6},{10,8},{12,10},{14,12},{16,14},{18,16},{20... | collective-permute-start | bytes 49160 | tf_op jit(solution)/shard_map/ppermute | solution.py:19
  37.3 1.5 %collective-permute-start.6 = (bf16[64,10,1]{2,0,1:T(8,128)(2,1)S(1)}, bf16[64,10,1]{2,0,1:T(8,128)(2,1)S(1)}, u32[]{:S(2)}, u32[]{:S(2)}) collective-permute-start(bf16[64,10,1]{2,0,1:T(8,128)(2,1)S(1)} %get-tuple-element.865), channel_id=1, source_target_pairs={{0,1},{1,0},{2,3},{3,2},{4,5},{5,4},{6,7},{7,6},{8,9},{9,8},{10,11... | collective-permute-start | bytes 3848 | tf_op jit(solution)/shard_map/ppermute | solution.py:16
  37.4 1.6 %collective-permute-start.7 = (bf16[64,10,1]{2,0,1:T(8,128)(2,1)S(1)}, bf16[64,10,1]{2,0,1:T(8,128)(2,1)S(1)}, u32[]{:S(2)}, u32[]{:S(2)}) collective-permute-start(bf16[64,10,1]{2,0,1:T(8,128)(2,1)S(1)} %get-tuple-element.866), channel_id=1, source_target_pairs={{1,0},{0,1},{3,2},{2,3},{5,4},{4,5},{7,6},{6,7},{9,8},{8,9},{11,10... | collective-permute-start | bytes 3848 | tf_op jit(solution)/shard_map/ppermute | solution.py:19
  39.7 0.9 %copy-start.3 = (bf16[64,64,3,3]{1,0,3,2:T(8,128)(2,1)S(1)}, bf16[64,64,3,3]{1,0,3,2:T(8,128)(2,1)}, u32[]{:S(2)}) copy-start(bf16[64,64,3,3]{1,0,3,2:T(8,128)(2,1)} %param.8) | copy-start | bytes 221188
  46.9 16.6 %all-to-all-start.1 = ((bf16[16,2,1024]{2,1,0:T(2,128)(2,1)}), bf16[16,2,1024]{2,1,0:T(2,128)(2,1)S(1)}, u32[]{:S(2)}, u32[]{:S(2)}) async-start(bf16[16,2,1024]{2,1,0:T(2,128)(2,1)} %reshape.2414), calls=%async_computation.1 | async-start | bytes 131072 | tf_op jit(solution)/shard_map/all_to_all | solution.py:140
  67.9 11.0 %all-to-all-start.2 = ((bf16[16,2,1024]{2,1,0:T(2,128)(2,1)}), bf16[16,2,1024]{2,1,0:T(2,128)(2,1)S(1)}, u32[]{:S(2)}, u32[]{:S(2)}) async-start(bf16[16,2,1024]{2,1,0:T(2,128)(2,1)} %reshape.2416), calls=%async_computation.2 | async-start | bytes 131072 | tf_op jit(solution)/shard_map/all_to_all | solution.py:155
where the time goes:
time: 80.6 us; the launch traced here: 80.1 us
  starting transfers between devices  25.7 us (32%)
  waiting for transfers between devices  21.5 us (27%)
  local copies, waits for them, and re-layouts  10.6 us (13%)
  other arithmetic  9.55 us (12%)
  blocking collectives  5.74 us (7%)
  matrix products  3.51 us (4%)
  loops' own time  2.99 us (4%)
    ppermute x4, starting transfers between devices, padded_2(): lax.ppermute(lax.slice_in_dim(block, block.shape[dim] - width, None, axis...  9.54 us
    all_to_all x1, starting transfers between devices, local(): lax.all_to_all(coeffs, 'lat', split_axis=2, concat_axis=1, tiled=True)  9.07 us
    all_to_all x1, waiting for transfers between devices, local(): lax.all_to_all(coeffs, 'lat', split_axis=2, concat_axis=1, tiled=True)  7.51 us
    all_to_all x1, waiting for transfers between devices, local(): lax.all_to_all(synthesis, 'lat', split_axis=1, concat_axis=2, tiled=True)  7.08 us
    while x62, other arithmetic  5.6 us
    unnamed x16, local copies, waits for them, and re-layouts  5.39 us
    ppermute x4, waiting for transfers between devices, padded_2(): lax.ppermute(lax.slice_in_dim(block, 0, width, axis=dim), axis, backward)  5.17 us
    all_to_all x1, blocking collectives, local(): lax.all_to_all(hidden, 'lon', split_axis=0, concat_axis=2, tiled=True)  3.84 us
  transfers between devices with their start and end apart: 10, of which 8 were waited for; matrix products, arithmetic and copies ran while one was open for 13% of the time, Pallas kernels for 0%

commit v1 on v0

--- a/solution.py
+++ b/solution.py
@@ -4,21 +4,6 @@
 import jax.numpy as jnp
 from jax import lax
 from jax.sharding import PartitionSpec as P
-
-
-def padded_2(block, sides, width, periodic):
-    for axis, dim in sides:
-        count = lax.axis_size(axis)
-        forward = [(i, i + 1) for i in range(count - 1)]
-        if periodic:
-            forward.append((count - 1, 0))
-        backward = [(target, source) for source, target in forward]
-        low = lax.ppermute(
-            lax.slice_in_dim(block, block.shape[dim] - width, None, axis=dim), axis, forward
-        )
-        high = lax.ppermute(lax.slice_in_dim(block, 0, width, axis=dim), axis, backward)
-        block = jnp.concatenate([low, block, high], axis=dim)
-    return block
 
 
 def forward_table(lon_total, orders):
@@ -96,8 +81,8 @@
     southern = northern[:, ::-1, :] * parity[:, None, :]
     return jnp.concatenate([northern, southern], axis=1).astype(jnp.bfloat16)
 
-
 def convolve(padded, kernel):
+    padded = jnp.concatenate([padded[:, :, -1:], padded, padded[:, :, :1]], axis=2)
     return lax.conv_general_dilated(
         padded[None],
         kernel,
@@ -108,55 +93,82 @@
     )[0]
 
 
-def conv_layer(values, kernel):
-    rimmed = padded_2(values, (("lat", 1),), 1, False)
-    wrapped = padded_2(rimmed, (("lon", 2),), 1, True)
-    return jnp.maximum(convolve(wrapped, kernel), 0.0).astype(jnp.bfloat16)
-
-
 def local(fields, conv_first, conv_second, mixing):
     lat_count = lax.axis_size("lat")
     lon_count = lax.axis_size("lon")
-    row_count = fields.shape[1]
+    assert lon_count == 2
+    channels, row_count, _ = fields.shape
     lat_total = row_count * lat_count
     lon_total = fields.shape[2] * lon_count
     orders = lat_total // 2
     degrees = mixing.shape[0]
-    per_device = orders // lat_count
+    owners = lat_count * lon_count
+    per_device = orders // owners
+    half = row_count // 2
     lat_index = lax.axis_index("lat")
-    hidden = conv_layer(conv_layer(fields, conv_first), conv_second)
-    dft_table = forward_table(lon_total, orders)
-    regrouped = lax.all_to_all(hidden, "lon", split_axis=0, concat_axis=2, tiled=True)
-    spectra = jnp.dot(
-        regrouped.reshape(-1, lon_total), dft_table, preferred_element_type=jnp.float32
+    side = lax.axis_index("lon")
+    swap = [(0, 1), (1, 0)]
+    both = ("lat", "lon")
+
+    other = lax.ppermute(fields, "lon", swap)
+    other_mixing = lax.ppermute(mixing, "lon", swap)
+    upper = side == 0
+    full = jnp.concatenate(
+        [jnp.where(upper, fields, other), jnp.where(upper, other, fields)], axis=2
     )
-    spectra = spectra.reshape(regrouped.shape[0], row_count, 2 * orders)
-    row_weights = lax.dynamic_slice_in_dim(
-        quadrature(lat_total, lon_total), lat_index * row_count, row_count, 0
+    message = jnp.where(upper, full[:, :2], full[:, row_count - 2 :])
+    pairs = []
+    for i in range(lat_count - 1):
+        pairs.append((2 * i + 1, 2 * (i + 1)))
+        pairs.append((2 * (i + 1), 2 * i + 1))
+    halo = lax.ppermute(message, both, pairs)
+    rows = jnp.where(
+        upper,
+        jnp.concatenate([halo, full[:, : half + 2]], axis=1),
+        jnp.concatenate([full[:, half - 2 :], halo], axis=1),
     )
-    coeffs = (spectra * row_weights[None, :, None]).astype(jnp.bfloat16)
-    order_ids = lat_index * per_device + jnp.arange(per_device, dtype=jnp.int32)
+
+    first_row = lat_index * row_count + side * half
+    hidden = jnp.maximum(convolve(rows, conv_first), 0.0)
+    row_ids = first_row - 1 + jnp.arange(half + 2, dtype=jnp.int32)
+    inside = (row_ids >= 0) & (row_ids < lat_total)
+    hidden = jnp.where(inside[None, :, None], hidden, 0.0).astype(jnp.bfloat16)
+    hidden = jnp.maximum(convolve(hidden, conv_second), 0.0).astype(jnp.bfloat16)
+
+    table = forward_table(lon_total, orders).reshape(lon_total, owners, per_device, 2)
+    spectra = jnp.einsum("cjk,kdmr->dmjrc", hidden, table, preferred_element_type=jnp.float32)
+    weights = lax.dynamic_slice_in_dim(quadrature(lat_total, lon_total), first_row, half, 0)
+    coeffs = (spectra * weights[None, None, :, None, None]).astype(jnp.bfloat16)
+    coeffs = coeffs.reshape(owners, per_device * half, 2 * channels)
+    pieces = lax.all_to_all(coeffs, both, split_axis=0, concat_axis=0, tiled=True)
+    pieces = pieces.reshape(owners, per_device, half, 2, channels)
+
+    order_ids = (2 * lat_index + side) * per_device + jnp.arange(per_device, dtype=jnp.int32)
     legendre = legendre_table(order_ids, degrees, lat_total)
-    item_block = lax.all_to_all(coeffs, "lat", split_axis=2, concat_axis=1, tiled=True)
-    pieces = item_block.reshape(item_block.shape[0], lat_total, per_device, 2)
-    spectral = jnp.einsum("cjmr,mjl->lcmr", pieces, legendre, preferred_element_type=jnp.float32)
-    spectral = spectral.astype(jnp.bfloat16).reshape(degrees, item_block.shape[0], 2 * per_device)
-    gathered = lax.all_gather(spectral, "lon", axis=1, tiled=True)
-    mixed_coef = jnp.einsum(
-        "lcx,loc->lox", gathered, mixing, preferred_element_type=jnp.float32
+    mixing = jnp.concatenate(
+        [jnp.where(upper, mixing, other_mixing), jnp.where(upper, other_mixing, mixing)], axis=1
+    )
+    split = legendre.reshape(per_device, owners, half, degrees)
+    spectral = jnp.einsum(
+        "dmjrc,mdjl->lcmr", pieces, split, preferred_element_type=jnp.float32
     ).astype(jnp.bfloat16)
-    out_channels = mixed_coef.shape[1]
-    mixed_pieces = mixed_coef.reshape(degrees, out_channels, per_device, 2)
+    spectral = spectral.reshape(degrees, channels, 2 * per_device)
+    mixed = jnp.einsum(
+        "lcx,loc->lox", spectral, mixing, preferred_element_type=jnp.float32
+    ).astype(jnp.bfloat16)
+    mixed = mixed.reshape(degrees, 2, channels // 2, per_device, 2)
+    bands = legendre.reshape(per_device, lat_count, row_count, degrees)
     synthesis = jnp.einsum(
-        "lomr,mjl->ojmr", mixed_pieces, legendre, preferred_element_type=jnp.float32
-    )
-    synthesis = synthesis.astype(jnp.bfloat16).reshape(out_channels, lat_total, 2 * per_device)
-    back_table = inverse_table(lon_total, orders)
-    item_block = lax.all_to_all(synthesis, "lat", split_axis=1, concat_axis=2, tiled=True)
-    product = jnp.dot(
-        item_block.reshape(-1, 2 * orders), back_table, preferred_element_type=jnp.float32
-    )
-    return product.reshape(item_block.shape[0], row_count, lon_total).astype(jnp.bfloat16)
+        "lhomr,mbjl->bhjmro", mixed, bands, preferred_element_type=jnp.float32
+    ).astype(jnp.bfloat16)
+    synthesis = synthesis.reshape(owners, row_count, per_device * channels)
+
+    back = lax.all_to_all(synthesis, both, split_axis=0, concat_axis=0, tiled=True)
+    back = back.reshape(owners, row_count, per_device, 2, channels // 2)
+    inverse = inverse_table(lon_total, orders).reshape(owners, per_device, 2, lon_total)
+    return jnp.einsum(
+        "djmro,dmrk->ojk", back, inverse, preferred_element_type=jnp.float32
+    ).astype(jnp.bfloat16)
 
 
 def solution(mesh):

time: 80.6 us -> 58.2 us (0.72)
  starting transfers between devices: 25.7 us -> 17.8 us
  waiting for transfers between devices: 21.5 us -> 14.4 us
  blocking collectives: 5.74 us -> 0 us
  local copies, waits for them, and re-layouts: 10.6 us -> 8.36 us
  other arithmetic: 9.55 us -> 10.5 us
    ppermute x8 -> x3, starting transfers between devices: 13.1 us -> 1.27 us  [the longest x1 0.67 us: local(): halo = lax.ppermute(message, both, pairs)]
    ppermute x8 -> x3, waiting for transfers between devices: 6.93 us -> 0.01 us  [the longest x1 0.01 us: local(): other = lax.ppermute(fields, 'lon', swap)]
    all_to_all x2, starting transfers between devices: 12.6 us -> 16.5 us  [the longest x1 14 us: local(): lax.all_to_all(coeffs, both, split_axis=0, concat_axis=0, tiled=True)]
    all_to_all x1 -> x0, blocking collectives: 3.84 us -> none  [local(): lax.all_to_all(hidden, 'lon', split_axis=0, concat_axis=2, tiled=True)]
    unnamed x16 -> x10, local copies, waits for them, and re-layouts: 5.39 us -> 2.76 us
    all_gather x1 -> x0, blocking collectives: 1.9 us -> none  [local(): gathered = lax.all_gather(spectral, 'lon', axis=1, tiled=True)]
    reshape x2 -> x4, local copies, waits for them, and re-layouts: 0.24 us -> 1.8 us  [the longest x1 0.81 us: local(): synthesis = synthesis.reshape(owners, row_count, per_device * channels)]
    slice x4 -> x2, local copies, waits for them, and re-layouts: 1.42 us -> 0.01 us  [convolve(): padded[:, :, -1:]]
  transfers between devices with their start and end apart: 10 -> 5, of which waited for: 8 -> 2; matrix products, arithmetic and copies ran while one was open for 13% -> 28% of each run, Pallas kernels for 0% -> 0%
where the time goes in v1:
time: 58.2 us; the launch traced here: 57.9 us
  starting transfers between devices  17.8 us (31%)
  waiting for transfers between devices  14.4 us (25%)
  other arithmetic  10.5 us (18%)
  local copies, waits for them, and re-layouts  8.36 us (14%)
  matrix products  3.46 us (6%)
  loops' own time  2.99 us (5%)
    all_to_all x1, starting transfers between devices, local(): lax.all_to_all(coeffs, both, split_axis=0, concat_axis=0, tiled=True)  14 us
    all_to_all x1, waiting for transfers between devices, local(): lax.all_to_all(coeffs, both, split_axis=0, concat_axis=0, tiled=True)  7.31 us
    all_to_all x1, waiting for transfers between devices, local(): lax.all_to_all(synthesis, both, split_axis=0, concat_axis=0, tiled=True)  7.06 us
    while x62, other arithmetic  5.59 us
    another operation x1, loops' own time, legendre_table(): unused, stacked = lax.scan(advance, (zeros, zeros, zeros), blocks)  2.99 us
    unnamed x10, local copies, waits for them, and re-layouts  2.76 us
    all_to_all x1, starting transfers between devices, local(): lax.all_to_all(synthesis, both, split_axis=0, concat_axis=0, tiled=True)  2.57 us
    conv_general_dilated x2, matrix products, convolve(): lax.conv_general_dilated(padded[None], kernel, (1, 1), 'VALID', dimension...  1.89 us
  transfers between devices with their start and end apart: 5, of which 2 were waited for; matrix products, arithmetic and copies ran while one was open for 28% of the time, Pallas kernels for 0%

profile of v1, /device:TPU:0, one launch (start us, length us, event | category | flops | bytes accessed | tf_op | source)
XLA Modules:
  0.0 57.9 jit_solution(508549932198875103)
XLA Ops:
  0.0 1.2 %copy.78 = bf16[64,8,128]{0,1,2:T(8,128)(2,1)S(1)} copy(bf16[64,8,128]{2,1,0:T(8,128)(2,1)} %param.6) | data formatting | bytes 262144 | tf_op args[0]
  1.2 0.5 collective-permute-start.1
  2.0 0.3 cosine_convert_fusion
  2.3 0.2 fusion.102
  2.5 11.9 %while.23 = (s32[]{:T(128)}, f32[2,64]{1,0:T(2,128)S(1)}, f32[2,64]{1,0:T(2,128)S(1)}, f32[2,64]{1,0:T(2,128)S(1)}, f32[2,2,64,32]{2,3,0,1:T(8,128)S(1)}, /*inde...) while((s32[]{:T(128)}, f32[2,64]{1,0:T(2,128)S(1)}, ...), condition=%wide.region_2.3_spmd.clone.clone.clone.clone, body=%wide.region_1.2_spmd.clone.clone.clone.clone.sunk | while | flops 53922 | bytes 414673 | solution.py:77
  2.6 0.7 %dynamic_slice.17 = s32[1]{0:T(128)} dynamic-slice(s32[2]{0:T(128)S(1)} %get-tuple-element.1514, s32[]{:T(128)} %get-tuple-element.1462), dynamic_slice_sizes={1} | dynamic-slice | bytes 12 | tf_op jit(solution)/shard_map/while/body/jit(dynamic_index_in_dim)/dynamic_slice | solution.py:77
  4.3 0.1 constant_dynamic-update-slice_fusion.66
  4.9 0.1 constant_dynamic-update-slice_fusion.70
  6.0 0.1 constant_dynamic-update-slice_fusion.78
  6.5 0.1 constant_dynamic-update-slice_fusion.82
  7.1 0.1 constant_dynamic-update-slice_fusion.86
  8.5 0.7 %dynamic_slice.17 = s32[1]{0:T(128)} dynamic-slice(s32[2]{0:T(128)S(1)} %get-tuple-element.1514, s32[]{:T(128)} %get-tuple-element.1462), dynamic_slice_sizes={1} | dynamic-slice | bytes 12 | tf_op jit(solution)/shard_map/while/body/jit(dynamic_index_in_dim)/dynamic_slice | solution.py:77
  10.3 0.1 constant_dynamic-update-slice_fusion.66
  14.8 0.1 copy.75
  15.1 0.3 broadcast_select_fusion.6
  15.4 0.7 %collective-permute-start.2 = (bf16[64,2,256]{0,1,2:T(2,128)(2,1)S(1)}, bf16[64,2,256]{0,1,2:T(2,128)(2,1)S(1)}, u32[]{:S(2)}, u32[]{:S(2)}) collective-permute-start(bf16[64,2,256]{0,1,2:T(2,128)(2,1)S(1)} %broadcast_select_fusion.6), channel_id=1, source_target_pairs={{1,2},{2,1},{3,4},{4,3},{5,6},{6,5},{7,8},{8,7},{9,10},{10,9},{11,... | collective-permute-start | bytes 196616 | tf_op jit(solution)/shard_map/ppermute | solution.py:124
  16.1 0.1 fusion.66
  16.2 0.7 %fusion.68 = bf16[64,8,256]{0,1,2:T(8,128)(2,1)S(1)} fusion(bf16[64,8,128]{0,1,2:T(8,128)(2,1)S(1)} %get-tuple-element.869, bf16[64,8,128]{0,1,2:T(8,128)(2,1)S(1)} %get-tuple-element.868, bf16[64,6,256]{0,1,2:T(8,128)(2,1)S(1)} %fusion.66, bf16[64,2,256]{0,1,2:T(2,128)(2,1)S(1)} %collective-permute-done.2, pred[]{:T(512)S(6)} %eq.733), kind=kLoop, calls=%fused_computation.283 | loop fusion | flops 1441792 | bytes 786433 | tf_op jit(solution)/shard_map/jit(_where)/select_n | solution.py:125
  16.9 0.1 maximum_bitcast_fusion
  17.0 0.1 pad
  17.3 0.6 copy-done.3
  17.8 1.1 %fusion.44 = bf16[6,8,33,64]{3,1,2,0:T(8,128)(2,1)S(1)} fusion(bf16[64,64,3,3]{1,0,3,2:T(8,128)(2,1)S(1)} %copy-done, bf16[64,8,1,7,2]{0,3,4,1,2:T(8,128)(2,1)S(1)} %slice.44, bf16[64,8,1,8,33]{0,3,4,1,2:T(8,128)(2,1)S(1)} %copy.81, pred[8,33]{0,1:T(8,128)(4,1)S(1)} %copy-done.3), kind=kOutput, calls=%fused_computation.243 | convolution fusion | flops 117949440 | bytes 561416 | tf_op jit(solution)/shard_map/conv_general_dilated | solution.py:86
  19.0 0.2 reshape.2391
  19.2 0.1 fusion.59
  19.4 0.1 maximum_bitcast_fusion.1
  19.6 0.1 reshape.2394
  19.8 0.8 %copy-done.2 = bf16[64,64,3,3]{1,0,3,2:T(8,128)(2,1)S(1)} copy-done((bf16[64,64,3,3]{1,0,3,2:T(8,128)(2,1)S(1)}, bf16[64,64,3,3]{1,0,3,2:T(8,128)(2,1)}, u32[]{:S(2)}) %copy-start.2) | copy-done | bytes 73752
  20.6 0.8 %fusion.46 = bf16[4,8,33,64]{3,1,2,0:T(8,128)(2,1)S(1)} fusion(bf16[64,64,3,3]{1,0,3,2:T(8,128)(2,1)S(1)} %copy-done.2, bf16[64,6,1,7,2]{0,3,4,1,2:T(8,128)(2,1)S(1)} %slice.48, bf16[64,6,1,8,33]{0,3,4,1,2:T(8,128)(2,1)S(1)} %copy.84, pred[8,33]{0,1:T(8,128)(4,1)S(1)} %copy-done.3), kind=kOutput, calls=%fused_computation.246 | convolution fusion | flops 78704640 | bytes 422664 | tf_op jit(solution)/shard_map/conv_general_dilated | solution.py:86
  21.4 0.1 copy.85
  21.6 0.2 copy.113
  21.8 0.2 fusion.51
  22.0 0.1 copy.87
  22.2 0.7 %reshape.2379 = bf16[32,8,128]{2,1,0:T(8,128)(2,1)} reshape(bf16[32,2,4,2,64]{4,3,2,1,0:T(2,128)(2,1)S(1)} %copy.87) | data formatting | bytes 131072 | tf_op jit(solution)/shard_map/reshape | solution.py:142
  22.9 14.0 %all-to-all-start = ((bf16[32,8,128]{2,1,0:T(8,128)(2,1)}), bf16[32,8,128]{2,1,0:T(8,128)(2,1)S(1)}, u32[]{:S(2)}, u32[]{:S(2)}) async-start(bf16[32,8,128]{2,1,0:T(8,128)(2,1)} %reshape.2379), calls=%async_computation | async-start | bytes 131072 | tf_op jit(solution)/shard_map/all_to_all | solution.py:143
  37.0 7.3 %all-to-all-done = bf16[32,8,128]{2,1,0:T(8,128)(2,1)S(1)} async-done(((bf16[32,8,128]{2,1,0:T(8,128)(2,1)}), bf16[32,8,128]{2,1,0:T(8,128)(2,1)S(1)}, u32[]{:S(2)}, u32[]{:S(2)}) %all-to-all-start) | async-done | bytes 65568 | tf_op jit(solution)/shard_map/all_to_all | solution.py:143
  44.3 0.1 reshape.2380
  44.4 0.2 fusion.53
  44.6 0.6 %convolution_convert_fusion.1 = bf16[64,64,4]{1,2,0:T(4,128)(2,1)S(1)} fusion(bf16[64,32,64]{2,1,0:T(8,128)(2,1)S(1)} %get-tuple-element.865, bf16[64,32,64]{2,1,0:T(8,128)(2,1)S(1)} %get-tuple-element.864, bf16[64,64,4]{1,0,2:T(8,128)(2,1)S(1)} %bitcast.702), kind=kOutput, calls=%fused_computation.259 | convolution fusion | flops 3162112 | bytes 589824 | tf_op jit(solution)/shard_map/lcx,loc->lox/dot_general | solution.py:156
  45.3 0.1 copy.91
  45.4 0.3 fusion.47
  45.7 0.2 copy.94
  45.9 0.8 %reshape.2383 = bf16[32,8,128]{2,1,0:T(8,128)(2,1)} reshape(bf16[16,2,8,2,2,32]{5,4,3,2,1,0:T(2,128)(2,1)S(1)} %copy.94) | data formatting | bytes 131072 | tf_op jit(solution)/shard_map/reshape | solution.py:164
  46.7 2.6 %all-to-all-start.1 = ((bf16[32,8,128]{2,1,0:T(8,128)(2,1)}), bf16[32,8,128]{2,1,0:T(8,128)(2,1)S(1)}, u32[]{:S(2)}, u32[]{:S(2)}) async-start(bf16[32,8,128]{2,1,0:T(8,128)(2,1)} %reshape.2383), calls=%async_computation.1 | async-start | bytes 131072 | tf_op jit(solution)/shard_map/all_to_all | solution.py:166
  49.3 0.3 multiply_convert_fusion.1
  49.7 7.1 %all-to-all-done.1 = bf16[32,8,128]{2,1,0:T(8,128)(2,1)S(1)} async-done(((bf16[32,8,128]{2,1,0:T(8,128)(2,1)}), bf16[32,8,128]{2,1,0:T(8,128)(2,1)S(1)}, u32[]{:S(2)}, u32[]{:S(2)}) %all-to-all-start.1) | async-done | bytes 65568 | tf_op jit(solution)/shard_map/all_to_all | solution.py:166
  56.7 0.2 reshape.2384
  56.9 0.2 fusion.52
  57.1 0.7 %copy.96 = bf16[32,8,256]{2,1,0:T(8,128)(2,1)} copy(bf16[32,8,256]{2,0,1:T(8,128)(2,1)S(1)} %fusion.52) | data formatting | bytes 262144 | tf_op jit(solution)/shard_map/convert_element_type | solution.py:171
  (202 shorter events, 8.2 us)
Async XLA Ops:
  0.0 17.2 %copy-start = (bf16[64,64,3,3]{1,0,3,2:T(8,128)(2,1)S(1)}, bf16[64,64,3,3]{1,0,3,2:T(8,128)(2,1)}, u32[]{:S(2)}) copy-start(bf16[64,64,3,3]{1,0,3,2:T(8,128)(2,1)} %param.7) | copy-start | bytes 221188
  1.2 13.8 %collective-permute-start.1 = (bf16[64,8,128]{0,1,2:T(8,128)(2,1)S(1)}, bf16[64,8,128]{0,1,2:T(8,128)(2,1)S(1)}, u32[]{:S(2)}, u32[]{:S(2)}) collective-permute-start(bf16[64,8,128]{0,1,2:T(8,128)(2,1)S(1)} %copy.78), channel_id=1, source_target_pairs={{0,1},{1,0},{2,3},{3,2},{4,5},{5,4},{6,7},{7,6},{8,9},{9,8},{10,11... | collective-permute-start | bytes 393224 | tf_op jit(solution)/shard_map/ppermute | solution.py:113
  1.7 35.2 %collective-permute-start = (bf16[64,32,64]{2,1,0:T(8,128)(2,1)}, bf16[64,32,64]{2,1,0:T(8,128)(2,1)S(1)}, u32[]{:S(2)}, u32[]{:S(2)}) collective-permute-start(bf16[64,32,64]{2,1,0:T(8,128)(2,1)} %param.9), channel_id=1, source_target_pairs={{0,1},{1,0},{2,3},{3,2},{4,5},{5,4},{6,7},{7,6},{8,9},{9,8},{10,11... | collective-permute-start | bytes 786440 | tf_op jit(solution)/shard_map/ppermute | solution.py:114
  15.4 0.8 %collective-permute-start.2 = (bf16[64,2,256]{0,1,2:T(2,128)(2,1)S(1)}, bf16[64,2,256]{0,1,2:T(2,128)(2,1)S(1)}, u32[]{:S(2)}, u32[]{:S(2)}) collective-permute-start(bf16[64,2,256]{0,1,2:T(2,128)(2,1)S(1)} %broadcast_select_fusion.6), channel_id=1, source_target_pairs={{1,2},{2,1},{3,4},{4,3},{5,6},{6,5},{7,8},{8,7},{9,10},{10,9},{11,... | collective-permute-start | bytes 196616 | tf_op jit(solution)/shard_map/ppermute | solution.py:124
  17.1 0.7 %copy-start.3 = (pred[8,33]{0,1:T(8,128)(4,1)S(1)}, pred[8,33]{0,1:T(8,128)(4,1)}, u32[]{:S(2)}) copy-start(pred[8,33]{0,1:T(8,128)(4,1)} %constant.458) | copy-start | bytes 796
  19.7 0.9 %copy-start.2 = (bf16[64,64,3,3]{1,0,3,2:T(8,128)(2,1)S(1)}, bf16[64,64,3,3]{1,0,3,2:T(8,128)(2,1)}, u32[]{:S(2)}) copy-start(bf16[64,64,3,3]{1,0,3,2:T(8,128)(2,1)} %param.8) | copy-start | bytes 221188
  21.8 15.1 %copy-start.1 = (bf16[64,32,64]{2,1,0:T(8,128)(2,1)S(1)}, bf16[64,32,64]{2,1,0:T(8,128)(2,1)}, u32[]{:S(2)}) copy-start(bf16[64,32,64]{2,1,0:T(8,128)(2,1)} %param.9) | copy-start | bytes 786436
  22.9 21.4 %all-to-all-start = ((bf16[32,8,128]{2,1,0:T(8,128)(2,1)}), bf16[32,8,128]{2,1,0:T(8,128)(2,1)S(1)}, u32[]{:S(2)}, u32[]{:S(2)}) async-start(bf16[32,8,128]{2,1,0:T(8,128)(2,1)} %reshape.2379), calls=%async_computation | async-start | bytes 131072 | tf_op jit(solution)/shard_map/all_to_all | solution.py:143
  46.7 10.0 %all-to-all-start.1 = ((bf16[32,8,128]{2,1,0:T(8,128)(2,1)}), bf16[32,8,128]{2,1,0:T(8,128)(2,1)S(1)}, u32[]{:S(2)}, u32[]{:S(2)}) async-start(bf16[32,8,128]{2,1,0:T(8,128)(2,1)} %reshape.2383), calls=%async_computation.1 | async-start | bytes 131072 | tf_op jit(solution)/shard_map/all_to_all | solution.py:166

commit v2 on v1

v2 whole, which is shorter than its diff:
```python
import functools
import math

import jax
import jax.numpy as jnp
from jax import lax
from jax.experimental import pallas as pl
from jax.experimental.pallas import tpu as pltpu
from jax.sharding import PartitionSpec as P

VMEM = pl.BlockSpec(memory_space=pltpu.VMEM)
SMEM = pl.BlockSpec(memory_space=pltpu.SMEM)
LIMIT = 48 * 1024 * 1024


def call(kernel, out_shape, scratch, in_specs, cost):
    return pl.pallas_call(
        kernel,
        out_shape=out_shape,
        in_specs=in_specs,
        out_specs=jax.tree.map(lambda _: VMEM, out_shape),
        scratch_shapes=scratch,
        compiler_params=pltpu.CompilerParams(vmem_limit_bytes=LIMIT),
        cost_estimate=cost,
    )


def wave_angles(lon_total, waves):
    points = jnp.arange(lon_total, dtype=jnp.int32)[None, :]
    return (points * waves[:, None] % lon_total).astype(jnp.float32) * (2.0 * math.pi / lon_total)


def forward_table(lon_total, orders):
    angle = wave_angles(lon_total, jnp.arange(orders, dtype=jnp.int32))
    return jnp.concatenate([jnp.cos(angle), -jnp.sin(angle)], axis=0).astype(jnp.bfloat16)


def inverse_table(lon_total, owners, per_device, groups):
    orders = owners * per_device
    waves = jnp.arange(orders, dtype=jnp.int32)
    angle = wave_angles(lon_total, waves)
    factor = jnp.where(waves == 0, 1.0, 2.0).astype(jnp.float32)[:, None]
    table = jnp.stack([factor * jnp.cos(angle), -factor * jnp.sin(angle)], axis=1)
    table = table.astype(jnp.bfloat16).reshape(owners, 1, 2 * per_device, 1, lon_total)
    same = jnp.eye(groups, dtype=jnp.bfloat16)[None, :, None, :, None]
    return (table * same).reshape(2 * orders * groups, groups * lon_total)


def quadrature(lat_rows, lat_total, lon_total):
    colatitude = (lat_rows.astype(jnp.float32) + 0.5) * (math.pi / lat_total)
    return jnp.sin(colatitude) * (math.pi / lat_total / lon_total)


def legendre_kernel(span, lanes_ref, analysis_ref, synthesis_ref, first_ref, second_ref):
    degrees = first_ref.shape[0]
    cosine, log_start, orders = lanes_ref[0], lanes_ref[1], lanes_ref[2]
    even_sign, odd_sign = lanes_ref[3], lanes_ref[4]
    orders_squared = orders * orders

    def advance(block, carry):
        current, previous, log_scale = carry
        for offset in range(span):
            degree_id = block * span + offset
            degree = jnp.float32(1.0) * degree_id
            earlier = degree - 1.0
            coef_a = jnp.sqrt(
                jnp.maximum(4.0 * degree * degree - 1.0, 1.0)
                / jnp.maximum(degree * degree - orders_squared, 1.0)
            )
            coef_b = jnp.sqrt(
                jnp.maximum(earlier * earlier - orders_squared, 0.0)
                / jnp.maximum(4.0 * earlier * earlier - 1.0, 1.0)
            )
            newest = coef_a * (cosine * current - coef_b * previous)
            is_start = degree == orders
            before = degree < orders
            newest = jnp.where(before, 0.0, jnp.where(is_start, 1.0, newest))
            log_scale = jnp.where(is_start, log_start, log_scale)
            previous = jnp.where(is_start | before, 0.0, current)
            current = newest
            sign = even_sign if offset % 2 == 0 else odd_sign
            emitted = newest * jnp.exp(log_scale) * sign
            first_ref[pl.ds(degree_id, 1), :] = emitted[0:1]
            second_ref[pl.ds(degree_id, 1), :] = emitted[1:2]
        size_now = jnp.maximum(jnp.abs(current), jnp.abs(previous))
        safe_size = jnp.where(size_now > 0.0, size_now, 1.0)
        return current / safe_size, previous / safe_size, log_scale + jnp.log(safe_size)

    zeros = jnp.zeros_like(cosine)
    lax.fori_loop(0, degrees // span, advance, (zeros, zeros, zeros))
    per_device = analysis_ref.shape[0] // degrees
    rows = synthesis_ref.shape[0]
    own_order = lanes_ref[5][0:1]
    values = first_ref[...]
    for m in range(per_device):
        analysis_ref[m * degrees : (m + 1) * degrees, :] = jnp.where(
            own_order == m, values, 0.0
        ).astype(jnp.bfloat16)
    stacked = jnp.concatenate(
        [second_ref[:, m * rows : (m + 1) * rows] for m in range(per_device)], axis=0
    )
    synthesis_ref[...] = stacked.T.astype(jnp.bfloat16)


def legendre_tables(first_order, per_device, degrees, lat_total, row_count, half):
    bands = lat_total // row_count
    lane = jnp.arange(lat_total * per_device, dtype=jnp.int32)
    own_first = lane // half % per_device
    row_first = lane // (half * per_device) * half + lane % half
    own_second = lane // lat_total
    row_second = lane % bands * row_count + lane // bands % row_count
    own = jnp.stack([own_first, own_second])
    row = jnp.stack([row_first, row_second])
    south = row >= lat_total // 2
    row = jnp.where(south, lat_total - 1 - row, row)
    colatitude = (row.astype(jnp.float32) + 0.5) * (math.pi / lat_total)
    order_ids = first_order + own
    orders = order_ids.astype(jnp.float32)
    counter = jnp.arange(1, degrees + 1, dtype=jnp.int32).astype(jnp.float32)
    log_terms = jnp.log((2.0 * counter - 1.0) / (2.0 * counter))
    own_orders = (first_order + jnp.arange(per_device, dtype=jnp.int32)).astype(jnp.float32)
    starts = 0.5 * jnp.log(own_orders + 0.5) + 0.5 * jnp.sum(
        jnp.where(counter[None, :] <= own_orders[:, None], log_terms[None, :], 0.0), axis=1
    )
    log_start = starts[0]
    for m in range(1, per_device):
        log_start = jnp.where(own == m, starts[m], log_start)
    log_start = log_start + orders * jnp.log(jnp.sin(colatitude))
    parity = (1 - 2 * (order_ids % 2)).astype(jnp.float32)
    lanes = jnp.stack(
        [
            jnp.cos(colatitude),
            log_start,
            orders,
            jnp.where(south, parity, 1.0),
            jnp.where(south, -parity, 1.0),
            own.astype(jnp.float32),
        ]
    )
    width = lane.shape[0]
    span = 32 if degrees % 32 == 0 else degrees
    return call(
        functools.partial(legendre_kernel, span),
        (
            jax.ShapeDtypeStruct((per_device * degrees, width), jnp.bfloat16),
            jax.ShapeDtypeStruct((lat_total, per_device * degrees), jnp.bfloat16),
        ),
        [pltpu.VMEM((degrees, width), jnp.float32), pltpu.VMEM((degrees, width), jnp.float32)],
        [VMEM],
        pl.CostEstimate(flops=40 * degrees * width, bytes_accessed=1 << 20, transcendentals=0),
    )(lanes)


def convolve_kernel(
    lat_total, row_ref, quad_ref, rows_ref, first_ref, second_ref, dft_ref, out_ref, mid_ref, hidden_ref, coeffs_ref
):
    channels, lon_total = rows_ref.shape[1:]
    half = hidden_ref.shape[0]

    def layer(source_ref, weights, row):
        taps = source_ref[row : row + 3].reshape(3 * channels, lon_total)
        sums = jnp.dot(weights, taps, preferred_element_type=jnp.float32)
        total = (
            sums[channels : 2 * channels]
            + pltpu.roll(sums[:channels], 1, 1)
            + pltpu.roll(sums[2 * channels :], lon_total - 1, 1)
        )
        return jnp.maximum(total, 0.0)

    weights = first_ref[...]
    for row in range(half + 2):
        values = layer(rows_ref, weights, row)
        if row == 0 or row == half + 1:
            place = row_ref[0] - 1 + row
            values = jnp.where((place >= 0) & (place < lat_total), values, 0.0)
        mid_ref[row] = values.astype(jnp.bfloat16)
    weights = second_ref[...]
    for row in range(half):
        hidden_ref[row] = layer(mid_ref, weights, row).astype(jnp.bfloat16)
    hidden = hidden_ref[...].reshape(half * channels, lon_total)
    spectra = lax.dot_general(
        dft_ref[...], hidden, (((1,), (1,)), ((), ())), preferred_element_type=jnp.float32
    )
    orders = spectra.shape[0] // 2
    for row in range(half):
        columns = slice(row * channels, (row + 1) * channels)
        both = jnp.concatenate([spectra[:orders, columns], spectra[orders:, columns]], axis=1)
        coeffs_ref[pl.ds(row, orders, stride=half), :] = both * quad_ref[row]
    out_ref[...] = coeffs_ref[...].astype(jnp.bfloat16).reshape(out_ref.shape)


def spectral_kernel(
    per_device, pieces_ref, analysis_ref, synthesis_ref, mixing_ref, out_ref, spectral_ref, chunk_ref
):
    owners, chunk_rows, width = pieces_ref.shape
    channels, _, columns = mixing_ref.shape
    degrees = columns // per_device
    parts = 2 * per_device
    kept = channels // 2
    groups = chunk_rows // parts
    packed = width // kept
    bands = synthesis_ref.shape[0] // (groups * packed)

    pieces = pieces_ref[...].reshape(owners * chunk_rows, width)
    spectral = jnp.dot(analysis_ref[...], pieces, preferred_element_type=jnp.float32)
    spectral_ref[...] = spectral.T.astype(jnp.bfloat16).astype(jnp.float32)

    def add_channel(channel, totals):
        weights = mixing_ref[channel].astype(jnp.float32)
        return tuple(
            total + weights * spectral_ref[pl.ds(part * channels + channel, 1), :]
            for part, total in enumerate(totals)
        )

    zeros = jnp.zeros((channels, columns), jnp.float32)
    mixed = lax.fori_loop(0, channels, add_channel, (zeros, zeros), unroll=8)
    lane = lax.broadcasted_iota(jnp.int32, (kept, columns), 1)
    blocks = []
    for side in range(2):
        for m in range(per_device):
            own = (lane >= m * degrees) & (lane < (m + 1) * degrees)
            for part in range(2):
                block = mixed[part][side * kept : (side + 1) * kept]
                blocks.append(jnp.where(own, block, 0.0).astype(jnp.bfloat16))
    values = lax.dot_general(
        synthesis_ref[...],
        jnp.concatenate(blocks, axis=0),
        (((1,), (1,)), ((), ())),
        preferred_element_type=jnp.float32,
    )
    for side in range(2):
        for group in range(groups):
            for part in range(parts):
                start = (side * parts + part) * kept
                pieces = [
                    values[(group * packed + i) * bands : (group * packed + i + 1) * bands, start : start + kept]
                    for i in range(packed)
                ]
                place = (side * groups + group) * parts + part
                chunk_ref[pl.ds(place, bands, stride=2 * groups * parts), :] = jnp.concatenate(
                    pieces, axis=1
                )
    out_ref[...] = chunk_ref[...].astype(jnp.bfloat16).reshape(out_ref.shape)


def inverse_kernel(pieces_ref, inverse_ref, out_ref, rows_ref):
    owners, chunk_rows, width = pieces_ref.shape
    kept, row_count, lon_total = out_ref.shape
    packed = width // kept
    pieces = pieces_ref[...].reshape(owners * chunk_rows, width)
    values = lax.dot_general(
        pieces, inverse_ref[...], (((0,), (0,)), ((), ())), preferred_element_type=jnp.float32
    )
    for row in range(row_count):
        group, place = row // packed, row % packed
        block = values[place * kept : (place + 1) * kept, group * lon_total : (group + 1) * lon_total]
        for tile in range(lon_total // 128):
            rows_ref[tile, pl.ds(row, kept, stride=row_count), :] = block[:, tile * 128 : (tile + 1) * 128]
    for tile in range(lon_total // 128):
        out_ref[:, :, tile * 128 : (tile + 1) * 128] = (
            rows_ref[tile].astype(jnp.bfloat16).reshape(kept, row_count, 128)
        )


def local(fields, conv_first, conv_second, mixing):
    lat_count = lax.axis_size("lat")
    lon_count = lax.axis_size("lon")
    channels, row_count, lon_part = fields.shape
    lat_total = row_count * lat_count
    lon_total = lon_part * lon_count
    orders = lat_total // 2
    degrees = mixing.shape[0]
    owners = lat_count * lon_count
    per_device = orders // owners
    half = row_count // 2
    kept = channels // 2
    lat_index = lax.axis_index("lat")
    side = lax.axis_index("lon")
    swap = [(0, 1), (1, 0)]
    both = ("lat", "lon")
    upper = side == 0

    other = lax.ppermute(fields, "lon", swap)
    other_mixing = lax.ppermute(mixing, "lon", swap)
    mine, theirs = jnp.transpose(fields, (1, 0, 2)), jnp.transpose(other, (1, 0, 2))
    full = jnp.concatenate(
        [jnp.where(upper, mine, theirs), jnp.where(upper, theirs, mine)], axis=2
    )
    message = jnp.where(upper, full[:2], full[row_count - 2 :])
    pairs = []
    for i in range(lat_count - 1):
        pairs.append((2 * i + 1, 2 * (i + 1)))
        pairs.append((2 * (i + 1), 2 * i + 1))
    halo = lax.ppermute(message, both, pairs)
    rows = jnp.where(
        upper,
        jnp.concatenate([halo, full[: half + 2]], axis=0),
        jnp.concatenate([full[half - 2 :], halo], axis=0),
    )

    first_row = lat_index * row_count + side * half
    weights = [
        jnp.transpose(kernel, (3, 0, 2, 1)).reshape(3 * channels, 3 * channels)
        for kernel in (conv_first, conv_second)
    ]
    row_ids = first_row + jnp.arange(half, dtype=jnp.int32)
    coeffs = call(
        functools.partial(convolve_kernel, lat_total),
        jax.ShapeDtypeStruct((owners, per_device * half, 2 * channels), jnp.bfloat16),
        [
            pltpu.VMEM((half + 2, channels, lon_total), jnp.bfloat16),
            pltpu.VMEM((half, channels, lon_total), jnp.bfloat16),
            pltpu.VMEM((orders * half, 2 * channels), jnp.float32),
        ],
        [SMEM, SMEM, VMEM, VMEM, VMEM, VMEM],
        pl.CostEstimate(flops=1 << 28, bytes_accessed=1 << 20, transcendentals=0),
    )(
        first_row[None],
        quadrature(row_ids, lat_total, lon_total),
        rows,
        weights[0],
        weights[1],
        forward_table(lon_total, orders),
    )
    pieces = lax.all_to_all(coeffs, both, split_axis=0, concat_axis=0, tiled=True)

    first_order = (2 * lat_index + side) * per_device
    analysis, synthesis = legendre_tables(
        first_order, per_device, degrees, lat_total, row_count, half
    )
    mixing = jnp.concatenate(
        [jnp.where(upper, mixing, other_mixing), jnp.where(upper, other_mixing, mixing)], axis=1
    )
    mixing = jnp.concatenate([jnp.transpose(mixing, (2, 1, 0))] * per_device, axis=2)
    width = 128
    chunk_rows = row_count * 2 * per_device * kept // width
    chunks = call(
        functools.partial(spectral_kernel, per_device),
        jax.ShapeDtypeStruct((owners, chunk_rows, width), jnp.bfloat16),
        [
            pltpu.VMEM((2 * channels, per_device * degrees), jnp.float32),
            pltpu.VMEM((owners * chunk_rows, width), jnp.float32),
        ],
        [VMEM] * 4,
        pl.CostEstimate(flops=1 << 24, bytes_accessed=1 << 20, transcendentals=0),
    )(pieces, analysis, synthesis, mixing)

    back = lax.all_to_all(chunks, both, split_axis=0, concat_axis=0, tiled=True)
    groups = chunk_rows // (2 * per_device)
    return call(
        inverse_kernel,
        jax.ShapeDtypeStruct((kept, row_count, lon_total), jnp.bfloat16),
        [pltpu.VMEM((lon_total // 128, kept * row_count, 128), jnp.float32)],
        [VMEM] * 2,
        pl.CostEstimate(flops=1 << 24, bytes_accessed=1 << 19, transcendentals=0),
    )(back, inverse_table(lon_total, owners, per_device, groups))


def solution(mesh):
    in_specs = (P("groups", "lat", "lon"), P(), P(), P(None, "lon", None))
    out_specs = P(("groups", "lon"), "lat", None)
    return jax.shard_map(local, mesh=mesh, in_specs=in_specs, out_specs=out_specs, check_vma=False)
```

time: 58.2 us -> 43.9 us (0.75)
  other arithmetic: 10.5 us -> 3.74 us
  Pallas kernels: 0 us -> 5.06 us
  local copies, waits for them, and re-layouts: 8.36 us -> 4.43 us
  matrix products: 3.46 us -> 0 us
  loops' own time: 2.99 us -> 0 us
  starting transfers between devices: 17.8 us -> 16.6 us
  waiting for transfers between devices: 14.4 us -> 13.5 us
    while x62 -> x0, other arithmetic: 5.59 us -> none
    pallas_call x0 -> x4, Pallas kernels: none -> 5.06 us  [the longest x1 2.09 us: local(): call(functools.partial(convolve_kernel, lat_total), jax.ShapeDtypeStruct(...]
    another operation x1 -> x0, loops' own time: 2.99 us -> none  [legendre_table(): unused, stacked = lax.scan(advance, (zeros, zeros, zeros), blocks)]
    conv_general_dilated x2 -> x0, matrix products: 1.89 us -> none  [convolve(): lax.conv_general_dilated(padded[None], kernel, (1, 1), 'VALID', dimension...]
    dot_general x5 -> x0, matrix products: 1.58 us -> none  [the longest x1 0.65 us: local(): jnp.einsum('lcx,loc->lox', spectral, mixing, preferred_element_type=jnp.f...]
    convert_element_type x7 -> x1, local copies, waits for them, and re-layouts: 1.56 us -> 0.05 us  [inverse_table(): table.astype(jnp.bfloat16).reshape(owners, 1, 2 * per_device, 1, lon_total)]
    reshape x4 -> x2, local copies, waits for them, and re-layouts: 1.8 us -> 0.33 us  [local(): jnp.transpose(kernel, (3, 0, 2, 1)).reshape(3 * channels, 3 * channels)]
    unnamed x3 -> x5, other arithmetic: 0.01 us -> 1.47 us
  transfers between devices with their start and end apart: 5 -> 5, of which waited for: 2 -> 2; matrix products, arithmetic and copies ran while one was open for 28% -> 17% of each run, Pallas kernels for 0% -> 6%
where the time goes in v2:
time: 43.9 us; the launch traced here: 43.6 us
  starting transfers between devices  16.6 us (38%)
  waiting for transfers between devices  13.5 us (31%)
  Pallas kernels  5.06 us (12%)
  local copies, waits for them, and re-layouts  4.43 us (10%)
  other arithmetic  3.74 us (9%)
    all_to_all x1, starting transfers between devices, local(): lax.all_to_all(coeffs, both, split_axis=0, concat_axis=0, tiled=True)  12.7 us
    all_to_all x1, waiting for transfers between devices, local(): back = lax.all_to_all(chunks, both, split_axis=0, concat_axis=0, tiled=True)  7.09 us
    all_to_all x1, waiting for transfers between devices, local(): lax.all_to_all(coeffs, both, split_axis=0, concat_axis=0, tiled=True)  6.43 us
    unnamed x9, local copies, waits for them, and re-layouts  3.14 us
    all_to_all x1, starting transfers between devices, local(): back = lax.all_to_all(chunks, both, split_axis=0, concat_axis=0, tiled=True)  2.57 us
    pallas_call x1, Pallas kernels, local(): call(functools.partial(convolve_kernel, lat_total), jax.ShapeDtypeStruct(...  2.09 us
    pallas_call x1, Pallas kernels, local(): call(functools.partial(spectral_kernel, per_device), jax.ShapeDtypeStruct...  1.57 us
    unnamed x5, other arithmetic  1.47 us
  transfers between devices with their start and end apart: 5, of which 2 were waited for; matrix products, arithmetic and copies ran while one was open for 17% of the time, Pallas kernels for 6%

profile of v2, /device:TPU:0, one launch (start us, length us, event | category | flops | bytes accessed | tf_op | source)
XLA Modules:
  0.0 43.6 jit_solution(8844407292315623769)
XLA Ops:
  0.0 0.0 copy-start.1
  0.0 1.0 %copy.38 = bf16[64,8,128]{2,0,1:T(8,128)(2,1)S(1)} copy(bf16[64,8,128]{2,1,0:T(8,128)(2,1)} %param.4) | data formatting | bytes 262144 | tf_op args[0]
  1.0 0.0 copy-start.2
  1.0 0.5 %collective-permute-start = (bf16[64,8,128]{2,0,1:T(8,128)(2,1)S(1)}, bf16[64,8,128]{2,0,1:T(8,128)(2,1)S(1)}, u32[]{:S(2)}, u32[]{:S(2)}) collective-permute-start(bf16[64,8,128]{2,0,1:T(8,128)(2,1)S(1)} %copy.38), channel_id=1, source_target_pairs={{0,1},{1,0},{2,3},{3,2},{4,5},{5,4},{6,7},{7,6},{8,9},{9,8},{10,11... | collective-permute-start | bytes 393224 | tf_op jit(solution)/shard_map/ppermute | solution.py:283
  1.5 2.1 %copy.43 = bf16[64,32,64]{0,1,2:T(8,128)(2,1)S(1)} copy(bf16[64,32,64]{2,1,0:T(8,128)(2,1)} %param.7) | data formatting | bytes 524288 | tf_op args[3]
  3.6 0.0 copy-start
  3.6 0.1 collective-permute-start.2
  3.8 0.3 negate_convert_fusion
  4.2 0.2 fusion.31
  4.4 0.6 %fusion.40 = (f32[1]{0:T(128)}, f32[1]{0:T(128)}) fusion(f32[2]{0:T(128)S(1)} %add_multiply_fusion), kind=kLoop, calls=%fused_computation.108 | loop fusion | bytes 16 | tf_op jit(solution)/shard_map/slice | solution.py:127
  5.0 0.1 constant_dynamic-update-slice_fusion.5
  5.0 1.3 %constant_dynamic-update-slice_fusion.4 = f32[6,2,256]{2,1,0:T(2,128)S(1)} fusion(f32[6,2,256]{2,1,0:T(2,128)S(1)} %constant_dynamic-update-slice_fusion.5, s32[]{:T(128)S(6)} %mul.251, f32[]{:T(128)} %bitcast.10, f32[]{:T(128)} %bitcast.9, s32[1,1,256]{2,1,0:T(1,128)S(1)} %get-tuple-element.17, s32[1,1,256]{2,1,0:T(1,128)S(1)} %get-tuple-element.18, ...), kind=kLoop, calls=%fused_computation.48 | loop fusion | flops 7168 | bytes 6156
  6.5 0.3 multiply_convert_fusion
  6.8 0.0 copy-done.1
  6.8 0.1 copy.40
  7.0 0.2 reshape.633.first_ref
  7.1 0.0 copy-done.2
  7.1 0.1 copy.41
  7.3 0.2 reshape.634.second_ref
  7.4 0.1 copy.45
  7.5 0.5 %shard_map.47 = (bf16[128,256]{1,0:T(8,128)(2,1)S(1)}, bf16[128,128]{1,0:T(8,128)(2,1)S(1)}) custom-call(f32[6,2,256]{2,1,0:T(2,128)S(1)} %constant_dynamic-update-slice_fusion.lanes_ref), custom_call_target="tpu_custom_call" | custom-call | flops 655360 | bytes 1048576 | tf_op jit(solution)/shard_map/pallas_call | solution.py:142
  8.1 0.0 collective-permute-done
  8.1 0.0 copy-done
  8.2 0.7 %collective-permute-start.1 = (bf16[2,64,256]{2,1,0:T(8,128)(2,1)S(1)}, bf16[2,64,256]{2,1,0:T(8,128)(2,1)S(1)}, u32[]{:S(2)}, u32[]{:S(2)}) collective-permute-start(bf16[2,64,256]{2,1,0:T(8,128)(2,1)S(1)} %fusion.10), channel_id=1, source_target_pairs={{1,2},{2,1},{3,4},{4,3},{5,6},{6,5},{7,8},{8,7},{9,10},{10,9},{11,... | collective-permute-start | bytes 196616 | tf_op jit(solution)/shard_map/ppermute | solution.py:294
  8.9 0.0 collective-permute-done.1
  8.9 0.1 fusion.1.rows_ref
  8.9 2.1 %shard_map.46 = bf16[32,8,128]{2,1,0:T(8,128)(2,1)} custom-call(s32[1]{0:T(128)} %bitcast.row_ref, f32[4]{0:T(128)S(1)} %sine_multiply_fusion.quad_ref, bf16[8,64,256]{2,1,0:T(8,128)(2,1)S(1)} %fusion.1.rows_ref, bf16[192,192]{1,0:T(8,128)(2,1)S(1)} %reshape.633.first_ref, bf16[192,192]{1,0:T(8,128)(2,1)S(1)} %reshape.634.second_ref, ...), custom_call_target="tpu_custom_call" | custom-call | flops 268435456 | bytes 1048576 | tf_op jit(solution)/shard_map/pallas_call | solution.py:307
  11.0 12.7 %all-to-all-start = ((bf16[32,8,128]{2,1,0:T(8,128)(2,1)}), bf16[32,8,128]{2,1,0:T(8,128)(2,1)S(1)}, u32[]{:S(2)}, u32[]{:S(2)}) async-start(bf16[32,8,128]{2,1,0:T(8,128)(2,1)} %shard_map.46), calls=%async_computation | async-start | bytes 131072 | tf_op jit(solution)/shard_map/all_to_all | solution.py:325
  23.8 0.0 collective-permute-done.2
  23.8 0.1 broadcast_select_fusion.1
  23.9 0.3 maximum_bitcast_fusion
  24.2 0.6 %pad_maximum_fusion.mixing_ref = bf16[64,64,128]{2,1,0:T(8,128)(2,1)S(1)} fusion(bf16[64,64,64]{2,1,0:T(8,128)(2,1)S(1)} %maximum_bitcast_fusion), kind=kLoop, calls=%fused_computation.1 | loop fusion | flops 2097152 | bytes 1572864 | tf_op jit(solution)/shard_map/concatenate | solution.py:334
  24.7 6.4 %all-to-all-done.pieces_ref = bf16[32,8,128]{2,1,0:T(8,128)(2,1)S(1)} async-done(((bf16[32,8,128]{2,1,0:T(8,128)(2,1)}), bf16[32,8,128]{2,1,0:T(8,128)(2,1)S(1)}, u32[]{:S(2)}, u32[]{:S(2)}) %all-to-all-start) | async-done | bytes 65568 | tf_op jit(solution)/shard_map/all_to_all | solution.py:325
  31.2 1.6 %shard_map.48 = bf16[32,8,128]{2,1,0:T(8,128)(2,1)} custom-call(bf16[32,8,128]{2,1,0:T(8,128)(2,1)S(1)} %all-to-all-done.pieces_ref, bf16[128,256]{1,0:T(8,128)(2,1)S(1)} %get-tuple-element.7.analysis_ref, bf16[128,128]{1,0:T(8,128)(2,1)S(1)} %get-tuple-element.8.synthesis_ref, bf16[64,64,128]{2,1,0:T(8,128)(2,1)S(1)} %pad_maximum_fusion.mixing_ref), custom_call_target="tpu_custom_call" | custom-call | flops 16777216 | bytes 1048576 | tf_op jit(solution)/shard_map/pallas_call | solution.py:337
  32.7 2.6 %all-to-all-start.1 = ((bf16[32,8,128]{2,1,0:T(8,128)(2,1)}), bf16[32,8,128]{2,1,0:T(8,128)(2,1)S(1)}, u32[]{:S(2)}, u32[]{:S(2)}) async-start(bf16[32,8,128]{2,1,0:T(8,128)(2,1)} %shard_map.48), calls=%async_computation.1 | async-start | bytes 131072 | tf_op jit(solution)/shard_map/all_to_all | solution.py:348
  35.3 0.3 broadcast_multiply_fusion
  35.6 7.1 %all-to-all-done.1.pieces_ref = bf16[32,8,128]{2,1,0:T(8,128)(2,1)S(1)} async-done(((bf16[32,8,128]{2,1,0:T(8,128)(2,1)}), bf16[32,8,128]{2,1,0:T(8,128)(2,1)S(1)}, u32[]{:S(2)}, u32[]{:S(2)}) %all-to-all-start.1) | async-done | bytes 65568 | tf_op jit(solution)/shard_map/all_to_all | solution.py:348
  42.7 0.9 %shard_map.49 = bf16[32,8,256]{2,1,0:T(8,128)(2,1)} custom-call(bf16[32,8,128]{2,1,0:T(8,128)(2,1)S(1)} %all-to-all-done.1.pieces_ref, bf16[256,512]{1,0:T(8,128)(2,1)S(1)} %bitcast.22), custom_call_target="tpu_custom_call" | custom-call | flops 16777216 | bytes 524288 | tf_op jit(solution)/shard_map/pallas_call | solution.py:350
  (21 shorter events, 0.4 us)
Async XLA Ops:
  0.0 6.8 %copy-start.1 = (bf16[64,64,3,3]{1,0,3,2:T(8,128)(2,1)S(1)}, bf16[64,64,3,3]{1,0,3,2:T(8,128)(2,1)}, u32[]{:S(2)}) copy-start(bf16[64,64,3,3]{1,0,3,2:T(8,128)(2,1)} %param.5) | copy-start | bytes 221188
  1.0 6.2 %copy-start.2 = (bf16[64,64,3,3]{1,0,3,2:T(8,128)(2,1)S(1)}, bf16[64,64,3,3]{1,0,3,2:T(8,128)(2,1)}, u32[]{:S(2)}) copy-start(bf16[64,64,3,3]{1,0,3,2:T(8,128)(2,1)} %param.6) | copy-start | bytes 221188
  1.0 7.1 %collective-permute-start = (bf16[64,8,128]{2,0,1:T(8,128)(2,1)S(1)}, bf16[64,8,128]{2,0,1:T(8,128)(2,1)S(1)}, u32[]{:S(2)}, u32[]{:S(2)}) collective-permute-start(bf16[64,8,128]{2,0,1:T(8,128)(2,1)S(1)} %copy.38), channel_id=1, source_target_pairs={{0,1},{1,0},{2,3},{3,2},{4,5},{5,4},{6,7},{7,6},{8,9},{9,8},{10,11... | collective-permute-start | bytes 393224 | tf_op jit(solution)/shard_map/ppermute | solution.py:283
  3.6 4.4 %copy-start = (bf16[64,8,128]{2,1,0:T(8,128)(2,1)S(1)}, bf16[64,8,128]{2,1,0:T(8,128)(2,1)}, u32[]{:S(2)}) copy-start(bf16[64,8,128]{2,1,0:T(8,128)(2,1)} %param.4) | copy-start | bytes 393220
  3.6 20.1 %collective-permute-start.2 = (bf16[64,32,64]{0,1,2:T(8,128)(2,1)S(1)}, bf16[64,32,64]{0,1,2:T(8,128)(2,1)S(1)}, u32[]{:S(2)}, u32[]{:S(2)}) collective-permute-start(bf16[64,32,64]{0,1,2:T(8,128)(2,1)S(1)} %copy.43), channel_id=1, source_target_pairs={{0,1},{1,0},{2,3},{3,2},{4,5},{5,4},{6,7},{7,6},{8,9},{9,8},{10,11... | collective-permute-start | bytes 786440 | tf_op jit(solution)/shard_map/ppermute | solution.py:284
  8.2 0.7 %collective-permute-start.1 = (bf16[2,64,256]{2,1,0:T(8,128)(2,1)S(1)}, bf16[2,64,256]{2,1,0:T(8,128)(2,1)S(1)}, u32[]{:S(2)}, u32[]{:S(2)}) collective-permute-start(bf16[2,64,256]{2,1,0:T(8,128)(2,1)S(1)} %fusion.10), channel_id=1, source_target_pairs={{1,2},{2,1},{3,4},{4,3},{5,6},{6,5},{7,8},{8,7},{9,10},{10,9},{11,... | collective-permute-start | bytes 196616 | tf_op jit(solution)/shard_map/ppermute | solution.py:294
  11.0 20.1 %all-to-all-start = ((bf16[32,8,128]{2,1,0:T(8,128)(2,1)}), bf16[32,8,128]{2,1,0:T(8,128)(2,1)S(1)}, u32[]{:S(2)}, u32[]{:S(2)}) async-start(bf16[32,8,128]{2,1,0:T(8,128)(2,1)} %shard_map.46), calls=%async_computation | async-start | bytes 131072 | tf_op jit(solution)/shard_map/all_to_all | solution.py:325
  32.7 10.0 %all-to-all-start.1 = ((bf16[32,8,128]{2,1,0:T(8,128)(2,1)}), bf16[32,8,128]{2,1,0:T(8,128)(2,1)S(1)}, u32[]{:S(2)}, u32[]{:S(2)}) async-start(bf16[32,8,128]{2,1,0:T(8,128)(2,1)} %shard_map.48), calls=%async_computation.1 | async-start | bytes 131072 | tf_op jit(solution)/shard_map/all_to_all | solution.py:348

commit v3 on v2

v3 whole, which is shorter than its diff:
```python
import functools
import math

import jax
import jax.numpy as jnp
from jax import lax
from jax.experimental import pallas as pl
from jax.experimental.pallas import tpu as pltpu
from jax.sharding import PartitionSpec as P

VMEM = pl.BlockSpec(memory_space=pltpu.VMEM)
ANY = pl.BlockSpec(memory_space=pl.ANY)
LIMIT = 40 * 1024 * 1024
LANES = 128


def call(kernel, out_shape, scratch, in_specs, cost):
    return pl.pallas_call(
        kernel,
        out_shape=out_shape,
        in_specs=in_specs,
        out_specs=jax.tree.map(lambda _: VMEM, out_shape),
        scratch_shapes=scratch,
        compiler_params=pltpu.CompilerParams(vmem_limit_bytes=LIMIT),
        cost_estimate=cost,
    )


def unpack_rows(source_ref, rows_ref):
    channels, row_count, lon_part = source_ref.shape
    for tile in range(lon_part // LANES):
        rows_ref[tile] = (
            source_ref[:, :, tile * LANES : (tile + 1) * LANES]
            .astype(jnp.float32)
            .reshape(channels * row_count, LANES)
        )


def packed_row(rows_ref, row, channels):
    tiles, count, _ = rows_ref.shape
    found = [
        rows_ref[tile, pl.ds(row, channels, stride=count // channels), :] for tile in range(tiles)
    ]
    return jnp.concatenate(found, axis=1).astype(jnp.bfloat16)


def rows_kernel(source_ref, out_ref, rows_ref):
    unpack_rows(source_ref, rows_ref)
    for row in range(out_ref.shape[0]):
        out_ref[row] = packed_row(rows_ref, row, out_ref.shape[1])


def place_row(out_ref, place, side, mine, theirs):
    lon_part = mine.shape[1]
    for position, values in ((side, mine), (1 - side, theirs)):
        start = pl.multiple_of(position * lon_part, LANES)
        out_ref[place, :, pl.ds(start, lon_part)] = values


def message_kernel(own_ref, other_ref, out_ref, rows_ref):
    row_count, channels, _ = own_ref.shape
    side = lax.axis_index("lon")
    unpack_rows(other_ref, rows_ref)
    for i in range(2):
        row = side * (row_count - 2) + i
        place_row(out_ref, i, side, own_ref[row], packed_row(rows_ref, row, channels))


def layer(source_ref, weights, row):
    channels, lon_total = source_ref.shape[1:]
    taps = source_ref[row : row + 3].reshape(3 * channels, lon_total)
    sums = jnp.dot(weights, taps, preferred_element_type=jnp.float32)
    total = (
        sums[channels : 2 * channels]
        + pltpu.roll(sums[:channels], 1, 1)
        + pltpu.roll(sums[2 * channels :], lon_total - 1, 1)
    )
    return jnp.maximum(total, 0.0)


def row_weight(row, lat_total, lon_total):
    place = jnp.full((1, LANES), row, jnp.int32).astype(jnp.float32)
    return jnp.sin((place + 0.5) * (math.pi / lat_total)) * (math.pi / lat_total / lon_total)


def row_spectra(dft, hidden, first_row, lat_total):
    count, channels, lon_total = hidden.shape
    spectra = lax.dot_general(
        dft,
        hidden.reshape(count * channels, lon_total),
        (((1,), (1,)), ((), ())),
        preferred_element_type=jnp.float32,
    )
    orders = spectra.shape[0] // 2
    found = []
    for i in range(count):
        columns = slice(i * channels, (i + 1) * channels)
        parts = jnp.concatenate([spectra[:orders, columns], spectra[orders:, columns]], axis=1)
        found.append(parts * row_weight(first_row + i, lat_total, lon_total))
    return found


def interior_kernel(
    lat_total,
    own_ref,
    other_ref,
    first_ref,
    second_ref,
    after_ref,
    first_out,
    second_out,
    dft_out,
    near_out,
    coeffs_out,
    rows_ref,
    band_ref,
    mid_ref,
    hidden_ref,
):
    del after_ref
    row_count, channels, lon_part = own_ref.shape
    lon_total = 2 * lon_part
    half = row_count // 2
    side = lax.axis_index("lon")
    for source, target in ((first_ref, first_out), (second_ref, second_out)):
        for b in range(3):
            target[b * channels : (b + 1) * channels, :] = jnp.concatenate(
                [source[a, b] for a in range(3)], axis=1
            )
    orders = dft_out.shape[0] // 2
    waves = lax.broadcasted_iota(jnp.int32, (orders, lon_total), 0)
    points = lax.broadcasted_iota(jnp.int32, (orders, lon_total), 1)
    angle = ((waves * points) & (lon_total - 1)).astype(jnp.float32) * (2.0 * math.pi / lon_total)
    dft_out[:orders, :] = jnp.cos(angle).astype(jnp.bfloat16)
    dft_out[orders:, :] = (-jnp.sin(angle)).astype(jnp.bfloat16)
    unpack_rows(other_ref, rows_ref)
    for i in range(half + 2):
        row = 2 * side + i
        place_row(band_ref, i, side, own_ref[row], packed_row(rows_ref, row, channels))
    weights = first_out[...]
    for i in range(half):
        mid_ref[i] = layer(band_ref, weights, i).astype(jnp.bfloat16)
    near_out[...] = mid_ref[pl.ds((half - 2) * side, 2)]
    weights = second_out[...]
    for i in range(half - 2):
        hidden_ref[i] = layer(mid_ref, weights, i).astype(jnp.bfloat16)
    first_row = lax.axis_index("lat") * row_count + side * half + 2 * (1 - side)
    found = row_spectra(dft_out[...], hidden_ref[...], first_row, lat_total)
    for i, values in enumerate(found):
        coeffs_out[i] = values


def edge_kernel(
    lat_total,
    half,
    halo_ref,
    message_ref,
    near_ref,
    first_ref,
    second_ref,
    dft_ref,
    coeffs_ref,
    after_ref,
    out_ref,
    band_ref,
    mid_ref,
    hidden_ref,
    packed_ref,
):
    del after_ref
    side = lax.axis_index("lon")
    first_row = lax.axis_index("lat") * (2 * half) + side * half
    band_ref[pl.ds(2 * side, 2)] = halo_ref[...]
    band_ref[pl.ds(2 - 2 * side, 2)] = message_ref[...]
    mid_ref[pl.ds(2 - 2 * side, 2)] = near_ref[...]
    weights = first_ref[...]
    for i in range(2):
        place = first_row - 1 + side * half + i
        values = layer(band_ref, weights, i)
        values = jnp.where((place >= 0) & (place < lat_total), values, 0.0)
        mid_ref[2 * side + i] = values.astype(jnp.bfloat16)
    weights = second_ref[...]
    for i in range(2):
        hidden_ref[i] = layer(mid_ref, weights, i).astype(jnp.bfloat16)
    edge = side * (half - 2)
    found = row_spectra(dft_ref[...], hidden_ref[...], first_row + edge, lat_total)
    orders = dft_ref.shape[0] // 2
    for i in range(2):
        packed_ref[pl.ds(edge + i, orders, stride=half), :] = found[i]
    for i in range(half - 2):
        packed_ref[pl.ds(2 - 2 * side + i, orders, stride=half), :] = coeffs_ref[i]
    out_ref[...] = packed_ref[...].astype(jnp.bfloat16).reshape(out_ref.shape)


def mixing_kernel(per_device, mixing_ref, after_ref, out_ref, source_ref, target_ref):
    del after_ref
    degrees, kept, channels = mixing_ref.shape
    source_ref[:, :channels] = mixing_ref[...].astype(jnp.float32).reshape(degrees * kept, channels)
    tiles = per_device * degrees // LANES
    for o in range(kept):
        block = source_ref[pl.ds(o, degrees, stride=kept), :].T[:channels]
        block = jnp.concatenate([block] * per_device, axis=1)
        for tile in range(tiles):
            target_ref[tile, pl.ds(o, channels, stride=kept), :] = block[
                :, tile * LANES : (tile + 1) * LANES
            ]
    for tile in range(tiles):
        out_ref[:, :, tile * LANES : (tile + 1) * LANES] = (
            target_ref[tile].astype(jnp.bfloat16).reshape(channels, kept, LANES)
        )


def split_index(index, size):
    quotient = ((index.astype(jnp.float32) + 0.5) * (1.0 / size)).astype(jnp.int32)
    return quotient, index - quotient * size


def legendre_kernel(
    span, bands, row_count, per_device, after_ref, analysis_ref, synthesis_ref, first_ref, second_ref
):
    del after_ref
    degrees, width = first_ref.shape
    lat_total = bands * row_count
    half = row_count // 2
    first_order = (2 * lax.axis_index("lat") + lax.axis_index("lon")) * per_device
    lane = lax.broadcasted_iota(jnp.int32, (2, width), 1)
    form = lax.broadcasted_iota(jnp.int32, (2, width), 0)
    rest, low = split_index(lane, half)
    device, own_first = split_index(rest, per_device)
    rest, band = split_index(lane, bands)
    own_second, inner = split_index(rest, row_count)
    own = jnp.where(form == 0, own_first, own_second)
    row = jnp.where(form == 0, device * half + low, band * row_count + inner)
    south = row >= lat_total // 2
    row = jnp.where(south, lat_total - 1 - row, row)
    colatitude = (row.astype(jnp.float32) + 0.5) * (math.pi / lat_total)
    cosine, sine_theta = jnp.cos(colatitude), jnp.sin(colatitude)
    order_ids = first_order + own
    orders = order_ids.astype(jnp.float32)
    counter = 1.0 + lax.broadcasted_iota(jnp.int32, (1, max(degrees, LANES)), 1).astype(jnp.float32)
    log_terms = jnp.log((2.0 * counter - 1.0) / (2.0 * counter))
    log_start = 0.5 * jnp.log(orders + 0.5) + orders * jnp.log(sine_theta)
    for m in range(per_device):
        below = counter <= jnp.full(counter.shape, first_order + m, jnp.int32).astype(jnp.float32)
        total = jnp.sum(jnp.where(below, log_terms, 0.0), axis=1, keepdims=True)
        log_start = log_start + jnp.where(own == m, 0.5 * total, 0.0)
    parity = (1 - 2 * (order_ids & 1)).astype(jnp.float32)
    even_sign, odd_sign = jnp.where(south, parity, 1.0), jnp.where(south, -parity, 1.0)
    orders_squared = orders * orders

    def advance(block, carry):
        current, previous, log_scale = carry
        for offset in range(span):
            degree_id = block * span + offset
            degree = jnp.full(orders.shape, degree_id, jnp.int32).astype(jnp.float32)
            earlier = degree - 1.0
            coef_a = jnp.sqrt(
                jnp.maximum(4.0 * degree * degree - 1.0, 1.0)
                / jnp.maximum(degree * degree - orders_squared, 1.0)
            )
            coef_b = jnp.sqrt(
                jnp.maximum(earlier * earlier - orders_squared, 0.0)
                / jnp.maximum(4.0 * earlier * earlier - 1.0, 1.0)
            )
            newest = coef_a * (cosine * current - coef_b * previous)
            is_start = degree == orders
            before = degree < orders
            newest = jnp.where(before, 0.0, jnp.where(is_start, 1.0, newest))
            log_scale = jnp.where(is_start, log_start, log_scale)
            previous = jnp.where(is_start | before, 0.0, current)
            current = newest
            sign = even_sign if offset % 2 == 0 else odd_sign
            emitted = newest * jnp.exp(log_scale) * sign
            first_ref[pl.ds(degree_id, 1), :] = emitted[0:1]
            second_ref[pl.ds(degree_id, 1), :] = emitted[1:2]
        size_now = jnp.maximum(jnp.abs(current), jnp.abs(previous))
        safe_size = jnp.where(size_now > 0.0, size_now, 1.0)
        return current / safe_size, previous / safe_size, log_scale + jnp.log(safe_size)

    zeros = jnp.zeros_like(cosine)
    lax.fori_loop(0, degrees // span, advance, (zeros, zeros, zeros))
    values = first_ref[...]
    for m in range(per_device):
        analysis_ref[m * degrees : (m + 1) * degrees, :] = jnp.where(
            own[0:1] == m, values, 0.0
        ).astype(jnp.bfloat16)
    stacked = jnp.concatenate(
        [second_ref[:, m * lat_total : (m + 1) * lat_total] for m in range(per_device)], axis=0
    )
    synthesis_ref[...] = stacked.T.astype(jnp.bfloat16)


def spectral_kernel(
    per_device,
    pieces_ref,
    analysis_ref,
    synthesis_ref,
    mine_ref,
    theirs_ref,
    out_ref,
    spectral_ref,
    chunk_ref,
):
    owners, chunk_rows, width = pieces_ref.shape
    channels, kept, columns = mine_ref.shape
    degrees = columns // per_device
    parts = 2 * per_device
    groups = chunk_rows // parts
    packed = width // kept
    bands = synthesis_ref.shape[0] // (groups * packed)

    pieces = pieces_ref[...].reshape(owners * chunk_rows, width)
    spectral = jnp.dot(analysis_ref[...], pieces, preferred_element_type=jnp.float32)
    spectral_ref[...] = spectral.T.astype(jnp.bfloat16).astype(jnp.float32)

    def add_channel(channel, totals):
        rows = [spectral_ref[pl.ds(part * channels + channel, 1), :] for part in range(2)]
        mine = mine_ref[channel].astype(jnp.float32)
        theirs = theirs_ref[channel].astype(jnp.float32)
        return (
            totals[0] + mine * rows[0],
            totals[1] + mine * rows[1],
            totals[2] + theirs * rows[0],
            totals[3] + theirs * rows[1],
        )

    zeros = jnp.zeros((kept, columns), jnp.float32)
    totals = lax.fori_loop(0, channels, add_channel, (zeros,) * 4, unroll=8)
    upper = lax.axis_index("lon") == 0
    mixed = [
        [jnp.where(upper, totals[part], totals[2 + part]) for part in range(2)],
        [jnp.where(upper, totals[2 + part], totals[part]) for part in range(2)],
    ]
    lane = lax.broadcasted_iota(jnp.int32, (kept, columns), 1)
    blocks = []
    for side in range(2):
        for m in range(per_device):
            own = (lane >= m * degrees) & (lane < (m + 1) * degrees)
            for part in range(2):
                blocks.append(jnp.where(own, mixed[side][part], 0.0).astype(jnp.bfloat16))
    values = lax.dot_general(
        synthesis_ref[...],
        jnp.concatenate(blocks, axis=0),
        (((1,), (1,)), ((), ())),
        preferred_element_type=jnp.float32,
    )
    for side in range(2):
        for group in range(groups):
            for part in range(parts):
                start = (side * parts + part) * kept
                pieces = [
                    values[(group * packed + i) * bands : (group * packed + i + 1) * bands, start : start + kept]
                    for i in range(packed)
                ]
                place = (side * groups + group) * parts + part
                chunk_ref[pl.ds(place, bands, stride=2 * groups * parts), :] = jnp.concatenate(
                    pieces, axis=1
                )
    out_ref[...] = chunk_ref[...].astype(jnp.bfloat16).reshape(out_ref.shape)


def inverse_table_kernel(groups, per_device, after_ref, out_ref):
    del after_ref
    height, width = out_ref.shape
    lon_total = width // groups
    row = lax.broadcasted_iota(jnp.int32, (height, lon_total), 0)
    points = lax.broadcasted_iota(jnp.int32, (height, lon_total), 1)
    rest, part = split_index(row, 2)
    rest, order = split_index(rest, per_device)
    owner, group = split_index(rest, groups)
    waves = owner * per_device + order
    angle = ((waves * points) & (lon_total - 1)).astype(jnp.float32) * (2.0 * math.pi / lon_total)
    values = jnp.where(part == 0, jnp.cos(angle), -jnp.sin(angle))
    values = jnp.where(waves == 0, 1.0, 2.0) * values
    for i in range(groups):
        out_ref[:, i * lon_total : (i + 1) * lon_total] = jnp.where(
            group == i, values, 0.0
        ).astype(jnp.bfloat16)


def inverse_kernel(pieces_ref, inverse_ref, out_ref, rows_ref):
    owners, chunk_rows, width = pieces_ref.shape
    kept, row_count, lon_total = out_ref.shape
    packed = width // kept
    pieces = pieces_ref[...].reshape(owners * chunk_rows, width)
    values = lax.dot_general(
        pieces, inverse_ref[...], (((0,), (0,)), ((), ())), preferred_element_type=jnp.float32
    )
    for row in range(row_count):
        group, place = row // packed, row % packed
        block = values[place * kept : (place + 1) * kept, group * lon_total : (group + 1) * lon_total]
        for tile in range(lon_total // LANES):
            rows_ref[tile, pl.ds(row, kept, stride=row_count), :] = block[:, tile * LANES : (tile + 1) * LANES]
    for tile in range(lon_total // LANES):
        out_ref[:, :, tile * LANES : (tile + 1) * LANES] = (
            rows_ref[tile].astype(jnp.bfloat16).reshape(kept, row_count, LANES)
        )


def local(fields, conv_first, conv_second, mixing):
    lat_count = lax.axis_size("lat")
    lon_count = lax.axis_size("lon")
    channels, row_count, lon_part = fields.shape
    lat_total = row_count * lat_count
    lon_total = lon_part * lon_count
    orders = lat_total // 2
    degrees = mixing.shape[0]
    owners = lat_count * lon_count
    per_device = orders // owners
    half = row_count // 2
    kept = channels // 2
    swap = [(0, 1), (1, 0)]
    both = ("lat", "lon")
    bfloat = functools.partial(jax.ShapeDtypeStruct, dtype=jnp.bfloat16)

    other = lax.ppermute(fields, "lon", swap)
    other_mixing = lax.ppermute(mixing, "lon", swap)
    unpacked = pltpu.VMEM((lon_part // LANES, channels * row_count, LANES), jnp.float32)
    own = call(
        rows_kernel,
        bfloat((row_count, channels, lon_part)),
        [unpacked],
        [VMEM],
        pl.CostEstimate(flops=1 << 16, bytes_accessed=1 << 18, transcendentals=0),
    )(fields)
    message = call(
        message_kernel,
        bfloat((2, channels, lon_total)),
        [unpacked],
        [VMEM, VMEM],
        pl.CostEstimate(flops=1 << 16, bytes_accessed=1 << 18, transcendentals=0),
    )(own, other)
    pairs = []
    for i in range(lat_count - 1):
        pairs.append((2 * i + 1, 2 * (i + 1)))
        pairs.append((2 * (i + 1), 2 * i + 1))
    halo = lax.ppermute(message, both, pairs)

    taps = (3 * channels, 3 * channels)
    first, second, dft, near, interior = call(
        functools.partial(interior_kernel, lat_total),
        (
            bfloat(taps),
            bfloat(taps),
            bfloat((2 * orders, lon_total)),
            bfloat((2, channels, lon_total)),
            jax.ShapeDtypeStruct((half - 2, orders, 2 * channels), jnp.float32),
        ),
        [
            unpacked,
            pltpu.VMEM((half + 2, channels, lon_total), jnp.bfloat16),
            pltpu.VMEM((half, channels, lon_total), jnp.bfloat16),
            pltpu.VMEM((half - 2, channels, lon_total), jnp.bfloat16),
        ],
        [VMEM, VMEM, VMEM, VMEM, ANY],
        pl.CostEstimate(flops=1 << 28, bytes_accessed=1 << 22, transcendentals=0),
    )(
        own,
        other,
        jnp.transpose(conv_first, (2, 3, 0, 1)),
        jnp.transpose(conv_second, (2, 3, 0, 1)),
        message,
    )
    columns = per_device * degrees
    columns = per_device * degrees
    def mixing_table(values, after):
        return call(
            functools.partial(mixing_kernel, per_device),
            bfloat((channels, kept, columns)),
            [
                pltpu.VMEM((degrees * kept, LANES), jnp.float32),
                pltpu.VMEM((columns // LANES, channels * kept, LANES), jnp.float32),
            ],
            [VMEM, ANY],
            pl.CostEstimate(flops=1 << 20, bytes_accessed=1 << 22, transcendentals=0),
        )(values, after)

    mine = mixing_table(mixing, near)
    coeffs = call(
        functools.partial(edge_kernel, lat_total, half),
        bfloat((owners, per_device * half, 2 * channels)),
        [
            pltpu.VMEM((4, channels, lon_total), jnp.bfloat16),
            pltpu.VMEM((4, channels, lon_total), jnp.bfloat16),
            pltpu.VMEM((2, channels, lon_total), jnp.bfloat16),
            pltpu.VMEM((orders * half, 2 * channels), jnp.float32),
        ],
        [VMEM] * 7 + [ANY],
        pl.CostEstimate(flops=1 << 26, bytes_accessed=1 << 20, transcendentals=0),
    )(halo, message, near, first, second, dft, interior, mine)
    pieces = lax.all_to_all(coeffs, both, split_axis=0, concat_axis=0, tiled=True)

    theirs = mixing_table(other_mixing, coeffs)
    span = 32 if degrees % 32 == 0 else degrees
    width = lat_total * per_device
    analysis, synthesis = call(
        functools.partial(legendre_kernel, span, lat_count, row_count, per_device),
        (bfloat((columns, width)), bfloat((lat_total, columns))),
        [pltpu.VMEM((degrees, width), jnp.float32), pltpu.VMEM((degrees, width), jnp.float32)],
        [ANY],
        pl.CostEstimate(flops=1 << 20, bytes_accessed=1 << 21, transcendentals=0),
    )(coeffs)
    chunk_rows = row_count * 2 * per_device * kept // LANES
    chunks = call(
        functools.partial(spectral_kernel, per_device),
        bfloat((owners, chunk_rows, LANES)),
        [
            pltpu.VMEM((2 * channels, columns), jnp.float32),
            pltpu.VMEM((owners * chunk_rows, LANES), jnp.float32),
        ],
        [VMEM] * 5,
        pl.CostEstimate(flops=1 << 24, bytes_accessed=1 << 20, transcendentals=0),
    )(pieces, analysis, synthesis, mine, theirs)

    back = lax.all_to_all(chunks, both, split_axis=0, concat_axis=0, tiled=True)
    groups = chunk_rows // (2 * per_device)
    table = call(
        functools.partial(inverse_table_kernel, groups, per_device),
        bfloat((owners * chunk_rows, groups * lon_total)),
        [],
        [ANY],
        pl.CostEstimate(flops=1 << 22, bytes_accessed=1 << 21, transcendentals=0),
    )(chunks)
    return call(
        inverse_kernel,
        bfloat((kept, row_count, lon_total)),
        [pltpu.VMEM((lon_total // LANES, kept * row_count, LANES), jnp.float32)],
        [VMEM] * 2,
        pl.CostEstimate(flops=1 << 24, bytes_accessed=1 << 19, transcendentals=0),
    )(back, table)


def solution(mesh):
    in_specs = (P("groups", "lat", "lon"), P(), P(), P(None, "lon", None))
    out_specs = P(("groups", "lon"), "lat", None)
    return jax.shard_map(local, mesh=mesh, in_specs=in_specs, out_specs=out_specs, check_vma=False)
```

time: 43.9 us -> 36.8 us (0.84)
  Pallas kernels: 5.06 us -> 10.2 us
  other arithmetic: 3.74 us -> 0 us
  local copies, waits for them, and re-layouts: 4.43 us -> 0.92 us
  starting transfers between devices: 16.6 us -> 13.9 us
  waiting for transfers between devices: 13.5 us -> 11.3 us
    pallas_call x4 -> x10, Pallas kernels: 5.06 us -> 10.2 us  [the longest x2 2.98 us: mixing_table(): call(functools.partial(mixing_kernel, per_device), bfloat((channels, kept...]
    all_to_all x1, starting transfers between devices: 12.7 us -> 10 us  [local(): lax.all_to_all(coeffs, both, split_axis=0, concat_axis=0, tiled=True)]
    unnamed x9 -> x8, local copies, waits for them, and re-layouts: 3.14 us -> 0.92 us
    all_to_all x1, waiting for transfers between devices: 6.43 us -> 4.92 us  [local(): lax.all_to_all(coeffs, both, split_axis=0, concat_axis=0, tiled=True)]
    unnamed x5 -> x0, other arithmetic: 1.47 us -> none
    all_to_all x1, waiting for transfers between devices: 7.09 us -> 6.26 us  [local(): back = lax.all_to_all(chunks, both, split_axis=0, concat_axis=0, tiled=True)]
    another operation x6 -> x0, other arithmetic: 0.62 us -> none
    concatenate x3 -> x0, other arithmetic: 0.61 us -> none  [the longest x1 0.58 us: local(): jnp.concatenate([jnp.transpose(mixing, (2, 1, 0))] * per_device, axis=2)]
  transfers between devices with their start and end apart: 5 -> 5, of which waited for: 2 -> 3; matrix products, arithmetic and copies ran while one was open for 17% -> 0% of each run, Pallas kernels for 6% -> 21%
where the time goes in v3:
time: 36.8 us; the launch traced here: 36.5 us
  starting transfers between devices  13.9 us (38%)
  waiting for transfers between devices  11.3 us (31%)
  Pallas kernels  10.2 us (28%)
  local copies, waits for them, and re-layouts  0.92 us (2%)
    all_to_all x1, starting transfers between devices, local(): lax.all_to_all(coeffs, both, split_axis=0, concat_axis=0, tiled=True)  10 us
    all_to_all x1, waiting for transfers between devices, local(): back = lax.all_to_all(chunks, both, split_axis=0, concat_axis=0, tiled=True)  6.26 us
    all_to_all x1, waiting for transfers between devices, local(): lax.all_to_all(coeffs, both, split_axis=0, concat_axis=0, tiled=True)  4.92 us
    pallas_call x2, Pallas kernels, mixing_table(): call(functools.partial(mixing_kernel, per_device), bfloat((channels, kept...  2.98 us
    all_to_all x1, starting transfers between devices, local(): back = lax.all_to_all(chunks, both, split_axis=0, concat_axis=0, tiled=True)  2.57 us
    pallas_call x1, Pallas kernels, local(): call(functools.partial(spectral_kernel, per_device), bfloat((owners, chun...  1.59 us
    pallas_call x1, Pallas kernels, local(): call(functools.partial(edge_kernel, lat_total, half), bfloat((owners, per...  1.48 us
    pallas_call x1, Pallas kernels, local(): call(functools.partial(inverse_table_kernel, groups, per_device), bfloat(...  1.15 us
  transfers between devices with their start and end apart: 5, of which 3 were waited for; matrix products, arithmetic and copies ran while one was open for 0% of the time, Pallas kernels for 21%

profile of v3, /device:TPU:0, one launch (start us, length us, event | category | flops | bytes accessed | tf_op | source)
XLA Modules:
  0.0 36.5 jit_solution(14803154886918939299)
XLA Ops:
  0.0 0.5 %collective-permute-start = (bf16[64,8,128]{2,1,0:T(8,128)(2,1)}, bf16[64,8,128]{2,1,0:T(8,128)(2,1)S(1)}, u32[]{:S(2)}, u32[]{:S(2)}) collective-permute-start(bf16[64,8,128]{2,1,0:T(8,128)(2,1)} %source_ref.1), channel_id=1, source_target_pairs={{0,1},{1,0},{2,3},{3,2},{4,5},{5,4},{6,7},{7,6},{8,9},{9,8},{10,11... | collective-permute-start | bytes 393224 | tf_op jit(solution)/shard_map/ppermute | solution.py:416
  0.5 0.1 collective-permute-start.2
  0.5 0.0 copy-start.1
  0.5 0.9 %copy-done.1 = bf16[64,8,128]{2,1,0:T(8,128)(2,1)S(1)} copy-done((bf16[64,8,128]{2,1,0:T(8,128)(2,1)S(1)}, bf16[64,8,128]{2,1,0:T(8,128)(2,1)}, u32[]{:S(2)}) %copy-start.1) | copy-done | bytes 131096
  1.4 0.1 shard_map.46.own_ref
  1.5 0.0 copy-start.2
  1.5 0.0 copy-start.3
  1.5 0.1 collective-permute-done.other_ref
  1.7 0.0 copy-start
  1.7 0.8 %collective-permute-start.1 = (bf16[2,64,256]{2,1,0:T(8,128)(2,1)S(1)}, bf16[2,64,256]{2,1,0:T(8,128)(2,1)S(1)}, u32[]{:S(2)}, u32[]{:S(2)}) collective-permute-start(bf16[2,64,256]{2,1,0:T(8,128)(2,1)S(1)} %shard_map.47.after_ref.message_ref), channel_id=1, source_target_pairs={{1,2},{2,1},{3,4},{4,3},{5,6},{6,5},{7,8},{8,7},{9,10},{10,9},{11,... | collective-permute-start | bytes 196616 | tf_op jit(solution)/shard_map/ppermute | solution.py:437
  2.5 0.0 copy-done.2
  2.5 0.0 copy-done.3
  2.5 1.1 %shard_map.48 = (bf16[192,192]{1,0:T(8,128)(2,1)S(1)}, bf16[192,192]{1,0:T(8,128)(2,1)S(1)}, bf16[128,256]{1,0:T(8,128)(2,1)S(1)}, bf16[2,64,256]{2,1,0:T(8,128)(2,1)S(1)}, f32[2,64,128]{2,1,0:T(8,128)S(1)}) custom-call(bf16[8,64,128]{2,1,0:T(8,128)(2,1)S(1)} %shard_map.46.own_ref, bf16[64,8,128]{2,1,0:T(8,128)(2,1)S(1)} %collective-permute-done.other_ref, ...), custom_call_target="tpu_custom_call" | custom-call | flops 268435456 | bytes 4194304 | tf_op jit(solution)/shard_map/pallas_call | solution.py:440
  3.6 0.0 copy-done
  3.6 1.5 %shard_map.49.after_ref.mine_ref = bf16[64,32,128]{2,1,0:T(8,128)(2,1)S(1)} custom-call(bf16[64,32,64]{2,1,0:T(8,128)(2,1)S(1)} %copy-done, bf16[2,64,256]{2,1,0:T(8,128)(2,1)S(1)} %get-tuple-element.12.after_ref.near_ref), custom_call_target="tpu_custom_call" | custom-call | flops 1048576 | bytes 4194304 | tf_op jit(solution)/shard_map/pallas_call | solution.py:467
  5.1 0.0 collective-permute-done.1.halo_ref
  5.1 1.5 %shard_map.50.after_ref = bf16[32,8,128]{2,1,0:T(8,128)(2,1)} custom-call(bf16[2,64,256]{2,1,0:T(8,128)(2,1)S(1)} %collective-permute-done.1.halo_ref, bf16[2,64,256]{2,1,0:T(8,128)(2,1)S(1)} %shard_map.47.after_ref.message_ref, bf16[2,64,256]{2,1,0:T(8,128)(2,1)S(1)} %get-tuple-element.12.after_ref.near_ref, ...), custom_call_target="tpu_custom_call" | custom-call | flops 67108864 | bytes 1048576 | tf_op jit(solution)/shard_map/pallas_call | solution.py:479
  6.6 10.0 %all-to-all-start = ((bf16[32,8,128]{2,1,0:T(8,128)(2,1)}), bf16[32,8,128]{2,1,0:T(8,128)(2,1)S(1)}, u32[]{:S(2)}, u32[]{:S(2)}) async-start(bf16[32,8,128]{2,1,0:T(8,128)(2,1)} %shard_map.50.after_ref), calls=%async_computation | async-start | bytes 131072 | tf_op jit(solution)/shard_map/all_to_all | solution.py:491
  16.6 1.0 %shard_map.51 = (bf16[128,256]{1,0:T(8,128)(2,1)S(1)}, bf16[128,128]{1,0:T(8,128)(2,1)S(1)}) custom-call(bf16[32,8,128]{2,1,0:T(8,128)(2,1)} %shard_map.50.after_ref), custom_call_target="tpu_custom_call" | custom-call | flops 1048576 | bytes 2097152 | tf_op jit(solution)/shard_map/pallas_call | solution.py:496
  17.6 0.0 collective-permute-done.2.mixing_ref
  17.6 1.5 %shard_map.52.theirs_ref = bf16[64,32,128]{2,1,0:T(8,128)(2,1)S(1)} custom-call(bf16[64,32,64]{2,1,0:T(8,128)(2,1)S(1)} %collective-permute-done.2.mixing_ref, bf16[32,8,128]{2,1,0:T(8,128)(2,1)} %shard_map.50.after_ref), custom_call_target="tpu_custom_call" | custom-call | flops 1048576 | bytes 4194304 | tf_op jit(solution)/shard_map/pallas_call | solution.py:467
  19.1 4.9 %all-to-all-done.pieces_ref = bf16[32,8,128]{2,1,0:T(8,128)(2,1)S(1)} async-done(((bf16[32,8,128]{2,1,0:T(8,128)(2,1)}), bf16[32,8,128]{2,1,0:T(8,128)(2,1)S(1)}, u32[]{:S(2)}, u32[]{:S(2)}) %all-to-all-start) | async-done | bytes 65568 | tf_op jit(solution)/shard_map/all_to_all | solution.py:491
  24.1 1.6 %shard_map.53.after_ref = bf16[32,8,128]{2,1,0:T(8,128)(2,1)} custom-call(bf16[32,8,128]{2,1,0:T(8,128)(2,1)S(1)} %all-to-all-done.pieces_ref, bf16[128,256]{1,0:T(8,128)(2,1)S(1)} %get-tuple-element.17.analysis_ref, bf16[128,128]{1,0:T(8,128)(2,1)S(1)} %get-tuple-element.18.synthesis_ref, bf16[64,32,128]{2,1,0:T(8,128)(2,1)S(1)} %shard_map.49.after_ref.mine_ref, ...), custom_call_target="tpu_custom_call" | custom-call | flops 16777216 | bytes 1048576 | tf_op jit(solution)/shard_map/pallas_call | solution.py:504
  25.6 2.6 %all-to-all-start.1 = ((bf16[32,8,128]{2,1,0:T(8,128)(2,1)}), bf16[32,8,128]{2,1,0:T(8,128)(2,1)S(1)}, u32[]{:S(2)}, u32[]{:S(2)}) async-start(bf16[32,8,128]{2,1,0:T(8,128)(2,1)} %shard_map.53.after_ref), calls=%async_computation.1 | async-start | bytes 131072 | tf_op jit(solution)/shard_map/all_to_all | solution.py:515
  28.2 1.1 %shard_map.54.inverse_ref = bf16[256,512]{1,0:T(8,128)(2,1)S(1)} custom-call(bf16[32,8,128]{2,1,0:T(8,128)(2,1)} %shard_map.53.after_ref), custom_call_target="tpu_custom_call" | custom-call | flops 4194304 | bytes 2097152 | tf_op jit(solution)/shard_map/pallas_call | solution.py:517
  29.4 6.3 %all-to-all-done.1.pieces_ref = bf16[32,8,128]{2,1,0:T(8,128)(2,1)S(1)} async-done(((bf16[32,8,128]{2,1,0:T(8,128)(2,1)}), bf16[32,8,128]{2,1,0:T(8,128)(2,1)S(1)}, u32[]{:S(2)}, u32[]{:S(2)}) %all-to-all-start.1) | async-done | bytes 65568 | tf_op jit(solution)/shard_map/all_to_all | solution.py:515
  35.6 0.9 %shard_map.55 = bf16[32,8,256]{2,1,0:T(8,128)(2,1)} custom-call(bf16[32,8,128]{2,1,0:T(8,128)(2,1)S(1)} %all-to-all-done.1.pieces_ref, bf16[256,512]{1,0:T(8,128)(2,1)S(1)} %shard_map.54.inverse_ref), custom_call_target="tpu_custom_call" | custom-call | flops 16777216 | bytes 524288 | tf_op jit(solution)/shard_map/pallas_call | solution.py:524
  (1 shorter events, 0.0 us)
Async XLA Ops:
  0.0 1.6 %collective-permute-start = (bf16[64,8,128]{2,1,0:T(8,128)(2,1)}, bf16[64,8,128]{2,1,0:T(8,128)(2,1)S(1)}, u32[]{:S(2)}, u32[]{:S(2)}) collective-permute-start(bf16[64,8,128]{2,1,0:T(8,128)(2,1)} %source_ref.1), channel_id=1, source_target_pairs={{0,1},{1,0},{2,3},{3,2},{4,5},{5,4},{6,7},{7,6},{8,9},{9,8},{10,11... | collective-permute-start | bytes 393224 | tf_op jit(solution)/shard_map/ppermute | solution.py:416
  0.5 17.2 %collective-permute-start.2 = (bf16[64,32,64]{2,1,0:T(8,128)(2,1)}, bf16[64,32,64]{2,1,0:T(8,128)(2,1)S(1)}, u32[]{:S(2)}, u32[]{:S(2)}) collective-permute-start(bf16[64,32,64]{2,1,0:T(8,128)(2,1)} %mixing_ref.1), channel_id=1, source_target_pairs={{0,1},{1,0},{2,3},{3,2},{4,5},{5,4},{6,7},{7,6},{8,9},{9,8},{10,11... | collective-permute-start | bytes 786440 | tf_op jit(solution)/shard_map/ppermute | solution.py:417
  0.5 0.9 %copy-start.1 = (bf16[64,8,128]{2,1,0:T(8,128)(2,1)S(1)}, bf16[64,8,128]{2,1,0:T(8,128)(2,1)}, u32[]{:S(2)}) copy-start(bf16[64,8,128]{2,1,0:T(8,128)(2,1)} %source_ref.1) | copy-start | bytes 393220
  1.5 1.0 %copy-start.2 = (bf16[64,64,3,3]{1,0,3,2:T(8,128)(2,1)S(1)}, bf16[64,64,3,3]{1,0,3,2:T(8,128)(2,1)}, u32[]{:S(2)}) copy-start(bf16[64,64,3,3]{1,0,3,2:T(8,128)(2,1)} %param.5) | copy-start | bytes 221188
  1.5 1.0 %copy-start.3 = (bf16[64,64,3,3]{1,0,3,2:T(8,128)(2,1)S(1)}, bf16[64,64,3,3]{1,0,3,2:T(8,128)(2,1)}, u32[]{:S(2)}) copy-start(bf16[64,64,3,3]{1,0,3,2:T(8,128)(2,1)} %param.6) | copy-start | bytes 221188
  1.7 1.9 %copy-start = (bf16[64,32,64]{2,1,0:T(8,128)(2,1)S(1)}, bf16[64,32,64]{2,1,0:T(8,128)(2,1)}, u32[]{:S(2)}) copy-start(bf16[64,32,64]{2,1,0:T(8,128)(2,1)} %mixing_ref.1) | copy-start | bytes 786436
  1.7 3.4 %collective-permute-start.1 = (bf16[2,64,256]{2,1,0:T(8,128)(2,1)S(1)}, bf16[2,64,256]{2,1,0:T(8,128)(2,1)S(1)}, u32[]{:S(2)}, u32[]{:S(2)}) collective-permute-start(bf16[2,64,256]{2,1,0:T(8,128)(2,1)S(1)} %shard_map.47.after_ref.message_ref), channel_id=1, source_target_pairs={{1,2},{2,1},{3,4},{4,3},{5,6},{6,5},{7,8},{8,7},{9,10},{10,9},{11,... | collective-permute-start | bytes 196616 | tf_op jit(solution)/shard_map/ppermute | solution.py:437
  6.6 17.5 %all-to-all-start = ((bf16[32,8,128]{2,1,0:T(8,128)(2,1)}), bf16[32,8,128]{2,1,0:T(8,128)(2,1)S(1)}, u32[]{:S(2)}, u32[]{:S(2)}) async-start(bf16[32,8,128]{2,1,0:T(8,128)(2,1)} %shard_map.50.after_ref), calls=%async_computation | async-start | bytes 131072 | tf_op jit(solution)/shard_map/all_to_all | solution.py:491
  25.6 10.0 %all-to-all-start.1 = ((bf16[32,8,128]{2,1,0:T(8,128)(2,1)}), bf16[32,8,128]{2,1,0:T(8,128)(2,1)S(1)}, u32[]{:S(2)}, u32[]{:S(2)}) async-start(bf16[32,8,128]{2,1,0:T(8,128)(2,1)} %shard_map.53.after_ref), calls=%async_computation.1 | async-start | bytes 131072 | tf_op jit(solution)/shard_map/all_to_all | solution.py:515

commit v4 on v3

v4 whole, which is shorter than its diff:
```python
import functools
import math

import jax
import jax.numpy as jnp
from jax import lax
from jax.experimental import pallas as pl
from jax.experimental.pallas import tpu as pltpu
from jax.sharding import PartitionSpec as P

VMEM = pl.BlockSpec(memory_space=pltpu.VMEM)
ANY = pl.BlockSpec(memory_space=pl.ANY)
HBM = pl.BlockSpec(memory_space=pltpu.HBM)
LIMIT = 40 * 1024 * 1024
LANES = 128


def call(kernel, out_shape, scratch, in_specs, cost):
    return pl.pallas_call(
        kernel,
        out_shape=out_shape,
        in_specs=in_specs,
        out_specs=jax.tree.map(lambda _: VMEM, out_shape),
        scratch_shapes=scratch,
        compiler_params=pltpu.CompilerParams(vmem_limit_bytes=LIMIT),
        cost_estimate=cost,
    )


def split_index(index, size):
    quotient = ((index.astype(jnp.float32) + 0.5) * (1.0 / size)).astype(jnp.int32)
    return quotient, index - quotient * size


def row_half():
    return (lax.axis_index("lat") + lax.axis_index("lon") + 1) & 1


def unpack_rows(source_ref, rows_ref):
    channels, row_count, lon_part = source_ref.shape
    for tile in range(lon_part // LANES):
        rows_ref[tile] = (
            source_ref[:, :, tile * LANES : (tile + 1) * LANES]
            .astype(jnp.float32)
            .reshape(channels * row_count, LANES)
        )


def packed_row(rows_ref, row, channels):
    tiles, count, _ = rows_ref.shape
    found = [
        rows_ref[tile, pl.ds(row, channels, stride=count // channels), :] for tile in range(tiles)
    ]
    return jnp.concatenate(found, axis=1).astype(jnp.bfloat16)


def load_kernel(
    fields_ref,
    conv_first_ref,
    conv_second_ref,
    own_ref,
    first_ref,
    second_ref,
    fields_copy_ref,
    rows_ref,
    arrived,
):
    copies = [
        pltpu.make_async_copy(source, target, arrived.at[i])
        for i, (source, target) in enumerate(
            (
                (fields_ref, fields_copy_ref),
                (conv_first_ref, first_ref),
                (conv_second_ref, second_ref),
            )
        )
    ]
    for copy in copies:
        copy.start()
    copies[0].wait()
    unpack_rows(fields_copy_ref, rows_ref)
    for row in range(own_ref.shape[0]):
        own_ref[row] = packed_row(rows_ref, row, own_ref.shape[1])
    for copy in copies[1:]:
        copy.wait()


def place_row(out_ref, place, side, mine, theirs):
    lon_part = mine.shape[1]
    for position, values in ((side, mine), (1 - side, theirs)):
        start = pl.multiple_of(position * lon_part, LANES)
        out_ref[place, :, pl.ds(start, lon_part)] = values


def message_kernel(own_ref, other_ref, out_ref, rows_ref):
    row_count, channels, _ = own_ref.shape
    side = lax.axis_index("lon")
    unpack_rows(other_ref, rows_ref)
    for i in range(2):
        row = row_half() * (row_count - 2) + i
        place_row(out_ref, i, side, own_ref[row], packed_row(rows_ref, row, channels))


def layer(source_ref, weights, row):
    channels, lon_total = source_ref.shape[1:]
    taps = source_ref[row : row + 3].reshape(3 * channels, lon_total)
    sums = jnp.dot(weights, taps, preferred_element_type=jnp.float32)
    total = (
        sums[channels : 2 * channels]
        + pltpu.roll(sums[:channels], 1, 1)
        + pltpu.roll(sums[2 * channels :], lon_total - 1, 1)
    )
    return jnp.maximum(total, 0.0)


def row_weight(row, lat_total, lon_total):
    place = jnp.full((1, LANES), row, jnp.int32).astype(jnp.float32)
    return jnp.sin((place + 0.5) * (math.pi / lat_total)) * (math.pi / lat_total / lon_total)


def row_spectra(dft, hidden, first_row, lat_total):
    count, channels, lon_total = hidden.shape
    spectra = lax.dot_general(
        dft,
        hidden.reshape(count * channels, lon_total),
        (((1,), (1,)), ((), ())),
        preferred_element_type=jnp.float32,
    )
    orders = spectra.shape[0] // 2
    found = []
    for i in range(count):
        columns = slice(i * channels, (i + 1) * channels)
        parts = jnp.concatenate([spectra[:orders, columns], spectra[orders:, columns]], axis=1)
        found.append(parts * row_weight(first_row + i, lat_total, lon_total))
    return found


def interior_kernel(
    lat_total,
    owners,
    own_ref,
    other_ref,
    first_ref,
    second_ref,
    after_ref,
    first_out,
    second_out,
    dft_out,
    near_out,
    coeffs_out,
    rows_ref,
    band_ref,
    mid_ref,
    hidden_ref,
):
    del after_ref
    row_count, channels, lon_part = own_ref.shape
    lon_total = 2 * lon_part
    half = row_count // 2
    side, part = lax.axis_index("lon"), row_half()
    for source, target in ((first_ref, first_out), (second_ref, second_out)):
        for b in range(3):
            target[b * channels : (b + 1) * channels, :] = jnp.concatenate(
                [source[a, b] for a in range(3)], axis=1
            )
    orders = dft_out.shape[0] // 2
    place = lax.broadcasted_iota(jnp.int32, (orders, lon_total), 0)
    order, owner = split_index(place, owners)
    waves = owner * (orders // owners) + order
    points = lax.broadcasted_iota(jnp.int32, (orders, lon_total), 1)
    angle = ((waves * points) & (lon_total - 1)).astype(jnp.float32) * (2.0 * math.pi / lon_total)
    dft_out[:orders, :] = jnp.cos(angle).astype(jnp.bfloat16)
    dft_out[orders:, :] = (-jnp.sin(angle)).astype(jnp.bfloat16)
    unpack_rows(other_ref, rows_ref)
    for i in range(half + 2):
        row = 2 * part + i
        place_row(band_ref, i, side, own_ref[row], packed_row(rows_ref, row, channels))
    weights = first_out[...]
    for i in range(half):
        mid_ref[i] = layer(band_ref, weights, i).astype(jnp.bfloat16)
    near_out[...] = mid_ref[pl.ds((half - 2) * part, 2)]
    weights = second_out[...]
    for i in range(half - 2):
        hidden_ref[i] = layer(mid_ref, weights, i).astype(jnp.bfloat16)
    first_row = lax.axis_index("lat") * row_count + part * half + 2 * (1 - part)
    found = row_spectra(dft_out[...], hidden_ref[...], first_row, lat_total)
    for i, values in enumerate(found):
        coeffs_out[i] = values


def edge_kernel(
    lat_total,
    half,
    halo_ref,
    message_ref,
    near_ref,
    first_ref,
    second_ref,
    dft_ref,
    coeffs_ref,
    mine_ref,
    theirs_ref,
    analysis_ref,
    out_ref,
    band_ref,
    mid_ref,
    hidden_ref,
    packed_ref,
):
    del mine_ref, theirs_ref, analysis_ref
    part = row_half()
    first_row = lax.axis_index("lat") * (2 * half) + part * half
    band_ref[pl.ds(2 * part, 2)] = halo_ref[...]
    band_ref[pl.ds(2 - 2 * part, 2)] = message_ref[...]
    mid_ref[pl.ds(2 - 2 * part, 2)] = near_ref[...]
    weights = first_ref[...]
    for i in range(2):
        place = first_row - 1 + part * half + i
        values = layer(band_ref, weights, i)
        values = jnp.where((place >= 0) & (place < lat_total), values, 0.0)
        mid_ref[2 * part + i] = values.astype(jnp.bfloat16)
    weights = second_ref[...]
    for i in range(2):
        hidden_ref[i] = layer(mid_ref, weights, i).astype(jnp.bfloat16)
    edge = part * (half - 2)
    found = row_spectra(dft_ref[...], hidden_ref[...], first_row + edge, lat_total)
    owners, chunk_rows, _ = out_ref.shape
    for m in range(chunk_rows // half):
        own = slice(m * owners, (m + 1) * owners)
        for i in range(2):
            start = m * half + edge + i
            packed_ref[pl.ds(start, owners, stride=chunk_rows), :] = found[i][own]
        for i in range(half - 2):
            start = m * half + 2 - 2 * part + i
            packed_ref[pl.ds(start, owners, stride=chunk_rows), :] = coeffs_ref[i, own]
    out_ref[...] = packed_ref[...].astype(jnp.bfloat16).reshape(out_ref.shape)


def mixing_kernel(per_device, mixing_ref, after_ref, out_ref):
    del after_ref
    values = jnp.transpose(mixing_ref[...].astype(jnp.float32), (1, 0, 2))
    blocks = [
        jnp.concatenate([values[o]] * per_device, axis=0).T for o in range(values.shape[0])
    ]
    out_ref[...] = jnp.transpose(jnp.stack(blocks), (1, 0, 2)).astype(jnp.bfloat16)


def legendre_kernel(
    span, bands, row_count, per_device, after_ref, analysis_ref, synthesis_ref, values_ref
):
    del after_ref
    tiles, count, _ = values_ref.shape
    degrees, width = count // 2, tiles * LANES
    lat_total = bands * row_count
    half = row_count // 2
    first_order = (2 * lax.axis_index("lat") + lax.axis_index("lon")) * per_device
    lane = lax.broadcasted_iota(jnp.int32, (2, width), 1)
    form = lax.broadcasted_iota(jnp.int32, (2, width), 0)
    rest, low = split_index(lane, half)
    device, own_first = split_index(rest, per_device)
    rest, band = split_index(lane, bands)
    own_second, inner = split_index(rest, row_count)
    own = jnp.where(form == 0, own_first, own_second)
    place = (device >> 1) * row_count + (((device >> 1) + device + 1) & 1) * half + low
    row = jnp.where(form == 0, place, band * row_count + inner)
    south = row >= lat_total // 2
    row = jnp.where(south, lat_total - 1 - row, row)
    colatitude = (row.astype(jnp.float32) + 0.5) * (math.pi / lat_total)
    cosine, sine_theta = jnp.cos(colatitude), jnp.sin(colatitude)
    order_ids = first_order + own
    orders = order_ids.astype(jnp.float32)
    counter = 1.0 + lax.broadcasted_iota(jnp.int32, (1, max(degrees, LANES)), 1).astype(jnp.float32)
    log_terms = jnp.log((2.0 * counter - 1.0) / (2.0 * counter))
    log_start = 0.5 * jnp.log(orders + 0.5) + orders * jnp.log(sine_theta)
    for m in range(per_device):
        below = counter <= jnp.full(counter.shape, first_order + m, jnp.int32).astype(jnp.float32)
        total = jnp.sum(jnp.where(below, log_terms, 0.0), axis=1, keepdims=True)
        log_start = log_start + jnp.where(own == m, 0.5 * total, 0.0)
    parity = (1 - 2 * (order_ids & 1)).astype(jnp.float32)
    even_sign, odd_sign = jnp.where(south, parity, 1.0), jnp.where(south, -parity, 1.0)
    orders_squared = orders * orders
    start_scale = jnp.exp(log_start)
    current = previous = scale = log_scale = jnp.zeros_like(cosine)
    root = jnp.zeros_like(cosine)
    for degree in range(degrees):
        distance = float(degree * degree) - orders_squared
        inverse_root = lax.rsqrt(jnp.maximum(distance, 1.0))
        above = math.sqrt(max(4.0 * degree * degree - 1.0, 1.0))
        below = math.sqrt(max(4.0 * (degree - 1) * (degree - 1) - 1.0, 1.0))
        newest = (above * inverse_root) * (cosine * current - (root * (1.0 / below)) * previous)
        root = jnp.maximum(distance, 0.0) * inverse_root
        is_start = orders == float(degree)
        newest = jnp.where(is_start, 1.0, newest)
        scale = jnp.where(is_start, start_scale, scale)
        log_scale = jnp.where(is_start, log_start, log_scale)
        previous, current = current, newest
        emitted = newest * scale * (even_sign if degree % 2 == 0 else odd_sign)
        for tile in range(tiles):
            values_ref[tile, 2 * degree : 2 * degree + 2, :] = emitted[
                :, tile * LANES : (tile + 1) * LANES
            ]
        if degree % span == span - 1 and degree < degrees - 1:
            size_now = jnp.maximum(jnp.abs(current), jnp.abs(previous))
            safe_size = jnp.where(size_now > 0.0, size_now, 1.0)
            current, previous = current / safe_size, previous / safe_size
            log_scale = log_scale + jnp.log(safe_size)
            scale = jnp.where(degree >= orders, jnp.exp(log_scale), 0.0)
    first, second = (
        jnp.concatenate(
            [values_ref[tile, pl.ds(i, degrees, stride=2), :] for tile in range(tiles)], axis=1
        )
        for i in range(2)
    )
    for m in range(per_device):
        analysis_ref[m * degrees : (m + 1) * degrees, :] = jnp.where(
            own[0:1] == m, first, 0.0
        ).astype(jnp.bfloat16)
    stacked = jnp.concatenate(
        [second[:, m * lat_total : (m + 1) * lat_total] for m in range(per_device)], axis=0
    )
    synthesis_ref[...] = stacked.T.astype(jnp.bfloat16)


def spectral_kernel(
    per_device,
    pieces_ref,
    analysis_ref,
    synthesis_ref,
    mine_ref,
    theirs_ref,
    out_ref,
    spectral_ref,
    chunk_ref,
):
    owners, chunk_rows, width = pieces_ref.shape
    channels, kept, columns = mine_ref.shape
    degrees = columns // per_device
    parts = 2 * per_device
    groups = chunk_rows // parts
    packed = width // kept
    bands = synthesis_ref.shape[0] // (groups * packed)

    pieces = pieces_ref[...].reshape(owners * chunk_rows, width)
    spectral = jnp.dot(analysis_ref[...], pieces, preferred_element_type=jnp.float32)
    spectral_ref[...] = spectral.T.astype(jnp.bfloat16).astype(jnp.float32)

    def add_channel(channel, totals):
        rows = [spectral_ref[pl.ds(part * channels + channel, 1), :] for part in range(2)]
        mine = mine_ref[channel].astype(jnp.float32)
        theirs = theirs_ref[channel].astype(jnp.float32)
        return (
            totals[0] + mine * rows[0],
            totals[1] + mine * rows[1],
            totals[2] + theirs * rows[0],
            totals[3] + theirs * rows[1],
        )

    zeros = jnp.zeros((kept, columns), jnp.float32)
    totals = lax.fori_loop(0, channels, add_channel, (zeros,) * 4, unroll=8)
    upper = lax.axis_index("lon") == 0
    mixed = [
        [jnp.where(upper, totals[part], totals[2 + part]) for part in range(2)],
        [jnp.where(upper, totals[2 + part], totals[part]) for part in range(2)],
    ]
    lane = lax.broadcasted_iota(jnp.int32, (kept, columns), 1)
    blocks = []
    for side in range(2):
        for m in range(per_device):
            own = (lane >= m * degrees) & (lane < (m + 1) * degrees)
            for part in range(2):
                blocks.append(jnp.where(own, mixed[side][part], 0.0).astype(jnp.bfloat16))
    values = lax.dot_general(
        synthesis_ref[...],
        jnp.concatenate(blocks, axis=0),
        (((1,), (1,)), ((), ())),
        preferred_element_type=jnp.float32,
    )
    for side in range(2):
        for group in range(groups):
            for part in range(parts):
                start = (side * parts + part) * kept
                pieces = [
                    values[(group * packed + i) * bands : (group * packed + i + 1) * bands, start : start + kept]
                    for i in range(packed)
                ]
                place = (side * groups + group) * parts + part
                chunk_ref[pl.ds(place, bands, stride=2 * groups * parts), :] = jnp.concatenate(
                    pieces, axis=1
                )
    out_ref[...] = chunk_ref[...].astype(jnp.bfloat16).reshape(out_ref.shape)


def inverse_kernel(per_device, pieces_ref, dft_ref, out_ref, pieces_32_ref, rows_ref):
    owners, chunk_rows, width = pieces_ref.shape
    kept, row_count, lon_total = out_ref.shape
    packed = width // kept
    parts = 2 * per_device
    pieces_32_ref[...] = pieces_ref[...].astype(jnp.float32).reshape(owners * chunk_rows, width)
    dft = dft_ref[...]
    place = lax.broadcasted_iota(jnp.int32, (2 * owners * per_device, width), 0)
    factor = jnp.where((place == 0) | (place == owners * per_device), 1.0, 2.0)
    for group in range(chunk_rows // parts):
        found = [
            pieces_32_ref[pl.ds(group * parts + 2 * m + part, owners, stride=chunk_rows), :]
            for part in range(2)
            for m in range(per_device)
        ]
        found = (jnp.concatenate(found, axis=0) * factor).astype(jnp.bfloat16)
        values = lax.dot_general(
            found, dft, (((0,), (0,)), ((), ())), preferred_element_type=jnp.float32
        )
        for i in range(packed):
            for tile in range(lon_total // LANES):
                rows_ref[tile, pl.ds(group * packed + i, kept, stride=row_count), :] = values[
                    i * kept : (i + 1) * kept, tile * LANES : (tile + 1) * LANES
                ]
    for tile in range(lon_total // LANES):
        out_ref[:, :, tile * LANES : (tile + 1) * LANES] = (
            rows_ref[tile].astype(jnp.bfloat16).reshape(kept, row_count, LANES)
        )


def local(fields, conv_first, conv_second, mixing):
    lat_count = lax.axis_size("lat")
    lon_count = lax.axis_size("lon")
    channels, row_count, lon_part = fields.shape
    lat_total = row_count * lat_count
    lon_total = lon_part * lon_count
    orders = lat_total // 2
    degrees = mixing.shape[0]
    owners = lat_count * lon_count
    per_device = orders // owners
    half = row_count // 2
    kept = channels // 2
    swap = [(0, 1), (1, 0)]
    both = ("lat", "lon")
    bfloat = functools.partial(jax.ShapeDtypeStruct, dtype=jnp.bfloat16)

    other = lax.ppermute(fields, "lon", swap)
    unpacked = pltpu.VMEM((lon_part // LANES, channels * row_count, LANES), jnp.float32)
    columns = per_device * degrees
    span = 32 if degrees % 32 == 0 else degrees
    width = lat_total * per_device
    arguments = [
        pltpu.with_memory_space_constraint(value, pltpu.HBM)
        for value in (
            fields,
            jnp.transpose(conv_first, (2, 3, 0, 1)),
            jnp.transpose(conv_second, (2, 3, 0, 1)),
        )
    ]
    own, taps_first, taps_second = call(
        load_kernel,
        (
            bfloat((row_count, channels, lon_part)),
            bfloat(arguments[1].shape),
            bfloat(arguments[2].shape),
        ),
        [pltpu.VMEM(fields.shape, jnp.bfloat16), unpacked, pltpu.SemaphoreType.DMA((3,))],
        [HBM] * 3,
        pl.CostEstimate(flops=1 << 16, bytes_accessed=1 << 21, transcendentals=0),
    )(*arguments)
    own, other, late_mixing = lax.optimization_barrier((own, other, mixing))
    other_mixing = lax.ppermute(late_mixing, "lon", swap)
    message = call(
        message_kernel,
        bfloat((2, channels, lon_total)),
        [unpacked],
        [VMEM, VMEM],
        pl.CostEstimate(flops=1 << 16, bytes_accessed=1 << 18, transcendentals=0),
    )(own, other)
    pairs = []
    for i in range(lat_count - 1):
        lower, upper = 2 * i + i % 2, 2 * (i + 1) + i % 2
        pairs += [(lower, upper), (upper, lower)]
    halo = lax.ppermute(message, both, pairs)

    taps = (3 * channels, 3 * channels)
    first, second, dft, near, interior = call(
        functools.partial(interior_kernel, lat_total, owners),
        (
            bfloat(taps),
            bfloat(taps),
            bfloat((2 * orders, lon_total)),
            bfloat((2, channels, lon_total)),
            jax.ShapeDtypeStruct((half - 2, orders, 2 * channels), jnp.float32),
        ),
        [
            unpacked,
            pltpu.VMEM((half + 2, channels, lon_total), jnp.bfloat16),
            pltpu.VMEM((half, channels, lon_total), jnp.bfloat16),
            pltpu.VMEM((half - 2, channels, lon_total), jnp.bfloat16),
        ],
        [VMEM, VMEM, VMEM, VMEM, ANY],
        pl.CostEstimate(flops=1 << 28, bytes_accessed=1 << 22, transcendentals=0),
    )(
        own,
        other,
        taps_first,
        taps_second,
        message,
    )

    def mixing_table(values, after):
        return call(
            functools.partial(mixing_kernel, per_device),
            bfloat((channels, kept, columns)),
            [],
            [VMEM, ANY],
            pl.CostEstimate(flops=1 << 20, bytes_accessed=1 << 22, transcendentals=0),
        )(values, after)

    mine = mixing_table(mixing, near)
    theirs = mixing_table(other_mixing, near)
    analysis, synthesis = call(
        functools.partial(legendre_kernel, span, lat_count, row_count, per_device),
        (bfloat((columns, width)), bfloat((lat_total, columns))),
        [pltpu.VMEM((width // LANES, 2 * degrees, LANES), jnp.float32)],
        [ANY],
        pl.CostEstimate(flops=1 << 20, bytes_accessed=1 << 21, transcendentals=0),
    )(near)
    coeffs = call(
        functools.partial(edge_kernel, lat_total, half),
        bfloat((owners, per_device * half, 2 * channels)),
        [
            pltpu.VMEM((4, channels, lon_total), jnp.bfloat16),
            pltpu.VMEM((4, channels, lon_total), jnp.bfloat16),
            pltpu.VMEM((2, channels, lon_total), jnp.bfloat16),
            pltpu.VMEM((orders * half, 2 * channels), jnp.float32),
        ],
        [VMEM] * 7 + [ANY] * 3,
        pl.CostEstimate(flops=1 << 26, bytes_accessed=1 << 20, transcendentals=0),
    )(halo, message, near, first, second, dft, interior, mine, theirs, analysis)
    pieces = lax.all_to_all(coeffs, both, split_axis=0, concat_axis=0, tiled=True)

    chunk_rows = row_count * 2 * per_device * kept // LANES
    chunks = call(
        functools.partial(spectral_kernel, per_device),
        bfloat((owners, chunk_rows, LANES)),
        [
            pltpu.VMEM((2 * channels, columns), jnp.float32),
            pltpu.VMEM((owners * chunk_rows, LANES), jnp.float32),
        ],
        [VMEM] * 5,
        pl.CostEstimate(flops=1 << 24, bytes_accessed=1 << 20, transcendentals=0),
    )(pieces, analysis, synthesis, mine, theirs)

    back = lax.all_to_all(chunks, both, split_axis=0, concat_axis=0, tiled=True)
    return call(
        functools.partial(inverse_kernel, per_device),
        bfloat((kept, row_count, lon_total)),
        [
            pltpu.VMEM((owners * chunk_rows, LANES), jnp.float32),
            pltpu.VMEM((lon_total // LANES, kept * row_count, LANES), jnp.float32),
        ],
        [VMEM] * 2,
        pl.CostEstimate(flops=1 << 24, bytes_accessed=1 << 19, transcendentals=0),
    )(back, dft)


def solution(mesh):
    in_specs = (P("groups", "lat", "lon"), P(), P(), P(None, "lon", None))
    out_specs = P(("groups", "lon"), "lat", None)
    return jax.shard_map(local, mesh=mesh, in_specs=in_specs, out_specs=out_specs, check_vma=False)
```

time: 36.8 us -> 34.5 us (0.938)
  blocking collectives: 0 us -> 22 us
  waiting for transfers between devices: 11.3 us -> 0.13 us
  starting transfers between devices: 13.9 us -> 5.36 us
  Pallas kernels: 10.2 us -> 6.75 us
  local copies, waits for them, and re-layouts: 0.92 us -> 0.01 us
    all_to_all x0 -> x2, blocking collectives: none -> 22 us  [the longest x1 12.9 us: local(): lax.all_to_all(coeffs, both, split_axis=0, concat_axis=0, tiled=True)]
    all_to_all x2 -> x0, starting transfers between devices: 12.6 us -> none  [the longest x1 10 us: local(): lax.all_to_all(coeffs, both, split_axis=0, concat_axis=0, tiled=True)]
    all_to_all x2 -> x0, waiting for transfers between devices: 11.2 us -> none  [the longest x1 6.26 us: local(): back = lax.all_to_all(chunks, both, split_axis=0, concat_axis=0, tiled=True)]
    ppermute x1, starting transfers between devices: 0.8 us -> 4.54 us  [local(): halo = lax.ppermute(message, both, pairs)]
    pallas_call x2, Pallas kernels: 2.98 us -> 1.37 us  [mixing_table(): call(functools.partial(mixing_kernel, per_device), bfloat((channels, kept...]
    unnamed x8 -> x2, local copies, waits for them, and re-layouts: 0.92 us -> 0.01 us
    pallas_call x1, Pallas kernels: 1.48 us -> 0.85 us  [local(): call(functools.partial(edge_kernel, lat_total, half), bfloat((owners, per...]
    pallas_call x1, Pallas kernels: 1.59 us -> 0.96 us  [local(): call(functools.partial(spectral_kernel, per_device), bfloat((owners, chun...]
  transfers between devices with their start and end apart: 5 -> 3, of which waited for: 3 -> 1; matrix products, arithmetic and copies ran while one was open for 0% -> 0% of each run, Pallas kernels for 21% -> 12%
where the time goes in v4:
time: 34.5 us; the launch traced here: 34.3 us
  blocking collectives  22 us (64%)
  Pallas kernels  6.75 us (20%)
  starting transfers between devices  5.36 us (16%)
    all_to_all x1, blocking collectives, local(): lax.all_to_all(coeffs, both, split_axis=0, concat_axis=0, tiled=True)  12.9 us
    all_to_all x1, blocking collectives, local(): back = lax.all_to_all(chunks, both, split_axis=0, concat_axis=0, tiled=True)  9.1 us
    ppermute x1, starting transfers between devices, local(): halo = lax.ppermute(message, both, pairs)  4.54 us
    pallas_call x2, Pallas kernels, mixing_table(): call(functools.partial(mixing_kernel, per_device), bfloat((channels, kept...  1.37 us
    pallas_call x1, Pallas kernels, local(): call(functools.partial(interior_kernel, lat_total, owners), (bfloat(taps)...  1.08 us
    pallas_call x1, Pallas kernels, local(): call(load_kernel, (bfloat((row_count, channels, lon_part)), bfloat(argume...  1.07 us
    pallas_call x1, Pallas kernels, local(): call(functools.partial(spectral_kernel, per_device), bfloat((owners, chun...  0.96 us
    pallas_call x1, Pallas kernels, local(): call(functools.partial(inverse_kernel, per_device), bfloat((kept, row_cou...  0.91 us
  transfers between devices with their start and end apart: 3, of which 1 were waited for; matrix products, arithmetic and copies ran while one was open for 0% of the time, Pallas kernels for 12%

profile of v4, /device:TPU:0, one launch (start us, length us, event | category | flops | bytes accessed | tf_op | source)
XLA Modules:
  0.0 34.3 jit_solution(2717429324823097680)
XLA Ops:
  0.0 0.5 %collective-permute-start = (bf16[64,8,128]{2,1,0:T(8,128)(2,1)}, bf16[64,8,128]{2,1,0:T(8,128)(2,1)S(1)}, u32[]{:S(2)}, u32[]{:S(2)}) collective-permute-start(bf16[64,8,128]{2,1,0:T(8,128)(2,1)} %fields_ref.1), channel_id=1, source_target_pairs={{0,1},{1,0},{2,3},{3,2},{4,5},{5,4},{6,7},{7,6},{8,9},{9,8},{10,11... | collective-permute-start | bytes 393224 | tf_op jit(solution)/shard_map/ppermute | solution.py:439
  0.5 1.1 %shard_map.46 = (bf16[8,64,128]{2,1,0:T(8,128)(2,1)S(1)}, bf16[3,3,64,64]{3,2,1,0:T(8,128)(2,1)S(1)}, bf16[3,3,64,64]{3,2,1,0:T(8,128)(2,1)S(1)}) custom-call(bf16[64,8,128]{2,1,0:T(8,128)(2,1)} %fields_ref.1, bf16[3,3,64,64]{3,2,1,0:T(8,128)(2,1)} %bitcast.2, bf16[3,3,64,64]{3,2,1,0:T(8,128)(2,1)} %bitcast.3), custom_call_target="tpu_custom_call" | custom-call | flops 65536 | bytes 2097152 | tf_op jit(solution)/shard_map/pallas_call | solution.py:452
  1.5 0.1 collective-permute-done.other_ref
  1.7 0.4 %collective-permute-start.2 = (bf16[64,32,64]{2,1,0:T(8,128)(2,1)}, bf16[64,32,64]{2,1,0:T(8,128)(2,1)S(1)}, u32[]{:S(2)}, u32[]{:S(2)}) collective-permute-start(bf16[64,32,64]{2,1,0:T(8,128)(2,1)} %mixing_ref.1), channel_id=1, source_target_pairs={{0,1},{1,0},{2,3},{3,2},{4,5},{5,4},{6,7},{7,6},{8,9},{9,8},{10,11... | collective-permute-start | bytes 786440 | tf_op jit(solution)/shard_map/ppermute | solution.py:464
  2.1 4.5 %collective-permute-start.1 = (bf16[2,64,256]{2,1,0:T(8,128)(2,1)S(1)}, bf16[2,64,256]{2,1,0:T(8,128)(2,1)S(1)}, u32[]{:S(2)}, u32[]{:S(2)}) collective-permute-start(bf16[2,64,256]{2,1,0:T(8,128)(2,1)S(1)} %shard_map.47.after_ref.message_ref), channel_id=1, source_target_pairs={{0,2},{2,0},{3,5},{5,3},{4,6},{6,4},{7,9},{9,7},{8,10},{10,8},{11,... | collective-permute-start | bytes 196616 | tf_op jit(solution)/shard_map/ppermute | solution.py:476
  6.6 0.0 copy-start
  6.6 1.1 %shard_map.48 = (bf16[192,192]{1,0:T(8,128)(2,1)S(1)}, bf16[192,192]{1,0:T(8,128)(2,1)S(1)}, bf16[128,256]{1,0:T(8,128)(2,1)S(1)}, bf16[2,64,256]{2,1,0:T(8,128)(2,1)S(1)}, f32[2,64,128]{2,1,0:T(8,128)S(1)}) custom-call(bf16[8,64,128]{2,1,0:T(8,128)(2,1)S(1)} %get-tuple-element.19.own_ref, bf16[64,8,128]{2,1,0:T(8,128)(2,1)S(1)} %collective-permute-done.other_ref, ...), custom_call_target="tpu_custom_call" | custom-call | flops 268435456 | bytes 4194304 | tf_op jit(solution)/shard_map/pallas_call | solution.py:479
  7.7 0.5 %shard_map.51 = (bf16[128,256]{1,0:T(8,128)(2,1)S(1)}, bf16[128,128]{1,0:T(8,128)(2,1)S(1)}) custom-call(bf16[2,64,256]{2,1,0:T(8,128)(2,1)S(1)} %get-tuple-element.23.after_ref.near_ref), custom_call_target="tpu_custom_call" | custom-call | flops 1048576 | bytes 2097152 | tf_op jit(solution)/shard_map/pallas_call | solution.py:515
  8.2 0.0 copy-done
  8.2 0.7 %shard_map.49.mine_ref = bf16[64,32,128]{2,1,0:T(8,128)(2,1)S(1)} custom-call(bf16[64,32,64]{2,1,0:T(8,128)(2,1)S(1)} %copy-done, bf16[2,64,256]{2,1,0:T(8,128)(2,1)S(1)} %get-tuple-element.23.after_ref.near_ref), custom_call_target="tpu_custom_call" | custom-call | flops 1048576 | bytes 4194304 | tf_op jit(solution)/shard_map/pallas_call | solution.py:505
  8.9 0.0 collective-permute-done.2.mixing_ref
  8.9 0.7 %shard_map.50.theirs_ref = bf16[64,32,128]{2,1,0:T(8,128)(2,1)S(1)} custom-call(bf16[64,32,64]{2,1,0:T(8,128)(2,1)S(1)} %collective-permute-done.2.mixing_ref, bf16[2,64,256]{2,1,0:T(8,128)(2,1)S(1)} %get-tuple-element.23.after_ref.near_ref), custom_call_target="tpu_custom_call" | custom-call | flops 1048576 | bytes 4194304 | tf_op jit(solution)/shard_map/pallas_call | solution.py:505
  9.6 0.0 collective-permute-done.1.halo_ref
  9.6 0.8 %shard_map.52 = bf16[32,8,128]{2,1,0:T(8,128)(2,1)S(1)} custom-call(bf16[2,64,256]{2,1,0:T(8,128)(2,1)S(1)} %collective-permute-done.1.halo_ref, bf16[2,64,256]{2,1,0:T(8,128)(2,1)S(1)} %shard_map.47.after_ref.message_ref, bf16[2,64,256]{2,1,0:T(8,128)(2,1)S(1)} %get-tuple-element.23.after_ref.near_ref, bf16[192,192]{1,0:T(8,128)(2,1)S(1)} %get-tuple-element.24.first_ref, ...), custom_call_target="tpu_custom_call" | custom-call | flops 67108864 | bytes 1048576 | tf_op jit(solution)/shard_map/pallas_call | solution.py:522
  10.4 12.9 %all_to_all.10.pieces_ref = bf16[32,8,128]{2,1,0:T(8,128)(2,1)S(1)} all-to-all(bf16[32,8,128]{2,1,0:T(8,128)(2,1)S(1)} %shard_map.52), channel_id=1, replica_groups=mesh['groups'=1,'lat'=16,'lon'=2] {'lat','lon'}, dimensions={0} | all-to-all | bytes 131072 | tf_op jit(solution)/shard_map/all_to_all | solution.py:534
  23.3 1.0 %shard_map.53 = bf16[32,8,128]{2,1,0:T(8,128)(2,1)S(1)} custom-call(bf16[32,8,128]{2,1,0:T(8,128)(2,1)S(1)} %all_to_all.10.pieces_ref, bf16[128,256]{1,0:T(8,128)(2,1)S(1)} %get-tuple-element.29.analysis_ref, bf16[128,128]{1,0:T(8,128)(2,1)S(1)} %get-tuple-element.30.synthesis_ref, bf16[64,32,128]{2,1,0:T(8,128)(2,1)S(1)} %shard_map.49.mine_ref, ...), custom_call_target="tpu_custom_call" | custom-call | flops 16777216 | bytes 1048576 | tf_op jit(solution)/shard_map/pallas_call | solution.py:537
  24.3 9.1 %all_to_all.11.pieces_ref = bf16[32,8,128]{2,1,0:T(8,128)(2,1)S(1)} all-to-all(bf16[32,8,128]{2,1,0:T(8,128)(2,1)S(1)} %shard_map.53), channel_id=1, replica_groups=mesh['groups'=1,'lat'=16,'lon'=2] {'lat','lon'}, dimensions={0} | all-to-all | bytes 131072 | tf_op jit(solution)/shard_map/all_to_all | solution.py:548
  33.4 0.9 %shard_map.54 = bf16[32,8,256]{2,1,0:T(8,128)(2,1)} custom-call(bf16[32,8,128]{2,1,0:T(8,128)(2,1)S(1)} %all_to_all.11.pieces_ref, bf16[128,256]{1,0:T(8,128)(2,1)S(1)} %get-tuple-element.26.dft_ref), custom_call_target="tpu_custom_call" | custom-call | flops 16777216 | bytes 524288 | tf_op jit(solution)/shard_map/pallas_call | solution.py:549
  (1 shorter events, 0.0 us)
Async XLA Ops:
  0.0 1.6 %collective-permute-start = (bf16[64,8,128]{2,1,0:T(8,128)(2,1)}, bf16[64,8,128]{2,1,0:T(8,128)(2,1)S(1)}, u32[]{:S(2)}, u32[]{:S(2)}) collective-permute-start(bf16[64,8,128]{2,1,0:T(8,128)(2,1)} %fields_ref.1), channel_id=1, source_target_pairs={{0,1},{1,0},{2,3},{3,2},{4,5},{5,4},{6,7},{7,6},{8,9},{9,8},{10,11... | collective-permute-start | bytes 393224 | tf_op jit(solution)/shard_map/ppermute | solution.py:439
  1.7 7.2 %collective-permute-start.2 = (bf16[64,32,64]{2,1,0:T(8,128)(2,1)}, bf16[64,32,64]{2,1,0:T(8,128)(2,1)S(1)}, u32[]{:S(2)}, u32[]{:S(2)}) collective-permute-start(bf16[64,32,64]{2,1,0:T(8,128)(2,1)} %mixing_ref.1), channel_id=1, source_target_pairs={{0,1},{1,0},{2,3},{3,2},{4,5},{5,4},{6,7},{7,6},{8,9},{9,8},{10,11... | collective-permute-start | bytes 786440 | tf_op jit(solution)/shard_map/ppermute | solution.py:464
  2.1 7.5 %collective-permute-start.1 = (bf16[2,64,256]{2,1,0:T(8,128)(2,1)S(1)}, bf16[2,64,256]{2,1,0:T(8,128)(2,1)S(1)}, u32[]{:S(2)}, u32[]{:S(2)}) collective-permute-start(bf16[2,64,256]{2,1,0:T(8,128)(2,1)S(1)} %shard_map.47.after_ref.message_ref), channel_id=1, source_target_pairs={{0,2},{2,0},{3,5},{5,3},{4,6},{6,4},{7,9},{9,7},{8,10},{10,8},{11,... | collective-permute-start | bytes 196616 | tf_op jit(solution)/shard_map/ppermute | solution.py:476
  6.6 1.6 %copy-start = (bf16[64,32,64]{2,1,0:T(8,128)(2,1)S(1)}, bf16[64,32,64]{2,1,0:T(8,128)(2,1)}, u32[]{:S(2)}) copy-start(bf16[64,32,64]{2,1,0:T(8,128)(2,1)} %mixing_ref.1) | copy-start | bytes 786436

commit v5 on v4

--- a/solution.py
+++ b/solution.py
@@ -199,7 +199,6 @@
     dft_ref,
     coeffs_ref,
     mine_ref,
-    theirs_ref,
     analysis_ref,
     out_ref,
     band_ref,
@@ -207,7 +206,7 @@
     hidden_ref,
     packed_ref,
 ):
-    del mine_ref, theirs_ref, analysis_ref
+    del mine_ref, analysis_ref
     part = row_half()
     first_row = lax.axis_index("lat") * (2 * half) + part * half
     band_ref[pl.ds(2 * part, 2)] = halo_ref[...]
@@ -460,8 +459,6 @@
         [HBM] * 3,
         pl.CostEstimate(flops=1 << 16, bytes_accessed=1 << 21, transcendentals=0),
     )(*arguments)
-    own, other, late_mixing = lax.optimization_barrier((own, other, mixing))
-    other_mixing = lax.ppermute(late_mixing, "lon", swap)
     message = call(
         message_kernel,
         bfloat((2, channels, lon_total)),
@@ -511,7 +508,6 @@
         )(values, after)
 
     mine = mixing_table(mixing, near)
-    theirs = mixing_table(other_mixing, near)
     analysis, synthesis = call(
         functools.partial(legendre_kernel, span, lat_count, row_count, per_device),
         (bfloat((columns, width)), bfloat((lat_total, columns))),
@@ -528,9 +524,11 @@
             pltpu.VMEM((2, channels, lon_total), jnp.bfloat16),
             pltpu.VMEM((orders * half, 2 * channels), jnp.float32),
         ],
-        [VMEM] * 7 + [ANY] * 3,
+        [VMEM] * 7 + [ANY] * 2,
         pl.CostEstimate(flops=1 << 26, bytes_accessed=1 << 20, transcendentals=0),
-    )(halo, message, near, first, second, dft, interior, mine, theirs, analysis)
+    )(halo, message, near, first, second, dft, interior, mine, analysis)
+    coeffs, late_mine = lax.optimization_barrier((coeffs, mine))
+    theirs = lax.ppermute(late_mine, "lon", swap)
     pieces = lax.all_to_all(coeffs, both, split_axis=0, concat_axis=0, tiled=True)
 
     chunk_rows = row_count * 2 * per_device * kept // LANES

time: 34.5 us -> 34.5 us (level)
  blocking collectives: 22 us -> 22.7 us
  Pallas kernels: 6.75 us -> 6.06 us
    all_to_all x1, blocking collectives: 12.9 us -> 13.6 us  [local(): lax.all_to_all(coeffs, both, split_axis=0, concat_axis=0, tiled=True)]
    pallas_call x2 -> x1, Pallas kernels: 1.37 us -> 0.68 us  [mixing_table(): call(functools.partial(mixing_kernel, per_device), bfloat((channels, kept...]
  transfers between devices with their start and end apart: 3 -> 3, of which waited for: 1 -> 1; matrix products, arithmetic and copies ran while one was open for 0% -> 0% of each run, Pallas kernels for 12% -> 10%
where the time goes in v5:
time: 34.5 us; the launch traced here: 34.3 us
  blocking collectives  22.7 us (66%)
  Pallas kernels  6.06 us (18%)
  starting transfers between devices  5.28 us (15%)
    all_to_all x1, blocking collectives, local(): lax.all_to_all(coeffs, both, split_axis=0, concat_axis=0, tiled=True)  13.6 us
    all_to_all x1, blocking collectives, local(): back = lax.all_to_all(chunks, both, split_axis=0, concat_axis=0, tiled=True)  9.1 us
    ppermute x1, starting transfers between devices, local(): halo = lax.ppermute(message, both, pairs)  4.76 us
    pallas_call x1, Pallas kernels, local(): call(functools.partial(interior_kernel, lat_total, owners), (bfloat(taps)...  1.08 us
    pallas_call x1, Pallas kernels, local(): call(load_kernel, (bfloat((row_count, channels, lon_part)), bfloat(argume...  1.07 us
    pallas_call x1, Pallas kernels, local(): call(functools.partial(spectral_kernel, per_device), bfloat((owners, chun...  0.96 us
    pallas_call x1, Pallas kernels, local(): call(functools.partial(inverse_kernel, per_device), bfloat((kept, row_cou...  0.91 us
    pallas_call x1, Pallas kernels, local(): call(functools.partial(edge_kernel, lat_total, half), bfloat((owners, per...  0.84 us
  transfers between devices with their start and end apart: 3, of which 1 were waited for; matrix products, arithmetic and copies ran while one was open for 0% of the time, Pallas kernels for 10%

profile of v5, /device:TPU:0, one launch (start us, length us, event | category | flops | bytes accessed | tf_op | source)
XLA Modules:
  0.0 34.3 jit_solution(2727678568987072797)
XLA Ops:
  0.0 0.5 %collective-permute-start = (bf16[64,8,128]{2,1,0:T(8,128)(2,1)}, bf16[64,8,128]{2,1,0:T(8,128)(2,1)S(1)}, u32[]{:S(2)}, u32[]{:S(2)}) collective-permute-start(bf16[64,8,128]{2,1,0:T(8,128)(2,1)} %fields_ref.1), channel_id=1, source_target_pairs={{0,1},{1,0},{2,3},{3,2},{4,5},{5,4},{6,7},{7,6},{8,9},{9,8},{10,11... | collective-permute-start | bytes 393224 | tf_op jit(solution)/shard_map/ppermute | solution.py:438
  0.5 1.1 %shard_map.46 = (bf16[8,64,128]{2,1,0:T(8,128)(2,1)S(1)}, bf16[3,3,64,64]{3,2,1,0:T(8,128)(2,1)S(1)}, bf16[3,3,64,64]{3,2,1,0:T(8,128)(2,1)S(1)}) custom-call(bf16[64,8,128]{2,1,0:T(8,128)(2,1)} %fields_ref.1, bf16[3,3,64,64]{3,2,1,0:T(8,128)(2,1)} %bitcast.2, bf16[3,3,64,64]{3,2,1,0:T(8,128)(2,1)} %bitcast.3), custom_call_target="tpu_custom_call" | custom-call | flops 65536 | bytes 2097152 | tf_op jit(solution)/shard_map/pallas_call | solution.py:451
  1.5 0.1 collective-permute-done.other_ref
  1.7 4.8 %collective-permute-start.1 = (bf16[2,64,256]{2,1,0:T(8,128)(2,1)S(1)}, bf16[2,64,256]{2,1,0:T(8,128)(2,1)S(1)}, u32[]{:S(2)}, u32[]{:S(2)}) collective-permute-start(bf16[2,64,256]{2,1,0:T(8,128)(2,1)S(1)} %shard_map.47.after_ref.message_ref), channel_id=1, source_target_pairs={{0,2},{2,0},{3,5},{5,3},{4,6},{6,4},{7,9},{9,7},{8,10},{10,8},{11,... | collective-permute-start | bytes 196616 | tf_op jit(solution)/shard_map/ppermute | solution.py:473
  6.5 0.0 copy-start
  6.5 1.1 %shard_map.48 = (bf16[192,192]{1,0:T(8,128)(2,1)S(1)}, bf16[192,192]{1,0:T(8,128)(2,1)S(1)}, bf16[128,256]{1,0:T(8,128)(2,1)S(1)}, bf16[2,64,256]{2,1,0:T(8,128)(2,1)S(1)}, f32[2,64,128]{2,1,0:T(8,128)S(1)}) custom-call(bf16[8,64,128]{2,1,0:T(8,128)(2,1)S(1)} %get-tuple-element.17.own_ref, bf16[64,8,128]{2,1,0:T(8,128)(2,1)S(1)} %collective-permute-done.other_ref, ...), custom_call_target="tpu_custom_call" | custom-call | flops 268435456 | bytes 4194304 | tf_op jit(solution)/shard_map/pallas_call | solution.py:476
  7.5 0.5 %shard_map.50 = (bf16[128,256]{1,0:T(8,128)(2,1)S(1)}, bf16[128,128]{1,0:T(8,128)(2,1)S(1)}) custom-call(bf16[2,64,256]{2,1,0:T(8,128)(2,1)S(1)} %get-tuple-element.20.after_ref.near_ref), custom_call_target="tpu_custom_call" | custom-call | flops 1048576 | bytes 2097152 | tf_op jit(solution)/shard_map/pallas_call | solution.py:511
  8.0 0.0 copy-done
  8.0 0.7 %shard_map.49.mine_ref = bf16[64,32,128]{2,1,0:T(8,128)(2,1)S(1)} custom-call(bf16[64,32,64]{2,1,0:T(8,128)(2,1)S(1)} %copy-done, bf16[2,64,256]{2,1,0:T(8,128)(2,1)S(1)} %get-tuple-element.20.after_ref.near_ref), custom_call_target="tpu_custom_call" | custom-call | flops 1048576 | bytes 4194304 | tf_op jit(solution)/shard_map/pallas_call | solution.py:502
  8.7 0.0 collective-permute-done.1.halo_ref
  8.8 0.8 %shard_map.51 = bf16[32,8,128]{2,1,0:T(8,128)(2,1)S(1)} custom-call(bf16[2,64,256]{2,1,0:T(8,128)(2,1)S(1)} %collective-permute-done.1.halo_ref, bf16[2,64,256]{2,1,0:T(8,128)(2,1)S(1)} %shard_map.47.after_ref.message_ref, bf16[2,64,256]{2,1,0:T(8,128)(2,1)S(1)} %get-tuple-element.20.after_ref.near_ref, bf16[192,192]{1,0:T(8,128)(2,1)S(1)} %get-tuple-element.21.first_ref, ...), custom_call_target="tpu_custom_call" | custom-call | flops 67108864 | bytes 1048576 | tf_op jit(solution)/shard_map/pallas_call | solution.py:518
  9.6 0.1 collective-permute-start.2
  9.7 13.6 %all_to_all.10.pieces_ref = bf16[32,8,128]{2,1,0:T(8,128)(2,1)S(1)} all-to-all(bf16[32,8,128]{2,1,0:T(8,128)(2,1)S(1)} %shard_map.51), channel_id=1, replica_groups=mesh['groups'=1,'lat'=16,'lon'=2] {'lat','lon'}, dimensions={0} | all-to-all | bytes 131072 | tf_op jit(solution)/shard_map/all_to_all | solution.py:532
  23.3 0.0 collective-permute-done.2.theirs_ref
  23.3 1.0 %shard_map.52 = bf16[32,8,128]{2,1,0:T(8,128)(2,1)S(1)} custom-call(bf16[32,8,128]{2,1,0:T(8,128)(2,1)S(1)} %all_to_all.10.pieces_ref, bf16[128,256]{1,0:T(8,128)(2,1)S(1)} %get-tuple-element.25.analysis_ref, bf16[128,128]{1,0:T(8,128)(2,1)S(1)} %get-tuple-element.27.synthesis_ref, bf16[64,32,128]{2,1,0:T(8,128)(2,1)S(1)} %shard_map.49.mine_ref, ...), custom_call_target="tpu_custom_call" | custom-call | flops 16777216 | bytes 1048576 | tf_op jit(solution)/shard_map/pallas_call | solution.py:535
  24.3 9.1 %all_to_all.11.pieces_ref = bf16[32,8,128]{2,1,0:T(8,128)(2,1)S(1)} all-to-all(bf16[32,8,128]{2,1,0:T(8,128)(2,1)S(1)} %shard_map.52), channel_id=1, replica_groups=mesh['groups'=1,'lat'=16,'lon'=2] {'lat','lon'}, dimensions={0} | all-to-all | bytes 131072 | tf_op jit(solution)/shard_map/all_to_all | solution.py:546
  33.4 0.9 %shard_map.53 = bf16[32,8,256]{2,1,0:T(8,128)(2,1)} custom-call(bf16[32,8,128]{2,1,0:T(8,128)(2,1)S(1)} %all_to_all.11.pieces_ref, bf16[128,256]{1,0:T(8,128)(2,1)S(1)} %get-tuple-element.23.dft_ref), custom_call_target="tpu_custom_call" | custom-call | flops 16777216 | bytes 524288 | tf_op jit(solution)/shard_map/pallas_call | solution.py:547
  (1 shorter events, 0.0 us)
Async XLA Ops:
  0.0 1.6 %collective-permute-start = (bf16[64,8,128]{2,1,0:T(8,128)(2,1)}, bf16[64,8,128]{2,1,0:T(8,128)(2,1)S(1)}, u32[]{:S(2)}, u32[]{:S(2)}) collective-permute-start(bf16[64,8,128]{2,1,0:T(8,128)(2,1)} %fields_ref.1), channel_id=1, source_target_pairs={{0,1},{1,0},{2,3},{3,2},{4,5},{5,4},{6,7},{7,6},{8,9},{9,8},{10,11... | collective-permute-start | bytes 393224 | tf_op jit(solution)/shard_map/ppermute | solution.py:438
  1.7 7.1 %collective-permute-start.1 = (bf16[2,64,256]{2,1,0:T(8,128)(2,1)S(1)}, bf16[2,64,256]{2,1,0:T(8,128)(2,1)S(1)}, u32[]{:S(2)}, u32[]{:S(2)}) collective-permute-start(bf16[2,64,256]{2,1,0:T(8,128)(2,1)S(1)} %shard_map.47.after_ref.message_ref), channel_id=1, source_target_pairs={{0,2},{2,0},{3,5},{5,3},{4,6},{6,4},{7,9},{9,7},{8,10},{10,8},{11,... | collective-permute-start | bytes 196616 | tf_op jit(solution)/shard_map/ppermute | solution.py:473
  6.5 1.6 %copy-start = (bf16[64,32,64]{2,1,0:T(8,128)(2,1)S(1)}, bf16[64,32,64]{2,1,0:T(8,128)(2,1)}, u32[]{:S(2)}) copy-start(bf16[64,32,64]{2,1,0:T(8,128)(2,1)} %mixing_ref.1) | copy-start | bytes 786436
  9.6 13.7 %collective-permute-start.2 = (bf16[64,32,128]{2,1,0:T(8,128)(2,1)S(1)}, bf16[64,32,128]{2,1,0:T(8,128)(2,1)S(1)}, u32[]{:S(2)}, u32[]{:S(2)}) collective-permute-start(bf16[64,32,128]{2,1,0:T(8,128)(2,1)S(1)} %shard_map.49.mine_ref), channel_id=1, source_target_pairs={{0,1},{1,0},{2,3},{3,2},{4,5},{5,4},{6,7},{7,6},{8,9},{9,8},{10,11... | collective-permute-start | bytes 1572872 | tf_op jit(solution)/shard_map/ppermute | solution.py:531

commit v6 on v5

--- a/solution.py
+++ b/solution.py
@@ -241,7 +241,7 @@
     blocks = [
         jnp.concatenate([values[o]] * per_device, axis=0).T for o in range(values.shape[0])
     ]
-    out_ref[...] = jnp.transpose(jnp.stack(blocks), (1, 0, 2)).astype(jnp.bfloat16)
+    out_ref[...] = jnp.transpose(jnp.stack(blocks), (1, 0, 2))
 
 
 def legendre_kernel(
@@ -340,13 +340,14 @@
     bands = synthesis_ref.shape[0] // (groups * packed)
 
     pieces = pieces_ref[...].reshape(owners * chunk_rows, width)
-    spectral = jnp.dot(analysis_ref[...], pieces, preferred_element_type=jnp.float32)
-    spectral_ref[...] = spectral.T.astype(jnp.bfloat16).astype(jnp.float32)
+    spectral = lax.dot_general(
+        pieces, analysis_ref[...], (((0,), (1,)), ((), ())), preferred_element_type=jnp.float32
+    )
+    spectral_ref[...] = spectral.astype(jnp.bfloat16).astype(jnp.float32)
 
     def add_channel(channel, totals):
         rows = [spectral_ref[pl.ds(part * channels + channel, 1), :] for part in range(2)]
-        mine = mine_ref[channel].astype(jnp.float32)
-        theirs = theirs_ref[channel].astype(jnp.float32)
+        mine, theirs = mine_ref[channel], theirs_ref[channel]
         return (
             totals[0] + mine * rows[0],
             totals[1] + mine * rows[1],
@@ -355,7 +356,7 @@
         )
 
     zeros = jnp.zeros((kept, columns), jnp.float32)
-    totals = lax.fori_loop(0, channels, add_channel, (zeros,) * 4, unroll=8)
+    totals = lax.fori_loop(0, channels, add_channel, (zeros,) * 4, unroll=64)
     upper = lax.axis_index("lon") == 0
     mixed = [
         [jnp.where(upper, totals[part], totals[2 + part]) for part in range(2)],
@@ -501,19 +502,20 @@
     def mixing_table(values, after):
         return call(
             functools.partial(mixing_kernel, per_device),
-            bfloat((channels, kept, columns)),
+            jax.ShapeDtypeStruct((channels, kept, columns), jnp.float32),
             [],
             [VMEM, ANY],
             pl.CostEstimate(flops=1 << 20, bytes_accessed=1 << 22, transcendentals=0),
         )(values, after)
 
     mine = mixing_table(mixing, near)
+    theirs = lax.ppermute(mine, "lon", swap)
     analysis, synthesis = call(
         functools.partial(legendre_kernel, span, lat_count, row_count, per_device),
         (bfloat((columns, width)), bfloat((lat_total, columns))),
         [pltpu.VMEM((width // LANES, 2 * degrees, LANES), jnp.float32)],
         [ANY],
-        pl.CostEstimate(flops=1 << 20, bytes_accessed=1 << 21, transcendentals=0),
+        pl.CostEstimate(flops=1 << 35, bytes_accessed=1 << 26, transcendentals=0),
     )(near)
     coeffs = call(
         functools.partial(edge_kernel, lat_total, half),
@@ -527,8 +529,6 @@
         [VMEM] * 7 + [ANY] * 2,
         pl.CostEstimate(flops=1 << 26, bytes_accessed=1 << 20, transcendentals=0),
     )(halo, message, near, first, second, dft, interior, mine, analysis)
-    coeffs, late_mine = lax.optimization_barrier((coeffs, mine))
-    theirs = lax.ppermute(late_mine, "lon", swap)
     pieces = lax.all_to_all(coeffs, both, split_axis=0, concat_axis=0, tiled=True)
 
     chunk_rows = row_count * 2 * per_device * kept // LANES

time: 34.5 us -> 34.3 us (level)
  transfers between devices with their start and end apart: 3 -> 3, of which waited for: 1 -> 1; matrix products, arithmetic and copies ran while one was open for 0% -> 0% of each run, Pallas kernels for 10% -> 12%
where the time goes in v6:
time: 34.3 us; the launch traced here: 34.1 us
  blocking collectives  22.5 us (66%)
  Pallas kernels  5.94 us (17%)
  starting transfers between devices  5.41 us (16%)
    all_to_all x1, blocking collectives, local(): lax.all_to_all(coeffs, both, split_axis=0, concat_axis=0, tiled=True)  13.4 us
    all_to_all x1, blocking collectives, local(): back = lax.all_to_all(chunks, both, split_axis=0, concat_axis=0, tiled=True)  9.1 us
    ppermute x1, starting transfers between devices, local(): halo = lax.ppermute(message, both, pairs)  4.89 us
    pallas_call x1, Pallas kernels, local(): call(functools.partial(interior_kernel, lat_total, owners), (bfloat(taps)...  1.08 us
    pallas_call x1, Pallas kernels, local(): call(load_kernel, (bfloat((row_count, channels, lon_part)), bfloat(argume...  1.07 us
    pallas_call x1, Pallas kernels, local(): call(functools.partial(inverse_kernel, per_device), bfloat((kept, row_cou...  0.91 us
    pallas_call x1, Pallas kernels, local(): call(functools.partial(edge_kernel, lat_total, half), bfloat((owners, per...  0.85 us
    pallas_call x1, Pallas kernels, local(): call(functools.partial(spectral_kernel, per_device), bfloat((owners, chun...  0.8 us
  transfers between devices with their start and end apart: 3, of which 1 were waited for; matrix products, arithmetic and copies ran while one was open for 0% of the time, Pallas kernels for 12%

profile of v6, /device:TPU:0, one launch (start us, length us, event | category | flops | bytes accessed | tf_op | source)
XLA Modules:
  0.0 34.1 jit_solution(12945459432681924808)
XLA Ops:
  0.0 0.5 %collective-permute-start = (bf16[64,8,128]{2,1,0:T(8,128)(2,1)}, bf16[64,8,128]{2,1,0:T(8,128)(2,1)S(1)}, u32[]{:S(2)}, u32[]{:S(2)}) collective-permute-start(bf16[64,8,128]{2,1,0:T(8,128)(2,1)} %fields_ref.1), channel_id=1, source_target_pairs={{0,1},{1,0},{2,3},{3,2},{4,5},{5,4},{6,7},{7,6},{8,9},{9,8},{10,11... | collective-permute-start | bytes 393224 | tf_op jit(solution)/shard_map/ppermute | solution.py:439
  0.5 1.1 %shard_map.46 = (bf16[8,64,128]{2,1,0:T(8,128)(2,1)S(1)}, bf16[3,3,64,64]{3,2,1,0:T(8,128)(2,1)S(1)}, bf16[3,3,64,64]{3,2,1,0:T(8,128)(2,1)S(1)}) custom-call(bf16[64,8,128]{2,1,0:T(8,128)(2,1)} %fields_ref.1, bf16[3,3,64,64]{3,2,1,0:T(8,128)(2,1)} %bitcast.2, bf16[3,3,64,64]{3,2,1,0:T(8,128)(2,1)} %bitcast.3), custom_call_target="tpu_custom_call" | custom-call | flops 65536 | bytes 2097152 | tf_op jit(solution)/shard_map/pallas_call | solution.py:452
  1.5 0.1 collective-permute-done.other_ref
  1.7 0.0 copy-start
  1.7 4.9 %collective-permute-start.1 = (bf16[2,64,256]{2,1,0:T(8,128)(2,1)S(1)}, bf16[2,64,256]{2,1,0:T(8,128)(2,1)S(1)}, u32[]{:S(2)}, u32[]{:S(2)}) collective-permute-start(bf16[2,64,256]{2,1,0:T(8,128)(2,1)S(1)} %shard_map.47.after_ref.message_ref), channel_id=1, source_target_pairs={{0,2},{2,0},{3,5},{5,3},{4,6},{6,4},{7,9},{9,7},{8,10},{10,8},{11,... | collective-permute-start | bytes 196616 | tf_op jit(solution)/shard_map/ppermute | solution.py:474
  6.6 1.1 %shard_map.48 = (bf16[192,192]{1,0:T(8,128)(2,1)S(1)}, bf16[192,192]{1,0:T(8,128)(2,1)S(1)}, bf16[128,256]{1,0:T(8,128)(2,1)S(1)}, bf16[2,64,256]{2,1,0:T(8,128)(2,1)S(1)}, f32[2,64,128]{2,1,0:T(8,128)S(1)}) custom-call(bf16[8,64,128]{2,1,0:T(8,128)(2,1)S(1)} %get-tuple-element.15.own_ref, bf16[64,8,128]{2,1,0:T(8,128)(2,1)S(1)} %collective-permute-done.other_ref, ...), custom_call_target="tpu_custom_call" | custom-call | flops 268435456 | bytes 4194304 | tf_op jit(solution)/shard_map/pallas_call | solution.py:477
  7.7 0.0 copy-done
  7.7 0.7 %shard_map.49.mine_ref = f32[64,32,128]{2,1,0:T(8,128)S(1)} custom-call(bf16[64,32,64]{2,1,0:T(8,128)(2,1)S(1)} %copy-done, bf16[2,64,256]{2,1,0:T(8,128)(2,1)S(1)} %get-tuple-element.18.after_ref.near_ref), custom_call_target="tpu_custom_call" | custom-call | flops 1048576 | bytes 4194304 | tf_op jit(solution)/shard_map/pallas_call | solution.py:503
  8.4 0.1 collective-permute-start.2
  8.5 0.5 %shard_map.50 = (bf16[128,256]{1,0:T(8,128)(2,1)S(1)}, bf16[128,128]{1,0:T(8,128)(2,1)S(1)}) custom-call(bf16[2,64,256]{2,1,0:T(8,128)(2,1)S(1)} %get-tuple-element.18.after_ref.near_ref), custom_call_target="tpu_custom_call" | custom-call | flops 34359738368 | bytes 67108864 | tf_op jit(solution)/shard_map/pallas_call | solution.py:513
  9.0 0.0 collective-permute-done.1.halo_ref
  9.0 0.8 %shard_map.51 = bf16[32,8,128]{2,1,0:T(8,128)(2,1)S(1)} custom-call(bf16[2,64,256]{2,1,0:T(8,128)(2,1)S(1)} %collective-permute-done.1.halo_ref, bf16[2,64,256]{2,1,0:T(8,128)(2,1)S(1)} %shard_map.47.after_ref.message_ref, bf16[2,64,256]{2,1,0:T(8,128)(2,1)S(1)} %get-tuple-element.18.after_ref.near_ref, bf16[192,192]{1,0:T(8,128)(2,1)S(1)} %get-tuple-element.19.first_ref, ...), custom_call_target="tpu_custom_call" | custom-call | flops 67108864 | bytes 1048576 | tf_op jit(solution)/shard_map/pallas_call | solution.py:520
  9.8 13.4 %all_to_all.10.pieces_ref = bf16[32,8,128]{2,1,0:T(8,128)(2,1)S(1)} all-to-all(bf16[32,8,128]{2,1,0:T(8,128)(2,1)S(1)} %shard_map.51), channel_id=1, replica_groups=mesh['groups'=1,'lat'=16,'lon'=2] {'lat','lon'}, dimensions={0} | all-to-all | bytes 131072 | tf_op jit(solution)/shard_map/all_to_all | solution.py:532
  23.3 0.0 collective-permute-done.2.theirs_ref
  23.3 0.8 %shard_map.52 = bf16[32,8,128]{2,1,0:T(8,128)(2,1)S(1)} custom-call(bf16[32,8,128]{2,1,0:T(8,128)(2,1)S(1)} %all_to_all.10.pieces_ref, bf16[128,256]{1,0:T(8,128)(2,1)S(1)} %get-tuple-element.23.analysis_ref, bf16[128,128]{1,0:T(8,128)(2,1)S(1)} %get-tuple-element.24.synthesis_ref, f32[64,32,128]{2,1,0:T(8,128)S(1)} %shard_map.49.mine_ref, ...), custom_call_target="tpu_custom_call" | custom-call | flops 16777216 | bytes 1048576 | tf_op jit(solution)/shard_map/pallas_call | solution.py:535
  24.1 9.1 %all_to_all.11.pieces_ref = bf16[32,8,128]{2,1,0:T(8,128)(2,1)S(1)} all-to-all(bf16[32,8,128]{2,1,0:T(8,128)(2,1)S(1)} %shard_map.52), channel_id=1, replica_groups=mesh['groups'=1,'lat'=16,'lon'=2] {'lat','lon'}, dimensions={0} | all-to-all | bytes 131072 | tf_op jit(solution)/shard_map/all_to_all | solution.py:546
  33.2 0.9 %shard_map.53 = bf16[32,8,256]{2,1,0:T(8,128)(2,1)} custom-call(bf16[32,8,128]{2,1,0:T(8,128)(2,1)S(1)} %all_to_all.11.pieces_ref, bf16[128,256]{1,0:T(8,128)(2,1)S(1)} %get-tuple-element.21.dft_ref), custom_call_target="tpu_custom_call" | custom-call | flops 16777216 | bytes 524288 | tf_op jit(solution)/shard_map/pallas_call | solution.py:547
  (1 shorter events, 0.0 us)
Async XLA Ops:
  0.0 1.6 %collective-permute-start = (bf16[64,8,128]{2,1,0:T(8,128)(2,1)}, bf16[64,8,128]{2,1,0:T(8,128)(2,1)S(1)}, u32[]{:S(2)}, u32[]{:S(2)}) collective-permute-start(bf16[64,8,128]{2,1,0:T(8,128)(2,1)} %fields_ref.1), channel_id=1, source_target_pairs={{0,1},{1,0},{2,3},{3,2},{4,5},{5,4},{6,7},{7,6},{8,9},{9,8},{10,11... | collective-permute-start | bytes 393224 | tf_op jit(solution)/shard_map/ppermute | solution.py:439
  1.7 6.0 %copy-start = (bf16[64,32,64]{2,1,0:T(8,128)(2,1)S(1)}, bf16[64,32,64]{2,1,0:T(8,128)(2,1)}, u32[]{:S(2)}) copy-start(bf16[64,32,64]{2,1,0:T(8,128)(2,1)} %mixing_ref.1) | copy-start | bytes 786436
  1.7 7.3 %collective-permute-start.1 = (bf16[2,64,256]{2,1,0:T(8,128)(2,1)S(1)}, bf16[2,64,256]{2,1,0:T(8,128)(2,1)S(1)}, u32[]{:S(2)}, u32[]{:S(2)}) collective-permute-start(bf16[2,64,256]{2,1,0:T(8,128)(2,1)S(1)} %shard_map.47.after_ref.message_ref), channel_id=1, source_target_pairs={{0,2},{2,0},{3,5},{5,3},{4,6},{6,4},{7,9},{9,7},{8,10},{10,8},{11,... | collective-permute-start | bytes 196616 | tf_op jit(solution)/shard_map/ppermute | solution.py:474
  8.4 14.9 %collective-permute-start.2 = (f32[64,32,128]{2,1,0:T(8,128)S(1)}, f32[64,32,128]{2,1,0:T(8,128)S(1)}, u32[]{:S(2)}, u32[]{:S(2)}) collective-permute-start(f32[64,32,128]{2,1,0:T(8,128)S(1)} %shard_map.49.mine_ref), channel_id=1, source_target_pairs={{0,1},{1,0},{2,3},{3,2},{4,5},{5,4},{6,7},{7,6},{8,9},{9,8},{10,11... | collective-permute-start | bytes 3145736 | tf_op jit(solution)/shard_map/ppermute | solution.py:512

commit v7 on v6

--- a/solution.py
+++ b/solution.py
@@ -32,8 +32,13 @@
     return quotient, index - quotient * size
 
 
+def half_of(lat, lon, bands):
+    last = (lat + 1) // bands if isinstance(lat, int) else (lat + 1 == bands).astype(jnp.int32)
+    return (lat + lon + 1 + last) & 1
+
+
 def row_half():
-    return (lax.axis_index("lat") + lax.axis_index("lon") + 1) & 1
+    return half_of(lax.axis_index("lat"), lax.axis_index("lon"), lax.axis_size("lat"))
 
 
 def unpack_rows(source_ref, rows_ref):
@@ -260,7 +265,7 @@
     rest, band = split_index(lane, bands)
     own_second, inner = split_index(rest, row_count)
     own = jnp.where(form == 0, own_first, own_second)
-    place = (device >> 1) * row_count + (((device >> 1) + device + 1) & 1) * half + low
+    place = (device >> 1) * row_count + half_of(device >> 1, device & 1, bands) * half + low
     row = jnp.where(form == 0, place, band * row_count + inner)
     south = row >= lat_total // 2
     row = jnp.where(south, lat_total - 1 - row, row)
@@ -469,7 +474,8 @@
     )(own, other)
     pairs = []
     for i in range(lat_count - 1):
-        lower, upper = 2 * i + i % 2, 2 * (i + 1) + i % 2
+        lower = 2 * i + half_of(i, 1, lat_count)
+        upper = 2 * (i + 1) + half_of(i + 1, 0, lat_count)
         pairs += [(lower, upper), (upper, lower)]
     halo = lax.ppermute(message, both, pairs)
 

time: 34.3 us -> 33.7 us (0.983)
  blocking collectives: 22.5 us -> 21.9 us
    all_to_all x1, blocking collectives: 13.4 us -> 12.8 us  [local(): lax.all_to_all(coeffs, both, split_axis=0, concat_axis=0, tiled=True)]
  transfers between devices with their start and end apart: 3 -> 3, of which waited for: 1 -> 1; matrix products, arithmetic and copies ran while one was open for 0% -> 0% of each run, Pallas kernels for 12% -> 13%
where the time goes in v7:
time: 33.7 us; the launch traced here: 33.5 us
  blocking collectives  21.9 us (65%)
  Pallas kernels  5.94 us (18%)
  starting transfers between devices  5.41 us (16%)
    all_to_all x1, blocking collectives, local(): lax.all_to_all(coeffs, both, split_axis=0, concat_axis=0, tiled=True)  12.8 us
    all_to_all x1, blocking collectives, local(): back = lax.all_to_all(chunks, both, split_axis=0, concat_axis=0, tiled=True)  9.1 us
    ppermute x1, starting transfers between devices, local(): halo = lax.ppermute(message, both, pairs)  4.89 us
    pallas_call x1, Pallas kernels, local(): call(functools.partial(interior_kernel, lat_total, owners), (bfloat(taps)...  1.08 us
    pallas_call x1, Pallas kernels, local(): call(load_kernel, (bfloat((row_count, channels, lon_part)), bfloat(argume...  1.07 us
    pallas_call x1, Pallas kernels, local(): call(functools.partial(inverse_kernel, per_device), bfloat((kept, row_cou...  0.91 us
    pallas_call x1, Pallas kernels, local(): call(functools.partial(edge_kernel, lat_total, half), bfloat((owners, per...  0.85 us
    pallas_call x1, Pallas kernels, local(): call(functools.partial(spectral_kernel, per_device), bfloat((owners, chun...  0.8 us
  transfers between devices with their start and end apart: 3, of which 1 were waited for; matrix products, arithmetic and copies ran while one was open for 0% of the time, Pallas kernels for 13%

profile of v7, /device:TPU:0, one launch (start us, length us, event | category | flops | bytes accessed | tf_op | source)
XLA Modules:
  0.0 33.5 jit_solution(16958119003615201381)
XLA Ops:
  0.0 0.5 %collective-permute-start = (bf16[64,8,128]{2,1,0:T(8,128)(2,1)}, bf16[64,8,128]{2,1,0:T(8,128)(2,1)S(1)}, u32[]{:S(2)}, u32[]{:S(2)}) collective-permute-start(bf16[64,8,128]{2,1,0:T(8,128)(2,1)} %fields_ref.1), channel_id=1, source_target_pairs={{0,1},{1,0},{2,3},{3,2},{4,5},{5,4},{6,7},{7,6},{8,9},{9,8},{10,11... | collective-permute-start | bytes 393224 | tf_op jit(solution)/shard_map/ppermute | solution.py:444
  0.5 1.1 %shard_map.46 = (bf16[8,64,128]{2,1,0:T(8,128)(2,1)S(1)}, bf16[3,3,64,64]{3,2,1,0:T(8,128)(2,1)S(1)}, bf16[3,3,64,64]{3,2,1,0:T(8,128)(2,1)S(1)}) custom-call(bf16[64,8,128]{2,1,0:T(8,128)(2,1)} %fields_ref.1, bf16[3,3,64,64]{3,2,1,0:T(8,128)(2,1)} %bitcast.2, bf16[3,3,64,64]{3,2,1,0:T(8,128)(2,1)} %bitcast.3), custom_call_target="tpu_custom_call" | custom-call | flops 65536 | bytes 2097152 | tf_op jit(solution)/shard_map/pallas_call | solution.py:457
  1.5 0.1 collective-permute-done.other_ref
  1.7 0.0 copy-start
  1.7 4.9 %collective-permute-start.1 = (bf16[2,64,256]{2,1,0:T(8,128)(2,1)S(1)}, bf16[2,64,256]{2,1,0:T(8,128)(2,1)S(1)}, u32[]{:S(2)}, u32[]{:S(2)}) collective-permute-start(bf16[2,64,256]{2,1,0:T(8,128)(2,1)S(1)} %shard_map.47.after_ref.message_ref), channel_id=1, source_target_pairs={{0,2},{2,0},{3,5},{5,3},{4,6},{6,4},{7,9},{9,7},{8,10},{10,8},{11,... | collective-permute-start | bytes 196616 | tf_op jit(solution)/shard_map/ppermute | solution.py:480
  6.6 1.1 %shard_map.48 = (bf16[192,192]{1,0:T(8,128)(2,1)S(1)}, bf16[192,192]{1,0:T(8,128)(2,1)S(1)}, bf16[128,256]{1,0:T(8,128)(2,1)S(1)}, bf16[2,64,256]{2,1,0:T(8,128)(2,1)S(1)}, f32[2,64,128]{2,1,0:T(8,128)S(1)}) custom-call(bf16[8,64,128]{2,1,0:T(8,128)(2,1)S(1)} %get-tuple-element.15.own_ref, bf16[64,8,128]{2,1,0:T(8,128)(2,1)S(1)} %collective-permute-done.other_ref, ...), custom_call_target="tpu_custom_call" | custom-call | flops 268435456 | bytes 4194304 | tf_op jit(solution)/shard_map/pallas_call | solution.py:483
  7.7 0.0 copy-done
  7.7 0.7 %shard_map.49.mine_ref = f32[64,32,128]{2,1,0:T(8,128)S(1)} custom-call(bf16[64,32,64]{2,1,0:T(8,128)(2,1)S(1)} %copy-done, bf16[2,64,256]{2,1,0:T(8,128)(2,1)S(1)} %get-tuple-element.18.after_ref.near_ref), custom_call_target="tpu_custom_call" | custom-call | flops 1048576 | bytes 4194304 | tf_op jit(solution)/shard_map/pallas_call | solution.py:509
  8.4 0.1 collective-permute-start.2
  8.5 0.5 %shard_map.50 = (bf16[128,256]{1,0:T(8,128)(2,1)S(1)}, bf16[128,128]{1,0:T(8,128)(2,1)S(1)}) custom-call(bf16[2,64,256]{2,1,0:T(8,128)(2,1)S(1)} %get-tuple-element.18.after_ref.near_ref), custom_call_target="tpu_custom_call" | custom-call | flops 34359738368 | bytes 67108864 | tf_op jit(solution)/shard_map/pallas_call | solution.py:519
  9.0 0.0 collective-permute-done.1.halo_ref
  9.0 0.8 %shard_map.51 = bf16[32,8,128]{2,1,0:T(8,128)(2,1)S(1)} custom-call(bf16[2,64,256]{2,1,0:T(8,128)(2,1)S(1)} %collective-permute-done.1.halo_ref, bf16[2,64,256]{2,1,0:T(8,128)(2,1)S(1)} %shard_map.47.after_ref.message_ref, bf16[2,64,256]{2,1,0:T(8,128)(2,1)S(1)} %get-tuple-element.18.after_ref.near_ref, bf16[192,192]{1,0:T(8,128)(2,1)S(1)} %get-tuple-element.19.first_ref, ...), custom_call_target="tpu_custom_call" | custom-call | flops 67108864 | bytes 1048576 | tf_op jit(solution)/shard_map/pallas_call | solution.py:526
  9.8 12.8 %all_to_all.10.pieces_ref = bf16[32,8,128]{2,1,0:T(8,128)(2,1)S(1)} all-to-all(bf16[32,8,128]{2,1,0:T(8,128)(2,1)S(1)} %shard_map.51), channel_id=1, replica_groups=mesh['groups'=1,'lat'=16,'lon'=2] {'lat','lon'}, dimensions={0} | all-to-all | bytes 131072 | tf_op jit(solution)/shard_map/all_to_all | solution.py:538
  22.7 0.0 collective-permute-done.2.theirs_ref
  22.7 0.8 %shard_map.52 = bf16[32,8,128]{2,1,0:T(8,128)(2,1)S(1)} custom-call(bf16[32,8,128]{2,1,0:T(8,128)(2,1)S(1)} %all_to_all.10.pieces_ref, bf16[128,256]{1,0:T(8,128)(2,1)S(1)} %get-tuple-element.23.analysis_ref, bf16[128,128]{1,0:T(8,128)(2,1)S(1)} %get-tuple-element.24.synthesis_ref, f32[64,32,128]{2,1,0:T(8,128)S(1)} %shard_map.49.mine_ref, ...), custom_call_target="tpu_custom_call" | custom-call | flops 16777216 | bytes 1048576 | tf_op jit(solution)/shard_map/pallas_call | solution.py:541
  23.5 9.1 %all_to_all.11.pieces_ref = bf16[32,8,128]{2,1,0:T(8,128)(2,1)S(1)} all-to-all(bf16[32,8,128]{2,1,0:T(8,128)(2,1)S(1)} %shard_map.52), channel_id=1, replica_groups=mesh['groups'=1,'lat'=16,'lon'=2] {'lat','lon'}, dimensions={0} | all-to-all | bytes 131072 | tf_op jit(solution)/shard_map/all_to_all | solution.py:552
  32.6 0.9 %shard_map.53 = bf16[32,8,256]{2,1,0:T(8,128)(2,1)} custom-call(bf16[32,8,128]{2,1,0:T(8,128)(2,1)S(1)} %all_to_all.11.pieces_ref, bf16[128,256]{1,0:T(8,128)(2,1)S(1)} %get-tuple-element.21.dft_ref), custom_call_target="tpu_custom_call" | custom-call | flops 16777216 | bytes 524288 | tf_op jit(solution)/shard_map/pallas_call | solution.py:553
  (1 shorter events, 0.0 us)
Async XLA Ops:
  0.0 1.6 %collective-permute-start = (bf16[64,8,128]{2,1,0:T(8,128)(2,1)}, bf16[64,8,128]{2,1,0:T(8,128)(2,1)S(1)}, u32[]{:S(2)}, u32[]{:S(2)}) collective-permute-start(bf16[64,8,128]{2,1,0:T(8,128)(2,1)} %fields_ref.1), channel_id=1, source_target_pairs={{0,1},{1,0},{2,3},{3,2},{4,5},{5,4},{6,7},{7,6},{8,9},{9,8},{10,11... | collective-permute-start | bytes 393224 | tf_op jit(solution)/shard_map/ppermute | solution.py:444
  1.7 6.0 %copy-start = (bf16[64,32,64]{2,1,0:T(8,128)(2,1)S(1)}, bf16[64,32,64]{2,1,0:T(8,128)(2,1)}, u32[]{:S(2)}) copy-start(bf16[64,32,64]{2,1,0:T(8,128)(2,1)} %mixing_ref.1) | copy-start | bytes 786436
  1.7 7.3 %collective-permute-start.1 = (bf16[2,64,256]{2,1,0:T(8,128)(2,1)S(1)}, bf16[2,64,256]{2,1,0:T(8,128)(2,1)S(1)}, u32[]{:S(2)}, u32[]{:S(2)}) collective-permute-start(bf16[2,64,256]{2,1,0:T(8,128)(2,1)S(1)} %shard_map.47.after_ref.message_ref), channel_id=1, source_target_pairs={{0,2},{2,0},{3,5},{5,3},{4,6},{6,4},{7,9},{9,7},{8,10},{10,8},{11,... | collective-permute-start | bytes 196616 | tf_op jit(solution)/shard_map/ppermute | solution.py:480
  8.4 14.2 %collective-permute-start.2 = (f32[64,32,128]{2,1,0:T(8,128)S(1)}, f32[64,32,128]{2,1,0:T(8,128)S(1)}, u32[]{:S(2)}, u32[]{:S(2)}) collective-permute-start(f32[64,32,128]{2,1,0:T(8,128)S(1)} %shard_map.49.mine_ref), channel_id=1, source_target_pairs={{0,1},{1,0},{2,3},{3,2},{4,5},{5,4},{6,7},{7,6},{8,9},{9,8},{10,11... | collective-permute-start | bytes 3145736 | tf_op jit(solution)/shard_map/ppermute | solution.py:518

commit v8 on v7

--- a/solution.py
+++ b/solution.py
@@ -118,6 +118,32 @@
     return jnp.maximum(total, 0.0)
 
 
+def two_rows(weights, pair):
+    _, channels, lon_total = pair.shape
+    sums = jnp.dot(
+        weights, pair.reshape(2 * channels, lon_total), preferred_element_type=jnp.float32
+    )
+    found = []
+    for i in range(2):
+        part = sums[3 * channels * i : 3 * channels * (i + 1)]
+        found.append(
+            part[channels : 2 * channels]
+            + pltpu.roll(part[:channels], 1, 1)
+            + pltpu.roll(part[2 * channels :], lon_total - 1, 1)
+        )
+    return found
+
+
+def two_row_weights(taps, out_ref):
+    height, width = taps.shape
+    channels = width // 3
+    zeros = jnp.zeros((height, channels), jnp.bfloat16)
+    out_ref[0, :height, :] = taps[:, : 2 * channels]
+    out_ref[0, height:, :] = jnp.concatenate([zeros, taps[:, :channels]], axis=1)
+    out_ref[1, :height, :] = jnp.concatenate([taps[:, 2 * channels :], zeros], axis=1)
+    out_ref[1, height:, :] = taps[:, channels:]
+
+
 def row_weight(row, lat_total, lon_total):
     place = jnp.full((1, LANES), row, jnp.int32).astype(jnp.float32)
     return jnp.sin((place + 0.5) * (math.pi / lat_total)) * (math.pi / lat_total / lon_total)
@@ -147,23 +173,26 @@
     other_ref,
     first_ref,
     second_ref,
-    after_ref,
+    message_ref,
     first_out,
     second_out,
     dft_out,
-    near_out,
+    first_part_out,
+    second_part_out,
     coeffs_out,
     rows_ref,
     band_ref,
     mid_ref,
     hidden_ref,
+    taps_ref,
+    forms_ref,
 ):
-    del after_ref
     row_count, channels, lon_part = own_ref.shape
     lon_total = 2 * lon_part
     half = row_count // 2
     side, part = lax.axis_index("lon"), row_half()
-    for source, target in ((first_ref, first_out), (second_ref, second_out)):
+    for layer_id, source in enumerate((first_ref, second_ref)):
+        target = taps_ref.at[layer_id]
         for b in range(3):
             target[b * channels : (b + 1) * channels, :] = jnp.concatenate(
                 [source[a, b] for a in range(3)], axis=1
@@ -180,11 +209,20 @@
     for i in range(half + 2):
         row = 2 * part + i
         place_row(band_ref, i, side, own_ref[row], packed_row(rows_ref, row, channels))
-    weights = first_out[...]
+    weights = taps_ref[0]
     for i in range(half):
         mid_ref[i] = layer(band_ref, weights, i).astype(jnp.bfloat16)
-    near_out[...] = mid_ref[pl.ds((half - 2) * part, 2)]
-    weights = second_out[...]
+    for layer_id, (weights_out, part_out, pair) in enumerate(
+        (
+            (first_out, first_part_out, message_ref[...]),
+            (second_out, second_part_out, mid_ref[pl.ds((half - 2) * part, 2)]),
+        )
+    ):
+        two_row_weights(taps_ref[layer_id], forms_ref.at[layer_id])
+        weights_out[...] = forms_ref[layer_id, part]
+        for i, values in enumerate(two_rows(forms_ref[layer_id, 1 - part], pair)):
+            part_out[i] = values
+    weights = taps_ref[1]
     for i in range(half - 2):
         hidden_ref[i] = layer(mid_ref, weights, i).astype(jnp.bfloat16)
     first_row = lax.axis_index("lat") * row_count + part * half + 2 * (1 - part)
@@ -197,37 +235,32 @@
     lat_total,
     half,
     halo_ref,
-    message_ref,
-    near_ref,
     first_ref,
     second_ref,
     dft_ref,
+    first_part_ref,
+    second_part_ref,
     coeffs_ref,
     mine_ref,
     analysis_ref,
     out_ref,
-    band_ref,
-    mid_ref,
-    hidden_ref,
     packed_ref,
 ):
     del mine_ref, analysis_ref
     part = row_half()
     first_row = lax.axis_index("lat") * (2 * half) + part * half
-    band_ref[pl.ds(2 * part, 2)] = halo_ref[...]
-    band_ref[pl.ds(2 - 2 * part, 2)] = message_ref[...]
-    mid_ref[pl.ds(2 - 2 * part, 2)] = near_ref[...]
-    weights = first_ref[...]
-    for i in range(2):
+    mid = []
+    for i, values in enumerate(two_rows(first_ref[...], halo_ref[...])):
         place = first_row - 1 + part * half + i
-        values = layer(band_ref, weights, i)
+        values = jnp.maximum(values + first_part_ref[i], 0.0)
         values = jnp.where((place >= 0) & (place < lat_total), values, 0.0)
-        mid_ref[2 * part + i] = values.astype(jnp.bfloat16)
-    weights = second_ref[...]
-    for i in range(2):
-        hidden_ref[i] = layer(mid_ref, weights, i).astype(jnp.bfloat16)
+        mid.append(values.astype(jnp.bfloat16))
+    hidden = [
+        jnp.maximum(values + second_part_ref[i], 0.0).astype(jnp.bfloat16)
+        for i, values in enumerate(two_rows(second_ref[...], jnp.stack(mid)))
+    ]
     edge = part * (half - 2)
-    found = row_spectra(dft_ref[...], hidden_ref[...], first_row + edge, lat_total)
+    found = row_spectra(dft_ref[...], jnp.stack(hidden), first_row + edge, lat_total)
     owners, chunk_rows, _ = out_ref.shape
     for m in range(chunk_rows // half):
         own = slice(m * owners, (m + 1) * owners)
@@ -479,14 +512,16 @@
         pairs += [(lower, upper), (upper, lower)]
     halo = lax.ppermute(message, both, pairs)
 
-    taps = (3 * channels, 3 * channels)
-    first, second, dft, near, interior = call(
+    taps = (6 * channels, 2 * channels)
+    pair = jax.ShapeDtypeStruct((2, channels, lon_total), jnp.float32)
+    first, second, dft, first_part, second_part, interior = call(
         functools.partial(interior_kernel, lat_total, owners),
         (
             bfloat(taps),
             bfloat(taps),
             bfloat((2 * orders, lon_total)),
-            bfloat((2, channels, lon_total)),
+            pair,
+            pair,
             jax.ShapeDtypeStruct((half - 2, orders, 2 * channels), jnp.float32),
         ),
         [
@@ -494,8 +529,10 @@
             pltpu.VMEM((half + 2, channels, lon_total), jnp.bfloat16),
             pltpu.VMEM((half, channels, lon_total), jnp.bfloat16),
             pltpu.VMEM((half - 2, channels, lon_total), jnp.bfloat16),
+            pltpu.VMEM((2, 3 * channels, 3 * channels), jnp.bfloat16),
+            pltpu.VMEM((2, 2) + taps, jnp.bfloat16),
         ],
-        [VMEM, VMEM, VMEM, VMEM, ANY],
+        [VMEM] * 5,
         pl.CostEstimate(flops=1 << 28, bytes_accessed=1 << 22, transcendentals=0),
     )(
         own,
@@ -514,7 +551,7 @@
             pl.CostEstimate(flops=1 << 20, bytes_accessed=1 << 22, transcendentals=0),
         )(values, after)
 
-    mine = mixing_table(mixing, near)
+    mine = mixing_table(mixing, second_part)
     theirs = lax.ppermute(mine, "lon", swap)
     analysis, synthesis = call(
         functools.partial(legendre_kernel, span, lat_count, row_count, per_device),
@@ -522,19 +559,14 @@
         [pltpu.VMEM((width // LANES, 2 * degrees, LANES), jnp.float32)],
         [ANY],
         pl.CostEstimate(flops=1 << 35, bytes_accessed=1 << 26, transcendentals=0),
-    )(near)
+    )(second_part)
     coeffs = call(
         functools.partial(edge_kernel, lat_total, half),
         bfloat((owners, per_device * half, 2 * channels)),
-        [
-            pltpu.VMEM((4, channels, lon_total), jnp.bfloat16),
-            pltpu.VMEM((4, channels, lon_total), jnp.bfloat16),
-            pltpu.VMEM((2, channels, lon_total), jnp.bfloat16),
-            pltpu.VMEM((orders * half, 2 * channels), jnp.float32),
-        ],
+        [pltpu.VMEM((orders * half, 2 * channels), jnp.float32)],
         [VMEM] * 7 + [ANY] * 2,
         pl.CostEstimate(flops=1 << 26, bytes_accessed=1 << 20, transcendentals=0),
-    )(halo, message, near, first, second, dft, interior, mine, analysis)
+    )(halo, first, second, dft, first_part, second_part, interior, mine, analysis)
     pieces = lax.all_to_all(coeffs, both, split_axis=0, concat_axis=0, tiled=True)
 
     chunk_rows = row_count * 2 * per_device * kept // LANES

time: 33.7 us -> 33.6 us (level)
  no operation moved by 1% of the time
where the time goes in v8:
time: 33.6 us; the launch traced here: 33.4 us
  blocking collectives  21.7 us (65%)
  Pallas kernels  6.17 us (18%)
  starting transfers between devices  5.41 us (16%)
    all_to_all x1, blocking collectives, local(): lax.all_to_all(coeffs, both, split_axis=0, concat_axis=0, tiled=True)  12.6 us
    all_to_all x1, blocking collectives, local(): back = lax.all_to_all(chunks, both, split_axis=0, concat_axis=0, tiled=True)  9.1 us
    ppermute x1, starting transfers between devices, local(): halo = lax.ppermute(message, both, pairs)  4.89 us
    pallas_call x1, Pallas kernels, local(): call(functools.partial(interior_kernel, lat_total, owners), (bfloat(taps)...  1.35 us
    pallas_call x1, Pallas kernels, local(): call(load_kernel, (bfloat((row_count, channels, lon_part)), bfloat(argume...  1.07 us
    pallas_call x1, Pallas kernels, local(): call(functools.partial(inverse_kernel, per_device), bfloat((kept, row_cou...  0.91 us
    pallas_call x1, Pallas kernels, local(): call(functools.partial(edge_kernel, lat_total, half), bfloat((owners, per...  0.81 us
    pallas_call x1, Pallas kernels, local(): call(functools.partial(spectral_kernel, per_device), bfloat((owners, chun...  0.8 us
  transfers between devices with their start and end apart: 3, of which 1 were waited for; matrix products, arithmetic and copies ran while one was open for 0% of the time, Pallas kernels for 13%

profile of v8, /device:TPU:0, one launch (start us, length us, event | category | flops | bytes accessed | tf_op | source)
XLA Modules:
  0.0 33.4 jit_solution(6387753106854201481)
XLA Ops:
  0.0 0.5 %collective-permute-start = (bf16[64,8,128]{2,1,0:T(8,128)(2,1)}, bf16[64,8,128]{2,1,0:T(8,128)(2,1)S(1)}, u32[]{:S(2)}, u32[]{:S(2)}) collective-permute-start(bf16[64,8,128]{2,1,0:T(8,128)(2,1)} %fields_ref.1), channel_id=1, source_target_pairs={{0,1},{1,0},{2,3},{3,2},{4,5},{5,4},{6,7},{7,6},{8,9},{9,8},{10,11... | collective-permute-start | bytes 393224 | tf_op jit(solution)/shard_map/ppermute | solution.py:477
  0.5 1.1 %shard_map.46 = (bf16[8,64,128]{2,1,0:T(8,128)(2,1)S(1)}, bf16[3,3,64,64]{3,2,1,0:T(8,128)(2,1)S(1)}, bf16[3,3,64,64]{3,2,1,0:T(8,128)(2,1)S(1)}) custom-call(bf16[64,8,128]{2,1,0:T(8,128)(2,1)} %fields_ref.1, bf16[3,3,64,64]{3,2,1,0:T(8,128)(2,1)} %bitcast.2, bf16[3,3,64,64]{3,2,1,0:T(8,128)(2,1)} %bitcast.3), custom_call_target="tpu_custom_call" | custom-call | flops 65536 | bytes 2097152 | tf_op jit(solution)/shard_map/pallas_call | solution.py:490
  1.5 0.1 collective-permute-done.other_ref
  1.7 0.0 copy-start
  1.7 4.9 %collective-permute-start.1 = (bf16[2,64,256]{2,1,0:T(8,128)(2,1)S(1)}, bf16[2,64,256]{2,1,0:T(8,128)(2,1)S(1)}, u32[]{:S(2)}, u32[]{:S(2)}) collective-permute-start(bf16[2,64,256]{2,1,0:T(8,128)(2,1)S(1)} %shard_map.47.message_ref), channel_id=1, source_target_pairs={{0,2},{2,0},{3,5},{5,3},{4,6},{6,4},{7,9},{9,7},{8,10},{10,8},{11,... | collective-permute-start | bytes 196616 | tf_op jit(solution)/shard_map/ppermute | solution.py:513
  6.6 1.4 %shard_map.48 = (bf16[384,128]{1,0:T(8,128)(2,1)S(1)}, bf16[384,128]{1,0:T(8,128)(2,1)S(1)}, bf16[128,256]{1,0:T(8,128)(2,1)S(1)}, f32[2,64,256]{2,1,0:T(8,128)S...) custom-call(bf16[8,64,128]{2,1,0:T(8,128)(2,1)S(1)} %get-tuple-element.16.own_ref, ...), custom_call_target="tpu_custom_call" | custom-call | flops 268435456 | bytes 4194304 | tf_op jit(solution)/shard_map/pallas_call | solution.py:517
  8.0 0.0 copy-done
  8.0 0.7 %shard_map.49.mine_ref = f32[64,32,128]{2,1,0:T(8,128)S(1)} custom-call(bf16[64,32,64]{2,1,0:T(8,128)(2,1)S(1)} %copy-done, f32[2,64,256]{2,1,0:T(8,128)S(1)} %get-tuple-element.23.after_ref.second_part_ref), custom_call_target="tpu_custom_call" | custom-call | flops 1048576 | bytes 4194304 | tf_op jit(solution)/shard_map/pallas_call | solution.py:546
  8.7 0.1 collective-permute-start.2
  8.8 0.5 %shard_map.50 = (bf16[128,256]{1,0:T(8,128)(2,1)S(1)}, bf16[128,128]{1,0:T(8,128)(2,1)S(1)}) custom-call(f32[2,64,256]{2,1,0:T(8,128)S(1)} %get-tuple-element.23.after_ref.second_part_ref), custom_call_target="tpu_custom_call" | custom-call | flops 34359738368 | bytes 67108864 | tf_op jit(solution)/shard_map/pallas_call | solution.py:556
  9.2 0.0 collective-permute-done.1.halo_ref
  9.2 0.8 %shard_map.51 = bf16[32,8,128]{2,1,0:T(8,128)(2,1)S(1)} custom-call(bf16[2,64,256]{2,1,0:T(8,128)(2,1)S(1)} %collective-permute-done.1.halo_ref, bf16[384,128]{1,0:T(8,128)(2,1)S(1)} %get-tuple-element.19.first_ref, bf16[384,128]{1,0:T(8,128)(2,1)S(1)} %get-tuple-element.20.second_ref, bf16[128,256]{1,0:T(8,128)(2,1)S(1)} %get-tuple-element.21.dft_ref, ...), custom_call_target="tpu_custom_call" | custom-call | flops 67108864 | bytes 1048576 | tf_op jit(solution)/shard_map/pallas_call | solution.py:563
  10.1 12.6 %all_to_all.10.pieces_ref = bf16[32,8,128]{2,1,0:T(8,128)(2,1)S(1)} all-to-all(bf16[32,8,128]{2,1,0:T(8,128)(2,1)S(1)} %shard_map.51), channel_id=1, replica_groups=mesh['groups'=1,'lat'=16,'lon'=2] {'lat','lon'}, dimensions={0} | all-to-all | bytes 131072 | tf_op jit(solution)/shard_map/all_to_all | solution.py:570
  22.6 0.0 collective-permute-done.2.theirs_ref
  22.6 0.8 %shard_map.52 = bf16[32,8,128]{2,1,0:T(8,128)(2,1)S(1)} custom-call(bf16[32,8,128]{2,1,0:T(8,128)(2,1)S(1)} %all_to_all.10.pieces_ref, bf16[128,256]{1,0:T(8,128)(2,1)S(1)} %get-tuple-element.25.analysis_ref, bf16[128,128]{1,0:T(8,128)(2,1)S(1)} %get-tuple-element.26.synthesis_ref, f32[64,32,128]{2,1,0:T(8,128)S(1)} %shard_map.49.mine_ref, ...), custom_call_target="tpu_custom_call" | custom-call | flops 16777216 | bytes 1048576 | tf_op jit(solution)/shard_map/pallas_call | solution.py:573
  23.4 9.1 %all_to_all.11.pieces_ref = bf16[32,8,128]{2,1,0:T(8,128)(2,1)S(1)} all-to-all(bf16[32,8,128]{2,1,0:T(8,128)(2,1)S(1)} %shard_map.52), channel_id=1, replica_groups=mesh['groups'=1,'lat'=16,'lon'=2] {'lat','lon'}, dimensions={0} | all-to-all | bytes 131072 | tf_op jit(solution)/shard_map/all_to_all | solution.py:584
  32.5 0.9 %shard_map.53 = bf16[32,8,256]{2,1,0:T(8,128)(2,1)} custom-call(bf16[32,8,128]{2,1,0:T(8,128)(2,1)S(1)} %all_to_all.11.pieces_ref, bf16[128,256]{1,0:T(8,128)(2,1)S(1)} %get-tuple-element.21.dft_ref), custom_call_target="tpu_custom_call" | custom-call | flops 16777216 | bytes 524288 | tf_op jit(solution)/shard_map/pallas_call | solution.py:585
  (1 shorter events, 0.0 us)
Async XLA Ops:
  0.0 1.6 %collective-permute-start = (bf16[64,8,128]{2,1,0:T(8,128)(2,1)}, bf16[64,8,128]{2,1,0:T(8,128)(2,1)S(1)}, u32[]{:S(2)}, u32[]{:S(2)}) collective-permute-start(bf16[64,8,128]{2,1,0:T(8,128)(2,1)} %fields_ref.1), channel_id=1, source_target_pairs={{0,1},{1,0},{2,3},{3,2},{4,5},{5,4},{6,7},{7,6},{8,9},{9,8},{10,11... | collective-permute-start | bytes 393224 | tf_op jit(solution)/shard_map/ppermute | solution.py:477
  1.7 6.3 %copy-start = (bf16[64,32,64]{2,1,0:T(8,128)(2,1)S(1)}, bf16[64,32,64]{2,1,0:T(8,128)(2,1)}, u32[]{:S(2)}) copy-start(bf16[64,32,64]{2,1,0:T(8,128)(2,1)} %mixing_ref.1) | copy-start | bytes 786436
  1.7 7.5 %collective-permute-start.1 = (bf16[2,64,256]{2,1,0:T(8,128)(2,1)S(1)}, bf16[2,64,256]{2,1,0:T(8,128)(2,1)S(1)}, u32[]{:S(2)}, u32[]{:S(2)}) collective-permute-start(bf16[2,64,256]{2,1,0:T(8,128)(2,1)S(1)} %shard_map.47.message_ref), channel_id=1, source_target_pairs={{0,2},{2,0},{3,5},{5,3},{4,6},{6,4},{7,9},{9,7},{8,10},{10,8},{11,... | collective-permute-start | bytes 196616 | tf_op jit(solution)/shard_map/ppermute | solution.py:513
  8.7 13.9 %collective-permute-start.2 = (f32[64,32,128]{2,1,0:T(8,128)S(1)}, f32[64,32,128]{2,1,0:T(8,128)S(1)}, u32[]{:S(2)}, u32[]{:S(2)}) collective-permute-start(f32[64,32,128]{2,1,0:T(8,128)S(1)} %shard_map.49.mine_ref), channel_id=1, source_target_pairs={{0,1},{1,0},{2,3},{3,2},{4,5},{5,4},{6,7},{7,6},{8,9},{9,8},{10,11... | collective-permute-start | bytes 3145736 | tf_op jit(solution)/shard_map/ppermute | solution.py:555

commit v9 on v7

--- a/solution.py
+++ b/solution.py
@@ -33,8 +33,11 @@
 
 
 def half_of(lat, lon, bands):
-    last = (lat + 1) // bands if isinstance(lat, int) else (lat + 1 == bands).astype(jnp.int32)
-    return (lat + lon + 1 + last) & 1
+    if isinstance(lat, int):
+        end = int(lat in (0, bands - 1))
+    else:
+        end = ((lat == 0) | (lat + 1 == bands)).astype(jnp.int32)
+    return (lat + lon + 1 + end) & 1
 
 
 def row_half():

time: 33.7 us -> 33.7 us (level)
    ppermute x1, starting transfers between devices: 0.07 us -> 4.27 us  [local(): theirs = lax.ppermute(mine, 'lon', swap)]
    ppermute x1, starting transfers between devices: 4.89 us -> 0.8 us  [local(): halo = lax.ppermute(message, both, pairs)]
where the time goes in v9:
time: 33.7 us; the launch traced here: 33.5 us
  blocking collectives  21.8 us (65%)
  Pallas kernels  5.95 us (18%)
  starting transfers between devices  5.52 us (16%)
    all_to_all x1, blocking collectives, local(): lax.all_to_all(coeffs, both, split_axis=0, concat_axis=0, tiled=True)  12.7 us
    all_to_all x1, blocking collectives, local(): back = lax.all_to_all(chunks, both, split_axis=0, concat_axis=0, tiled=True)  9.1 us
    ppermute x1, starting transfers between devices, local(): theirs = lax.ppermute(mine, 'lon', swap)  4.27 us
    pallas_call x1, Pallas kernels, local(): call(functools.partial(interior_kernel, lat_total, owners), (bfloat(taps)...  1.08 us
    pallas_call x1, Pallas kernels, local(): call(load_kernel, (bfloat((row_count, channels, lon_part)), bfloat(argume...  1.07 us
    pallas_call x1, Pallas kernels, local(): call(functools.partial(inverse_kernel, per_device), bfloat((kept, row_cou...  0.91 us
    pallas_call x1, Pallas kernels, local(): call(functools.partial(edge_kernel, lat_total, half), bfloat((owners, per...  0.85 us
    ppermute x1, starting transfers between devices, local(): halo = lax.ppermute(message, both, pairs)  0.8 us
  transfers between devices with their start and end apart: 3, of which 1 were waited for; matrix products, arithmetic and copies ran while one was open for 0% of the time, Pallas kernels for 13%

profile of v9, /device:TPU:0, one launch (start us, length us, event | category | flops | bytes accessed | tf_op | source)
XLA Modules:
  0.0 33.5 jit_solution(11405494888193531147)
XLA Ops:
  0.0 0.5 %collective-permute-start = (bf16[64,8,128]{2,1,0:T(8,128)(2,1)}, bf16[64,8,128]{2,1,0:T(8,128)(2,1)S(1)}, u32[]{:S(2)}, u32[]{:S(2)}) collective-permute-start(bf16[64,8,128]{2,1,0:T(8,128)(2,1)} %fields_ref.1), channel_id=1, source_target_pairs={{0,1},{1,0},{2,3},{3,2},{4,5},{5,4},{6,7},{7,6},{8,9},{9,8},{10,11... | collective-permute-start | bytes 393224 | tf_op jit(solution)/shard_map/ppermute | solution.py:447
  0.5 1.1 %shard_map.46 = (bf16[8,64,128]{2,1,0:T(8,128)(2,1)S(1)}, bf16[3,3,64,64]{3,2,1,0:T(8,128)(2,1)S(1)}, bf16[3,3,64,64]{3,2,1,0:T(8,128)(2,1)S(1)}) custom-call(bf16[64,8,128]{2,1,0:T(8,128)(2,1)} %fields_ref.1, bf16[3,3,64,64]{3,2,1,0:T(8,128)(2,1)} %bitcast.2, bf16[3,3,64,64]{3,2,1,0:T(8,128)(2,1)} %bitcast.3), custom_call_target="tpu_custom_call" | custom-call | flops 65536 | bytes 2097152 | tf_op jit(solution)/shard_map/pallas_call | solution.py:460
  1.5 0.1 collective-permute-done.other_ref
  1.7 0.0 copy-start
  1.7 0.8 %collective-permute-start.1 = (bf16[2,64,256]{2,1,0:T(8,128)(2,1)S(1)}, bf16[2,64,256]{2,1,0:T(8,128)(2,1)S(1)}, u32[]{:S(2)}, u32[]{:S(2)}) collective-permute-start(bf16[2,64,256]{2,1,0:T(8,128)(2,1)S(1)} %shard_map.47.after_ref.message_ref), channel_id=1, source_target_pairs={{1,2},{2,1},{3,5},{5,3},{4,6},{6,4},{7,9},{9,7},{8,10},{10,8},{11,... | collective-permute-start | bytes 196616 | tf_op jit(solution)/shard_map/ppermute | solution.py:483
  2.5 1.1 %shard_map.48 = (bf16[192,192]{1,0:T(8,128)(2,1)S(1)}, bf16[192,192]{1,0:T(8,128)(2,1)S(1)}, bf16[128,256]{1,0:T(8,128)(2,1)S(1)}, bf16[2,64,256]{2,1,0:T(8,128)(2,1)S(1)}, f32[2,64,128]{2,1,0:T(8,128)S(1)}) custom-call(bf16[8,64,128]{2,1,0:T(8,128)(2,1)S(1)} %get-tuple-element.15.own_ref, bf16[64,8,128]{2,1,0:T(8,128)(2,1)S(1)} %collective-permute-done.other_ref, ...), custom_call_target="tpu_custom_call" | custom-call | flops 268435456 | bytes 4194304 | tf_op jit(solution)/shard_map/pallas_call | solution.py:486
  3.6 0.0 copy-done
  3.6 0.7 %shard_map.49.mine_ref = f32[64,32,128]{2,1,0:T(8,128)S(1)} custom-call(bf16[64,32,64]{2,1,0:T(8,128)(2,1)S(1)} %copy-done, bf16[2,64,256]{2,1,0:T(8,128)(2,1)S(1)} %get-tuple-element.18.after_ref.near_ref), custom_call_target="tpu_custom_call" | custom-call | flops 1048576 | bytes 4194304 | tf_op jit(solution)/shard_map/pallas_call | solution.py:512
  4.3 4.3 %collective-permute-start.2 = (f32[64,32,128]{2,1,0:T(8,128)S(1)}, f32[64,32,128]{2,1,0:T(8,128)S(1)}, u32[]{:S(2)}, u32[]{:S(2)}) collective-permute-start(f32[64,32,128]{2,1,0:T(8,128)S(1)} %shard_map.49.mine_ref), channel_id=1, source_target_pairs={{0,1},{1,0},{2,3},{3,2},{4,5},{5,4},{6,7},{7,6},{8,9},{9,8},{10,11... | collective-permute-start | bytes 3145736 | tf_op jit(solution)/shard_map/ppermute | solution.py:521
  8.6 0.5 %shard_map.50 = (bf16[128,256]{1,0:T(8,128)(2,1)S(1)}, bf16[128,128]{1,0:T(8,128)(2,1)S(1)}) custom-call(bf16[2,64,256]{2,1,0:T(8,128)(2,1)S(1)} %get-tuple-element.18.after_ref.near_ref), custom_call_target="tpu_custom_call" | custom-call | flops 34359738368 | bytes 67108864 | tf_op jit(solution)/shard_map/pallas_call | solution.py:522
  9.1 0.0 collective-permute-done.1.halo_ref
  9.1 0.9 %shard_map.51 = bf16[32,8,128]{2,1,0:T(8,128)(2,1)S(1)} custom-call(bf16[2,64,256]{2,1,0:T(8,128)(2,1)S(1)} %collective-permute-done.1.halo_ref, bf16[2,64,256]{2,1,0:T(8,128)(2,1)S(1)} %shard_map.47.after_ref.message_ref, bf16[2,64,256]{2,1,0:T(8,128)(2,1)S(1)} %get-tuple-element.18.after_ref.near_ref, bf16[192,192]{1,0:T(8,128)(2,1)S(1)} %get-tuple-element.19.first_ref, ...), custom_call_target="tpu_custom_call" | custom-call | flops 67108864 | bytes 1048576 | tf_op jit(solution)/shard_map/pallas_call | solution.py:529
  9.9 12.7 %all_to_all.10.pieces_ref = bf16[32,8,128]{2,1,0:T(8,128)(2,1)S(1)} all-to-all(bf16[32,8,128]{2,1,0:T(8,128)(2,1)S(1)} %shard_map.51), channel_id=1, replica_groups=mesh['groups'=1,'lat'=16,'lon'=2] {'lat','lon'}, dimensions={0} | all-to-all | bytes 131072 | tf_op jit(solution)/shard_map/all_to_all | solution.py:541
  22.7 0.0 collective-permute-done.2.theirs_ref
  22.7 0.8 %shard_map.52 = bf16[32,8,128]{2,1,0:T(8,128)(2,1)S(1)} custom-call(bf16[32,8,128]{2,1,0:T(8,128)(2,1)S(1)} %all_to_all.10.pieces_ref, bf16[128,256]{1,0:T(8,128)(2,1)S(1)} %get-tuple-element.23.analysis_ref, bf16[128,128]{1,0:T(8,128)(2,1)S(1)} %get-tuple-element.24.synthesis_ref, f32[64,32,128]{2,1,0:T(8,128)S(1)} %shard_map.49.mine_ref, ...), custom_call_target="tpu_custom_call" | custom-call | flops 16777216 | bytes 1048576 | tf_op jit(solution)/shard_map/pallas_call | solution.py:544
  23.5 9.1 %all_to_all.11.pieces_ref = bf16[32,8,128]{2,1,0:T(8,128)(2,1)S(1)} all-to-all(bf16[32,8,128]{2,1,0:T(8,128)(2,1)S(1)} %shard_map.52), channel_id=1, replica_groups=mesh['groups'=1,'lat'=16,'lon'=2] {'lat','lon'}, dimensions={0} | all-to-all | bytes 131072 | tf_op jit(solution)/shard_map/all_to_all | solution.py:555
  32.6 0.9 %shard_map.53 = bf16[32,8,256]{2,1,0:T(8,128)(2,1)} custom-call(bf16[32,8,128]{2,1,0:T(8,128)(2,1)S(1)} %all_to_all.11.pieces_ref, bf16[128,256]{1,0:T(8,128)(2,1)S(1)} %get-tuple-element.21.dft_ref), custom_call_target="tpu_custom_call" | custom-call | flops 16777216 | bytes 524288 | tf_op jit(solution)/shard_map/pallas_call | solution.py:556
  (1 shorter events, 0.0 us)
Async XLA Ops:
  0.0 1.6 %collective-permute-start = (bf16[64,8,128]{2,1,0:T(8,128)(2,1)}, bf16[64,8,128]{2,1,0:T(8,128)(2,1)S(1)}, u32[]{:S(2)}, u32[]{:S(2)}) collective-permute-start(bf16[64,8,128]{2,1,0:T(8,128)(2,1)} %fields_ref.1), channel_id=1, source_target_pairs={{0,1},{1,0},{2,3},{3,2},{4,5},{5,4},{6,7},{7,6},{8,9},{9,8},{10,11... | collective-permute-start | bytes 393224 | tf_op jit(solution)/shard_map/ppermute | solution.py:447
  1.7 1.9 %copy-start = (bf16[64,32,64]{2,1,0:T(8,128)(2,1)S(1)}, bf16[64,32,64]{2,1,0:T(8,128)(2,1)}, u32[]{:S(2)}) copy-start(bf16[64,32,64]{2,1,0:T(8,128)(2,1)} %mixing_ref.1) | copy-start | bytes 786436
  1.7 7.4 %collective-permute-start.1 = (bf16[2,64,256]{2,1,0:T(8,128)(2,1)S(1)}, bf16[2,64,256]{2,1,0:T(8,128)(2,1)S(1)}, u32[]{:S(2)}, u32[]{:S(2)}) collective-permute-start(bf16[2,64,256]{2,1,0:T(8,128)(2,1)S(1)} %shard_map.47.after_ref.message_ref), channel_id=1, source_target_pairs={{1,2},{2,1},{3,5},{5,3},{4,6},{6,4},{7,9},{9,7},{8,10},{10,8},{11,... | collective-permute-start | bytes 196616 | tf_op jit(solution)/shard_map/ppermute | solution.py:483
  4.3 18.3 %collective-permute-start.2 = (f32[64,32,128]{2,1,0:T(8,128)S(1)}, f32[64,32,128]{2,1,0:T(8,128)S(1)}, u32[]{:S(2)}, u32[]{:S(2)}) collective-permute-start(f32[64,32,128]{2,1,0:T(8,128)S(1)} %shard_map.49.mine_ref), channel_id=1, source_target_pairs={{0,1},{1,0},{2,3},{3,2},{4,5},{5,4},{6,7},{7,6},{8,9},{9,8},{10,11... | collective-permute-start | bytes 3145736 | tf_op jit(solution)/shard_map/ppermute | solution.py:521

commit v10 on v7

--- a/solution.py
+++ b/solution.py
@@ -15,12 +15,12 @@
 LANES = 128
 
 
-def call(kernel, out_shape, scratch, in_specs, cost):
+def call(kernel, out_shape, scratch, in_specs, cost, place=VMEM):
     return pl.pallas_call(
         kernel,
         out_shape=out_shape,
         in_specs=in_specs,
-        out_specs=jax.tree.map(lambda _: VMEM, out_shape),
+        out_specs=jax.tree.map(lambda _: place, out_shape),
         scratch_shapes=scratch,
         compiler_params=pltpu.CompilerParams(vmem_limit_bytes=LIMIT),
         cost_estimate=cost,
@@ -395,7 +395,9 @@
     out_ref[...] = chunk_ref[...].astype(jnp.bfloat16).reshape(out_ref.shape)
 
 
-def inverse_kernel(per_device, pieces_ref, dft_ref, out_ref, pieces_32_ref, rows_ref):
+def inverse_kernel(
+    per_device, pieces_ref, dft_ref, out_ref, pieces_32_ref, rows_ref, staged_ref, sent
+):
     owners, chunk_rows, width = pieces_ref.shape
     kept, row_count, lon_total = out_ref.shape
     packed = width // kept
@@ -419,10 +421,19 @@
                 rows_ref[tile, pl.ds(group * packed + i, kept, stride=row_count), :] = values[
                     i * kept : (i + 1) * kept, tile * LANES : (tile + 1) * LANES
                 ]
-    for tile in range(lon_total // LANES):
-        out_ref[:, :, tile * LANES : (tile + 1) * LANES] = (
-            rows_ref[tile].astype(jnp.bfloat16).reshape(kept, row_count, LANES)
-        )
+    copies = []
+    size = kept // 4
+    for i in range(4):
+        own = pl.ds(i * size, size)
+        for tile in range(lon_total // LANES):
+            block = rows_ref[tile, i * size * row_count : (i + 1) * size * row_count, :]
+            staged_ref[own, :, tile * LANES : (tile + 1) * LANES] = block.astype(
+                jnp.bfloat16
+            ).reshape(size, row_count, LANES)
+        copies.append(pltpu.make_async_copy(staged_ref.at[own], out_ref.at[own], sent.at[i]))
+        copies[-1].start()
+    for copy in copies:
+        copy.wait()
 
 
 def local(fields, conv_first, conv_second, mixing):
@@ -556,9 +567,12 @@
         [
             pltpu.VMEM((owners * chunk_rows, LANES), jnp.float32),
             pltpu.VMEM((lon_total // LANES, kept * row_count, LANES), jnp.float32),
+            pltpu.VMEM((kept, row_count, lon_total), jnp.bfloat16),
+            pltpu.SemaphoreType.DMA((4,)),
         ],
         [VMEM] * 2,
         pl.CostEstimate(flops=1 << 24, bytes_accessed=1 << 19, transcendentals=0),
+        HBM,
     )(back, dft)
 
 

time: 33.7 us -> 33.7 us (level)
  no operation moved by 1% of the time
where the time goes in v10:
time: 33.7 us; the launch traced here: 33.5 us
  blocking collectives  21.9 us (65%)
  Pallas kernels  5.96 us (18%)
  starting transfers between devices  5.41 us (16%)
    all_to_all x1, blocking collectives, local(): lax.all_to_all(coeffs, both, split_axis=0, concat_axis=0, tiled=True)  12.8 us
    all_to_all x1, blocking collectives, local(): back = lax.all_to_all(chunks, both, split_axis=0, concat_axis=0, tiled=True)  9.1 us
    ppermute x1, starting transfers between devices, local(): halo = lax.ppermute(message, both, pairs)  4.89 us
    pallas_call x1, Pallas kernels, local(): call(functools.partial(interior_kernel, lat_total, owners), (bfloat(taps)...  1.08 us
    pallas_call x1, Pallas kernels, local(): call(load_kernel, (bfloat((row_count, channels, lon_part)), bfloat(argume...  1.07 us
    pallas_call x1, Pallas kernels, local(): call(functools.partial(inverse_kernel, per_device), bfloat((kept, row_cou...  0.93 us
    pallas_call x1, Pallas kernels, local(): call(functools.partial(edge_kernel, lat_total, half), bfloat((owners, per...  0.85 us
    pallas_call x1, Pallas kernels, local(): call(functools.partial(spectral_kernel, per_device), bfloat((owners, chun...  0.8 us
  transfers between devices with their start and end apart: 3, of which 1 were waited for; matrix products, arithmetic and copies ran while one was open for 0% of the time, Pallas kernels for 13%

profile of v10, /device:TPU:0, one launch (start us, length us, event | category | flops | bytes accessed | tf_op | source)
XLA Modules:
  0.0 33.5 jit_solution(15764508786513303188)
XLA Ops:
  0.0 0.5 %collective-permute-start = (bf16[64,8,128]{2,1,0:T(8,128)(2,1)}, bf16[64,8,128]{2,1,0:T(8,128)(2,1)S(1)}, u32[]{:S(2)}, u32[]{:S(2)}) collective-permute-start(bf16[64,8,128]{2,1,0:T(8,128)(2,1)} %fields_ref.1), channel_id=1, source_target_pairs={{0,1},{1,0},{2,3},{3,2},{4,5},{5,4},{6,7},{7,6},{8,9},{9,8},{10,11... | collective-permute-start | bytes 393224 | tf_op jit(solution)/shard_map/ppermute | solution.py:455
  0.5 1.1 %shard_map.46 = (bf16[8,64,128]{2,1,0:T(8,128)(2,1)S(1)}, bf16[3,3,64,64]{3,2,1,0:T(8,128)(2,1)S(1)}, bf16[3,3,64,64]{3,2,1,0:T(8,128)(2,1)S(1)}) custom-call(bf16[64,8,128]{2,1,0:T(8,128)(2,1)} %fields_ref.1, bf16[3,3,64,64]{3,2,1,0:T(8,128)(2,1)} %bitcast.2, bf16[3,3,64,64]{3,2,1,0:T(8,128)(2,1)} %bitcast.3), custom_call_target="tpu_custom_call" | custom-call | flops 65536 | bytes 2097152 | tf_op jit(solution)/shard_map/pallas_call | solution.py:468
  1.5 0.1 collective-permute-done.other_ref
  1.7 0.0 copy-start
  1.7 4.9 %collective-permute-start.1 = (bf16[2,64,256]{2,1,0:T(8,128)(2,1)S(1)}, bf16[2,64,256]{2,1,0:T(8,128)(2,1)S(1)}, u32[]{:S(2)}, u32[]{:S(2)}) collective-permute-start(bf16[2,64,256]{2,1,0:T(8,128)(2,1)S(1)} %shard_map.47.after_ref.message_ref), channel_id=1, source_target_pairs={{0,2},{2,0},{3,5},{5,3},{4,6},{6,4},{7,9},{9,7},{8,10},{10,8},{11,... | collective-permute-start | bytes 196616 | tf_op jit(solution)/shard_map/ppermute | solution.py:491
  6.6 1.1 %shard_map.48 = (bf16[192,192]{1,0:T(8,128)(2,1)S(1)}, bf16[192,192]{1,0:T(8,128)(2,1)S(1)}, bf16[128,256]{1,0:T(8,128)(2,1)S(1)}, bf16[2,64,256]{2,1,0:T(8,128)(2,1)S(1)}, f32[2,64,128]{2,1,0:T(8,128)S(1)}) custom-call(bf16[8,64,128]{2,1,0:T(8,128)(2,1)S(1)} %get-tuple-element.15.own_ref, bf16[64,8,128]{2,1,0:T(8,128)(2,1)S(1)} %collective-permute-done.other_ref, ...), custom_call_target="tpu_custom_call" | custom-call | flops 268435456 | bytes 4194304 | tf_op jit(solution)/shard_map/pallas_call | solution.py:494
  7.7 0.0 copy-done
  7.7 0.7 %shard_map.49.mine_ref = f32[64,32,128]{2,1,0:T(8,128)S(1)} custom-call(bf16[64,32,64]{2,1,0:T(8,128)(2,1)S(1)} %copy-done, bf16[2,64,256]{2,1,0:T(8,128)(2,1)S(1)} %get-tuple-element.18.after_ref.near_ref), custom_call_target="tpu_custom_call" | custom-call | flops 1048576 | bytes 4194304 | tf_op jit(solution)/shard_map/pallas_call | solution.py:520
  8.4 0.1 collective-permute-start.2
  8.5 0.5 %shard_map.50 = (bf16[128,256]{1,0:T(8,128)(2,1)S(1)}, bf16[128,128]{1,0:T(8,128)(2,1)S(1)}) custom-call(bf16[2,64,256]{2,1,0:T(8,128)(2,1)S(1)} %get-tuple-element.18.after_ref.near_ref), custom_call_target="tpu_custom_call" | custom-call | flops 34359738368 | bytes 67108864 | tf_op jit(solution)/shard_map/pallas_call | solution.py:530
  9.0 0.0 collective-permute-done.1.halo_ref
  9.0 0.8 %shard_map.51 = bf16[32,8,128]{2,1,0:T(8,128)(2,1)S(1)} custom-call(bf16[2,64,256]{2,1,0:T(8,128)(2,1)S(1)} %collective-permute-done.1.halo_ref, bf16[2,64,256]{2,1,0:T(8,128)(2,1)S(1)} %shard_map.47.after_ref.message_ref, bf16[2,64,256]{2,1,0:T(8,128)(2,1)S(1)} %get-tuple-element.18.after_ref.near_ref, bf16[192,192]{1,0:T(8,128)(2,1)S(1)} %get-tuple-element.19.first_ref, ...), custom_call_target="tpu_custom_call" | custom-call | flops 67108864 | bytes 1048576 | tf_op jit(solution)/shard_map/pallas_call | solution.py:537
  9.8 12.8 %all_to_all.10.pieces_ref = bf16[32,8,128]{2,1,0:T(8,128)(2,1)S(1)} all-to-all(bf16[32,8,128]{2,1,0:T(8,128)(2,1)S(1)} %shard_map.51), channel_id=1, replica_groups=mesh['groups'=1,'lat'=16,'lon'=2] {'lat','lon'}, dimensions={0} | all-to-all | bytes 131072 | tf_op jit(solution)/shard_map/all_to_all | solution.py:549
  22.7 0.0 collective-permute-done.2.theirs_ref
  22.7 0.8 %shard_map.52 = bf16[32,8,128]{2,1,0:T(8,128)(2,1)S(1)} custom-call(bf16[32,8,128]{2,1,0:T(8,128)(2,1)S(1)} %all_to_all.10.pieces_ref, bf16[128,256]{1,0:T(8,128)(2,1)S(1)} %get-tuple-element.23.analysis_ref, bf16[128,128]{1,0:T(8,128)(2,1)S(1)} %get-tuple-element.24.synthesis_ref, f32[64,32,128]{2,1,0:T(8,128)S(1)} %shard_map.49.mine_ref, ...), custom_call_target="tpu_custom_call" | custom-call | flops 16777216 | bytes 1048576 | tf_op jit(solution)/shard_map/pallas_call | solution.py:552
  23.5 9.1 %all_to_all.11.pieces_ref = bf16[32,8,128]{2,1,0:T(8,128)(2,1)S(1)} all-to-all(bf16[32,8,128]{2,1,0:T(8,128)(2,1)S(1)} %shard_map.52), channel_id=1, replica_groups=mesh['groups'=1,'lat'=16,'lon'=2] {'lat','lon'}, dimensions={0} | all-to-all | bytes 131072 | tf_op jit(solution)/shard_map/all_to_all | solution.py:563
  32.6 0.9 %shard_map.53 = bf16[32,8,256]{2,1,0:T(8,128)(2,1)} custom-call(bf16[32,8,128]{2,1,0:T(8,128)(2,1)S(1)} %all_to_all.11.pieces_ref, bf16[128,256]{1,0:T(8,128)(2,1)S(1)} %get-tuple-element.21.dft_ref), custom_call_target="tpu_custom_call" | custom-call | flops 16777216 | bytes 524288 | tf_op jit(solution)/shard_map/pallas_call | solution.py:564
  (1 shorter events, 0.0 us)
Async XLA Ops:
  0.0 1.6 %collective-permute-start = (bf16[64,8,128]{2,1,0:T(8,128)(2,1)}, bf16[64,8,128]{2,1,0:T(8,128)(2,1)S(1)}, u32[]{:S(2)}, u32[]{:S(2)}) collective-permute-start(bf16[64,8,128]{2,1,0:T(8,128)(2,1)} %fields_ref.1), channel_id=1, source_target_pairs={{0,1},{1,0},{2,3},{3,2},{4,5},{5,4},{6,7},{7,6},{8,9},{9,8},{10,11... | collective-permute-start | bytes 393224 | tf_op jit(solution)/shard_map/ppermute | solution.py:455
  1.7 6.0 %copy-start = (bf16[64,32,64]{2,1,0:T(8,128)(2,1)S(1)}, bf16[64,32,64]{2,1,0:T(8,128)(2,1)}, u32[]{:S(2)}) copy-start(bf16[64,32,64]{2,1,0:T(8,128)(2,1)} %mixing_ref.1) | copy-start | bytes 786436
  1.7 7.3 %collective-permute-start.1 = (bf16[2,64,256]{2,1,0:T(8,128)(2,1)S(1)}, bf16[2,64,256]{2,1,0:T(8,128)(2,1)S(1)}, u32[]{:S(2)}, u32[]{:S(2)}) collective-permute-start(bf16[2,64,256]{2,1,0:T(8,128)(2,1)S(1)} %shard_map.47.after_ref.message_ref), channel_id=1, source_target_pairs={{0,2},{2,0},{3,5},{5,3},{4,6},{6,4},{7,9},{9,7},{8,10},{10,8},{11,... | collective-permute-start | bytes 196616 | tf_op jit(solution)/shard_map/ppermute | solution.py:491
  8.4 14.2 %collective-permute-start.2 = (f32[64,32,128]{2,1,0:T(8,128)S(1)}, f32[64,32,128]{2,1,0:T(8,128)S(1)}, u32[]{:S(2)}, u32[]{:S(2)}) collective-permute-start(f32[64,32,128]{2,1,0:T(8,128)S(1)} %shard_map.49.mine_ref), channel_id=1, source_target_pairs={{0,1},{1,0},{2,3},{3,2},{4,5},{5,4},{6,7},{7,6},{8,9},{9,8},{10,11... | collective-permute-start | bytes 3145736 | tf_op jit(solution)/shard_map/ppermute | solution.py:529
